TPU v7x, 32 devices: a whole 2x2x4 slice. The times are simulated.
32 devices in a mesh: grp: 2 (over x), slab: 16 (over z, y, core).
Axes of the slice: x: 2, y: 2, z: 4, core: 2. Of those that a mesh axis runs over, the one named last changes fastest.
Arguments:
- thermal_state_values: float32 [64, 128], P(('grp', 'slab')), may hold values from -6 to 6
- thermal_kappa_values: float32 [32, 32], P(('grp', 'slab')), may hold values from 0.5 to 2
- nodal_heating_input: float32 [64, 128], P(('grp', 'slab')), may hold values from -24 to 24
- frozen_share_map: float32 [256, 2048], P('grp', 'slab'), may hold values from 0 to 1
- crystal_label_map: int32 [256, 2048], P('grp', 'slab'), may hold values from 0 to 7999
- growth_reach_table: int32 [8000, 6], replicated, may hold values from 1 to 4
- seed_site_slots: int32 [8192], P(('grp', 'slab')), may hold values from 0 to 16383
- seed_crystal_label: int32 [8192], P(('grp', 'slab')), may hold values from 0 to 7999
Outputs:
- new_temperature: float32 [64, 128], P(('grp', 'slab'))
- new_solid: float32 [256, 2048], P('grp', 'slab')
Inputs may be any that keep to these rules, and one draw needn't show every extreme that they name: `seed_site_slots`: each entry is a cell of the brick of the device that holds the entry, numbered x * 8 * 16 + y * 16 + z in that brick's own coordinates; entries may repeat.
All inputs are finite; a program needn't handle non-finite values.
Results may differ from a plain program's by a relative error of at most 0.0001.
Values sent between devices are 32-bit elements; how exact they have to be, the bound alone decides.
No kernel may reach another device: no remote copies, remote signals or barrier semaphores. Data moves between devices by JAX's collectives and lax.ppermute only.
A program may use at most 128 MiB of HBM per device.

v0:
```python
import jax
import jax.numpy as jnp
from jax import lax
from jax.sharding import PartitionSpec as P

HEX_COUNT_LATER = 2
CPC = 8


HIGHEST = lax.Precision.HIGHEST
step_size = 0.004
DERIVS = ((-3.0, 4.0, -1.0), (-1.0, 0.0, 1.0), (1.0, -4.0, 3.0))
WEIGHTS = (1.0 / 6.0, 2.0 / 3.0, 1.0 / 6.0)


def passed_along(array, axis, by):
    count = lax.axis_size(axis)
    return lax.ppermute(array, axis, [(i, (i + by) % count) for i in range(count)])


def extended_2(array, sides, width):
    for axis, dim in sides:
        count, length = (lax.axis_size(axis), array.shape[dim])
        up = [(i, (i + 1) % count) for i in range(count)]
        down = [(j, i) for i, j in up]
        last = lax.slice_in_dim(array, length - width, length, axis=dim)
        first = lax.slice_in_dim(array, 0, width, axis=dim)
        before = lax.ppermute(last, axis, up)
        after = lax.ppermute(first, axis, down)
        array = jnp.concatenate([before, array, after], axis=dim)
    return array


def alternate(even_part, odd_part, which_axis):
    stacked = jnp.stack([even_part, odd_part], which_axis + 1)
    shape = list(even_part.shape)
    shape[which_axis] = 2 * shape[which_axis]
    return stacked.reshape(shape)


def spread_periodic(values, which_axis):
    even_part = WEIGHTS[0] * values + WEIGHTS[2] * jnp.roll(values, 1, which_axis)
    return alternate(even_part, WEIGHTS[1] * values, which_axis)


def spread_open(values, which_axis):
    count = values.shape[which_axis]
    zero_plane = jnp.zeros_like(lax.slice_in_dim(values, 0, 1, 1, which_axis))
    even_part = WEIGHTS[0] * jnp.concatenate([values, zero_plane], which_axis) + WEIGHTS[
        2
    ] * jnp.concatenate([zero_plane, values], which_axis)
    paired = alternate(
        lax.slice_in_dim(even_part, 0, count, 1, which_axis), WEIGHTS[1] * values, which_axis
    )
    return jnp.concatenate(
        [paired, lax.slice_in_dim(even_part, count, count + 1, 1, which_axis)], which_axis
    )


def place_even(values, which_axis):
    return alternate(values, jnp.zeros_like(values), which_axis)


def coefficients(kappa, rows_y):
    layers = kappa.shape[0]
    cube = kappa.reshape(layers, rows_y, -1)
    along_x = spread_periodic(spread_periodic(cube, 1), 2).reshape(layers, -1)
    along_y = spread_periodic(place_even(spread_open(cube, 0), 1), 2).reshape(2 * layers + 1, -1)
    along_z = place_even(spread_periodic(spread_open(cube, 0), 1), 2).reshape(2 * layers + 1, -1)
    return (along_x, along_y, along_z)


def contract(first, second, third, coefficient):
    terms = []
    for point in range(3):
        slope = DERIVS[point][0] * first + DERIVS[point][1] * second + DERIVS[point][2] * third
        terms.append(WEIGHTS[point] * coefficient * slope)
    results = []
    for local in range(3):
        results.append(
            DERIVS[0][local] * terms[0] + DERIVS[1][local] * terms[1] + DERIVS[2][local] * terms[2]
        )
    return results


def local_action(extended, coeff_set, plane_width):
    along_x, along_y, along_z = coeff_set
    layers = along_x.shape[0]
    flat = extended.shape[1]
    first = extended[0 : 2 * layers : 2]
    second = extended[1 : 2 * layers : 2]
    third = extended[2 : 2 * layers + 1 : 2]
    parts = contract(first, second, third, along_x)
    zero_plane = jnp.zeros((1, flat), jnp.float32)
    even_part = jnp.concatenate([parts[0], zero_plane], 0) + jnp.concatenate(
        [zero_plane, parts[2]], 0
    )
    result = jnp.concatenate([alternate(even_part[:layers], parts[1], 0), even_part[layers:]], 0)
    parts = contract(
        extended,
        jnp.roll(extended, -plane_width, 1),
        jnp.roll(extended, -2 * plane_width, 1),
        along_y,
    )
    result = (
        result
        + parts[0]
        + jnp.roll(parts[1], plane_width, 1)
        + jnp.roll(parts[2], 2 * plane_width, 1)
    )
    z_index = jnp.arange(flat) % plane_width
    ahead_two = jnp.where(
        z_index == plane_width - 2,
        jnp.roll(extended, plane_width - 2, 1),
        jnp.roll(extended, -2, 1),
    )
    parts = contract(extended, jnp.roll(extended, -1, 1), ahead_two, along_z)
    behind_two = jnp.where(
        z_index == 0, jnp.roll(parts[2], 2 - plane_width, 1), jnp.roll(parts[2], 2, 1)
    )
    return result + parts[0] + jnp.roll(parts[1], 1, 1) + behind_two


def node_mass(length):
    return jnp.where(jnp.arange(length) % 2 == 0, 1.0 / 3.0, 2.0 / 3.0).astype(jnp.float32)


def basis_columns():
    points = (jnp.arange(CPC, dtype=jnp.float32) + 0.5) / CPC
    return jnp.stack(
        [
            2.0 * (points - 0.5) * (points - 1.0),
            -4.0 * points * (points - 1.0),
            2.0 * points * (points - 0.5),
        ],
        axis=1,
    )


def element_matrix(count, node_count):
    columns = basis_columns()
    cell = jnp.arange(count * CPC)
    element = cell // CPC
    within = cell % CPC
    node = jnp.arange(node_count)[:, None]
    matrix = jnp.zeros((node_count, count * CPC), jnp.float32)
    for local in range(3):
        matrix = matrix + jnp.where(
            node == (2 * element[None, :] + local) % node_count,
            columns[within, local][None, :],
            0.0,
        )
    return matrix


def interp_rows(tensor, matrix_y, matrix_z):
    row_count, node_rows, plane_width = tensor.shape
    deep = jnp.dot(
        tensor.reshape(row_count * node_rows, plane_width), matrix_z, precision=HIGHEST
    ).reshape(row_count, node_rows, -1)
    result = jnp.einsum("rqz,qy->ryz", deep, matrix_y, precision=HIGHEST)
    return result.reshape(row_count, -1)


def next_plane(values):
    return passed_along(values[:1], ("grp", "slab"), -1)


def body(
    thermal_state_values,
    thermal_kappa_values,
    nodal_heating_input,
    frozen_share_map,
    crystal_label_map,
    growth_reach_table,
    seed_site_slots,
    seed_crystal_label,
):
    layers = thermal_kappa_values.shape[0]
    rows_y = thermal_kappa_values.shape[1] // HEX_COUNT_LATER
    plane_width = 2 * HEX_COUNT_LATER
    depth = CPC * HEX_COUNT_LATER
    flat_nodes = thermal_state_values.shape[1]
    mass_plane = (node_mass(2 * rows_y)[:, None] * node_mass(plane_width)[None, :]).reshape(
        1, flat_nodes
    )
    lumped_mass = node_mass(2 * layers)[:, None] * mass_plane
    kappa_ext = jnp.concatenate(
        [passed_along(thermal_kappa_values, ("grp", "slab"), 1), thermal_kappa_values], 0
    )
    coeff_set = coefficients(kappa_ext, rows_y)

    def operate(values):
        upper_plane = next_plane(values)
        lower_plane = passed_along(values, ("grp", "slab"), 1)
        acted = local_action(
            jnp.concatenate([lower_plane, values, upper_plane], 0), coeff_set, plane_width
        )
        return acted[2 : 2 * layers + 2]

    rate_one = (nodal_heating_input - operate(thermal_state_values)) / lumped_mass
    middle = thermal_state_values + step_size * rate_one
    rate_two = (nodal_heating_input - operate(middle)) / lumped_mass
    new_field = thermal_state_values + 0.5 * step_size * (rate_one + rate_two)
    extended = jnp.concatenate([new_field, next_plane(new_field)], 0)
    matrix_x = element_matrix(layers, 2 * layers + 1).T
    matrix_z = element_matrix(HEX_COUNT_LATER, plane_width)
    planes_x = jnp.dot(matrix_x, extended, precision=HIGHEST)
    slab_cells = interp_rows(
        planes_x.reshape(layers * CPC, 2 * rows_y, plane_width),
        element_matrix(rows_y, 2 * rows_y),
        matrix_z,
    )
    cell_temp = lax.all_to_all(slab_cells, "slab", split_axis=1, concat_axis=0, tiled=True)
    edge_x = frozen_share_map.shape[0]
    flat_cells = frozen_share_map.shape[1]
    edge_y = flat_cells // depth
    level_table = growth_reach_table.T.astype(jnp.float32) / 4.0
    weighted = jnp.take(level_table, crystal_label_map, axis=1) * frozen_share_map[None]
    quarter = jnp.transpose(weighted[:4].reshape(4, edge_x, edge_y, depth), (0, 2, 3, 1))
    padded = extended_2(quarter, (("grp", 3), ("slab", 1)), 1)
    sideways = (
        padded[0, 1:-1, :, 2:]
        + padded[1, 1:-1, :, :-2]
        + padded[2, 2:, :, 1:-1]
        + padded[3, :-2, :, 1:-1]
    )
    gathered = jnp.transpose(sideways, (2, 0, 1)).reshape(edge_x, flat_cells)
    depth_index = jnp.arange(flat_cells) % depth
    gathered = gathered + jnp.where(
        depth_index == depth - 1, jnp.roll(weighted[4], depth - 1, 1), jnp.roll(weighted[4], -1, 1)
    )
    gathered = gathered + jnp.where(
        depth_index == 0, jnp.roll(weighted[5], 1 - depth, 1), jnp.roll(weighted[5], 1, 1)
    )
    mean_level = jnp.sum(growth_reach_table.astype(jnp.float32), axis=1) / 6.0
    site_value = jnp.take(mean_level, seed_crystal_label)
    nucleation = (
        jnp.zeros((edge_x * flat_cells,), jnp.float32)
        .at[seed_site_slots]
        .add(site_value)
        .reshape(edge_x, flat_cells)
    )
    undercool = jnp.maximum(-cell_temp, 0.0)
    capture_rate = undercool * undercool * gathered + undercool * nucleation
    new_solid = frozen_share_map + (1.0 - frozen_share_map) * (1.0 - jnp.exp(-capture_rate))
    return (new_field, new_solid)


def solution(mesh):
    in_specs = (
        P(("grp", "slab"), None),
        P(("grp", "slab"), None),
        P(("grp", "slab"), None),
        P("grp", "slab"),
        P("grp", "slab"),
        P(),
        P(("grp", "slab")),
        P(("grp", "slab")),
    )
    out_specs = (P(("grp", "slab"), None), P("grp", "slab"))
    return jax.shard_map(body, mesh=mesh, in_specs=in_specs, out_specs=out_specs, check_vma=False)
```

profile of v0, /device:TPU:0, one launch (start us, length us, event | category | flops | bytes accessed | tf_op | source)
XLA Modules:
  0.0 117.9 jit_solution(4050520135835879176)
XLA Ops:
  0.6 0.5 collective-permute-start
  1.1 2.6 %collective-permute-start.1 = (f32[2,128]{1,0:T(2,128)}, f32[2,128]{1,0:T(2,128)S(1)}, u32[]{:S(2)}, u32[]{:S(2)}) collective-permute-start(f32[2,128]{1,0:T(2,128)} %param.8), channel_id=1, source_target_pairs={{0,1},{1,2},{2,3},{3,4},{4,5},{5,6},{6,7},{7,8},{8,9},{9,10},{10,1... | collective-permute-start | bytes 3080 | tf_op jit(solution)/shard_map/ppermute | solution.py:18
  3.8 0.7 slice.296
  4.4 3.4 %collective-permute-start.2 = (f32[1,128]{1,0:T(1,128)S(1)}, f32[1,128]{1,0:T(1,128)S(1)}, u32[]{:S(2)}, u32[]{:S(2)}) collective-permute-start(f32[1,128]{1,0:T(1,128)S(1)} %slice.296), channel_id=1, source_target_pairs={{0,31},{1,0},{2,1},{3,2},{4,3},{5,4},{6,5},{7,6},{8,7},{9,8},{10,9... | collective-permute-start | bytes 1544 | tf_op jit(solution)/shard_map/ppermute | solution.py:18
  7.8 0.9 bitcast_clamp_fusion
  8.7 0.9 compare_and_fusion
  9.6 1.0 convert_reduce_fusion
  10.6 3.1 %copy.293 = f32[6,8000]{0,1:T(8,128)} copy(f32[6,8000]{1,0:T(8,128)S(1)} %get-tuple-element.37) | data formatting | bytes 384000 | tf_op jit(solution)/shard_map/div | solution.py:218
  13.7 56.9 %gather_fusion.9 = f32[16384,6]{1,0:T(8,128)} fusion(f32[6,8000]{0,1:T(8,128)} %copy.293, s32[16384]{0:T(1024)S(1)} %bitcast_clamp_fusion), kind=kCustom, calls=%fused_computation.9 | custom fusion | bytes 851968 | tf_op jit(solution)/shard_map/jit(_take)/gather | solution.py:219
  70.6 5.3 %copy.294 = f32[128,128,6]{1,0,2:T(8,128)S(1)} copy(f32[128,128,6]{2,1,0:T(8,128)} %bitcast.130) | data formatting | bytes 786432 | tf_op jit(solution)/shard_map/jit(_take)/gather | solution.py:219
  76.0 0.1 copy.295
  76.2 0.1 fusion.101
  76.3 2.0 %collective-permute-start.6 = (f32[4,8,16,1]{3,2,1,0:T(8,128)S(1)}, f32[4,8,16,1]{3,2,1,0:T(8,128)S(1)}, u32[]{:S(2)}, u32[]{:S(2)}) collective-permute-start(f32[4,8,16,1]{3,2,1,0:T(8,128)S(1)} %get-tuple-element.35), channel_id=1, source_target_pairs={{16,0},{0,16},{17,1},{1,17},{18,2},{2,18},{19,3},{3,19},{20,4},{4,... | collective-permute-start | bytes 6152 | tf_op jit(solution)/shard_map/ppermute | solution.py:29
  78.3 0.1 collective-permute-start.7
  78.7 1.7 %gather_fusion.10 = f32[256]{0:T(256)S(1)} fusion(f32[8000]{0:T(1024)S(1)} %broadcast_multiply_fusion, s32[1024]{0:T(1024)S(1)} %pad_clamp_fusion), kind=kCustom, calls=%fused_computation.10 | custom fusion | bytes 3072 | tf_op jit(solution)/shard_map/jit(_take)/gather | solution.py:237
  82.7 0.1 copy.252
  82.9 0.2 mul.738
  83.4 0.1 copy.275
  84.2 0.1 copy.253
  84.4 0.2 mul.745
  84.5 0.1 copy.277
  84.7 0.1 copy.279
  84.9 0.1 copy.266
  85.1 0.1 copy.268
  86.5 5.3 %collective-permute-start.4 = (f32[1,128]{1,0:T(1,128)S(1)}, f32[1,128]{1,0:T(1,128)S(1)}, u32[]{:S(2)}, u32[]{:S(2)}) collective-permute-start(f32[1,128]{1,0:T(1,128)S(1)} %slice.329), channel_id=1, source_target_pairs={{0,31},{1,0},{2,1},{3,2},{4,3},{5,4},{6,5},{7,6},{8,7},{9,8},{10,9... | collective-permute-start | bytes 1544 | tf_op jit(solution)/shard_map/ppermute | solution.py:18
  91.9 0.6 gather_fusion.5
  92.5 0.6 gather_fusion.4
  93.1 0.6 gather_fusion.3
  93.8 0.6 gather_fusion.8
  94.4 0.6 gather_fusion.7
  95.1 0.6 gather_fusion.6
  95.7 1.0 gather_fusion.2
  96.7 1.0 gather_fusion.1
  97.7 1.0 gather_fusion
  100.0 0.1 pad_maximum_fusion.8
  100.1 0.5 collective-permute-start.9
  100.6 4.0 %collective-permute-start.8 = (f32[4,1,16,130]{3,2,1,0:T(8,128)S(1)}, f32[4,1,16,130]{3,2,1,0:T(8,128)S(1)}, u32[]{:S(2)}, u32[]{:S(2)}) collective-permute-start(f32[4,1,16,130]{3,2,1,0:T(8,128)S(1)} %get-tuple-element.30), channel_id=1, source_target_pairs={{1,0},{2,1},{3,2},{4,3},{5,4},{6,5},{7,6},{8,7},{9,8},{10,9},{11,1... | collective-permute-start | bytes 99848 | tf_op jit(solution)/shard_map/ppermute | solution.py:29
  104.6 0.3 fusion.48
  105.0 0.3 fusion.52
  105.3 0.2 fusion.14
  105.5 0.2 copy.291
  105.7 0.2 all_to_all.10
  105.9 0.7 copy.292
  106.5 3.7 %all-to-all-start = ((f32[8,16,128]{2,0,1:T(8,128)}), f32[8,16,128]{2,0,1:T(8,128)S(1)}, u32[]{:S(2)}, u32[]{:S(2)}) async-start(f32[8,16,128]{2,0,1:T(8,128)} %copy.292), calls=%async_computation | async-start | bytes 131072 | tf_op jit(solution)/shard_map/all_to_all | solution.py:214
  110.6 2.0 %scatter_custom_fusion = f32[16384]{0:T(1024)S(1)} fusion(s32[256]{0:T(256)S(1)} %compare_select_fusion.2, f32[256]{0:T(256)S(1)} %and_select_fusion, f32[]{:T(128)} %constant.295.clone.1), kind=kCustom, calls=%fused_computation.47 | custom fusion | flops 256 | bytes 65540 | tf_op jit(solution)/shard_map/scatter-add | solution.py:241
  112.6 0.2 fusion
  112.9 4.3 %all-to-all-done = f32[8,16,128]{2,0,1:T(8,128)S(1)} async-done(((f32[8,16,128]{2,0,1:T(8,128)}), f32[8,16,128]{2,0,1:T(8,128)S(1)}, u32[]{:S(2)}, u32[]{:S(2)}) %all-to-all-start) | async-done | bytes 65568 | tf_op jit(solution)/shard_map/all_to_all | solution.py:214
  117.1 0.8 fusion.11
  (173 shorter events, 6.5 us)
Async XLA Ops:
  0.6 80.1 %collective-permute-start = (f32[1,32]{1,0:T(1,128)}, f32[1,32]{1,0:T(1,128)S(1)}, u32[]{:S(2)}, u32[]{:S(2)}) collective-permute-start(f32[1,32]{1,0:T(1,128)} %param.9), channel_id=1, source_target_pairs={{0,1},{1,2},{2,3},{3,4},{4,5},{5,6},{6,7},{7,8},{8,9},{9,10},{10,1... | collective-permute-start | bytes 392 | tf_op jit(solution)/shard_map/ppermute | solution.py:18
  1.1 84.2 %collective-permute-start.1 = (f32[2,128]{1,0:T(2,128)}, f32[2,128]{1,0:T(2,128)S(1)}, u32[]{:S(2)}, u32[]{:S(2)}) collective-permute-start(f32[2,128]{1,0:T(2,128)} %param.8), channel_id=1, source_target_pairs={{0,1},{1,2},{2,3},{3,4},{4,5},{5,6},{6,7},{7,8},{8,9},{9,10},{10,1... | collective-permute-start | bytes 3080 | tf_op jit(solution)/shard_map/ppermute | solution.py:18
  4.4 80.9 %collective-permute-start.2 = (f32[1,128]{1,0:T(1,128)S(1)}, f32[1,128]{1,0:T(1,128)S(1)}, u32[]{:S(2)}, u32[]{:S(2)}) collective-permute-start(f32[1,128]{1,0:T(1,128)S(1)} %slice.296), channel_id=1, source_target_pairs={{0,31},{1,0},{2,1},{3,2},{4,3},{5,4},{6,5},{7,6},{8,7},{9,8},{10,9... | collective-permute-start | bytes 1544 | tf_op jit(solution)/shard_map/ppermute | solution.py:18
  10.6 65.3 %copy-start = (f32[128,128]{1,0:T(8,128)S(1)}, f32[128,128]{1,0:T(8,128)}, u32[]{:S(2)}) copy-start(f32[128,128]{1,0:T(8,128)} %param.11) | copy-start | bytes 196612
  13.7 65.0 %copy-start.5 = (s32[256]{0:T(256)S(1)}, s32[256]{0:T(256)}, u32[]{:S(2)}) copy-start(s32[256]{0:T(256)} %param.14) | copy-start | bytes 3076
  13.7 65.0 %copy-start.3 = (s32[256]{0:T(256)S(1)}, s32[256]{0:T(256)}, u32[]{:S(2)}) copy-start(s32[256]{0:T(256)} %param.15) | copy-start | bytes 3076
  13.7 67.1 %copy-start.6 = (f32[1,32]{1,0:T(1,128)S(1)}, f32[1,32]{1,0:T(1,128)}, u32[]{:S(2)}) copy-start(f32[1,32]{1,0:T(1,128)} %param.9) | copy-start | bytes 388
  70.6 14.7 %copy-start.1 = (f32[2,128]{1,0:T(2,128)S(1)}, f32[2,128]{1,0:T(2,128)}, u32[]{:S(2)}) copy-start(f32[2,128]{1,0:T(2,128)} %param.8) | copy-start | bytes 3076
  70.6 15.8 %copy-start.4 = (f32[2,128]{1,0:T(2,128)S(1)}, f32[2,128]{1,0:T(2,128)}, u32[]{:S(2)}) copy-start(f32[2,128]{1,0:T(2,128)} %param.10) | copy-start | bytes 3076
  76.3 23.6 %collective-permute-start.6 = (f32[4,8,16,1]{3,2,1,0:T(8,128)S(1)}, f32[4,8,16,1]{3,2,1,0:T(8,128)S(1)}, u32[]{:S(2)}, u32[]{:S(2)}) collective-permute-start(f32[4,8,16,1]{3,2,1,0:T(8,128)S(1)} %get-tuple-element.35), channel_id=1, source_target_pairs={{16,0},{0,16},{17,1},{1,17},{18,2},{2,18},{19,3},{3,19},{20,4},{4,... | collective-permute-start | bytes 6152 | tf_op jit(solution)/shard_map/ppermute | solution.py:29
  78.3 21.7 %collective-permute-start.7 = (f32[4,8,16,1]{3,2,1,0:T(8,128)S(1)}, f32[4,8,16,1]{3,2,1,0:T(8,128)S(1)}, u32[]{:S(2)}, u32[]{:S(2)}) collective-permute-start(f32[4,8,16,1]{3,2,1,0:T(8,128)S(1)} %get-tuple-element.34), channel_id=1, source_target_pairs={{0,16},{16,0},{1,17},{17,1},{2,18},{18,2},{3,19},{19,3},{4,20},{20... | collective-permute-start | bytes 6152 | tf_op jit(solution)/shard_map/ppermute | solution.py:28
  86.5 12.3 %collective-permute-start.3 = (f32[2,128]{1,0:T(2,128)S(1)}, f32[2,128]{1,0:T(2,128)S(1)}, u32[]{:S(2)}, u32[]{:S(2)}) collective-permute-start(f32[2,128]{1,0:T(2,128)S(1)} %get-tuple-element.16), channel_id=1, source_target_pairs={{0,1},{1,2},{2,3},{3,4},{4,5},{5,6},{6,7},{7,8},{8,9},{9,10},{10,1... | collective-permute-start | bytes 3080 | tf_op jit(solution)/shard_map/ppermute | solution.py:18
  86.5 12.2 %collective-permute-start.4 = (f32[1,128]{1,0:T(1,128)S(1)}, f32[1,128]{1,0:T(1,128)S(1)}, u32[]{:S(2)}, u32[]{:S(2)}) collective-permute-start(f32[1,128]{1,0:T(1,128)S(1)} %slice.329), channel_id=1, source_target_pairs={{0,31},{1,0},{2,1},{3,2},{4,3},{5,4},{6,5},{7,6},{8,7},{9,8},{10,9... | collective-permute-start | bytes 1544 | tf_op jit(solution)/shard_map/ppermute | solution.py:18
  99.9 18.0 %copy-start.2 = (f32[2,128]{1,0:T(2,128)}, f32[2,128]{1,0:T(2,128)S(1)}, u32[]{:S(2)}) copy-start(f32[2,128]{1,0:T(2,128)S(1)} %multiply_add_fusion.8) | copy-start | bytes 3076
  99.9 4.7 %collective-permute-start.5 = (f32[1,128]{1,0:T(1,128)S(1)}, f32[1,128]{1,0:T(1,128)S(1)}, u32[]{:S(2)}, u32[]{:S(2)}) collective-permute-start(f32[1,128]{1,0:T(1,128)S(1)} %slice.356), channel_id=1, source_target_pairs={{0,31},{1,0},{2,1},{3,2},{4,3},{5,4},{6,5},{7,6},{8,7},{9,8},{10,9... | collective-permute-start | bytes 1544 | tf_op jit(solution)/shard_map/ppermute | solution.py:18
  100.1 12.5 %collective-permute-start.9 = (f32[4,1,16,130]{3,2,1,0:T(8,128)S(1)}, f32[4,1,16,130]{3,2,1,0:T(8,128)S(1)}, u32[]{:S(2)}, u32[]{:S(2)}) collective-permute-start(f32[4,1,16,130]{3,2,1,0:T(8,128)S(1)} %get-tuple-element.31), channel_id=1, source_target_pairs={{0,1},{1,2},{2,3},{3,4},{4,5},{5,6},{6,7},{7,8},{8,9},{9,10},{10,1... | collective-permute-start | bytes 99848 | tf_op jit(solution)/shard_map/ppermute | solution.py:28
  100.6 12.0 %collective-permute-start.8 = (f32[4,1,16,130]{3,2,1,0:T(8,128)S(1)}, f32[4,1,16,130]{3,2,1,0:T(8,128)S(1)}, u32[]{:S(2)}, u32[]{:S(2)}) collective-permute-start(f32[4,1,16,130]{3,2,1,0:T(8,128)S(1)} %get-tuple-element.30), channel_id=1, source_target_pairs={{1,0},{2,1},{3,2},{4,3},{5,4},{6,5},{7,6},{8,7},{9,8},{10,9},{11,1... | collective-permute-start | bytes 99848 | tf_op jit(solution)/shard_map/ppermute | solution.py:29
  106.5 10.6 %all-to-all-start = ((f32[8,16,128]{2,0,1:T(8,128)}), f32[8,16,128]{2,0,1:T(8,128)S(1)}, u32[]{:S(2)}, u32[]{:S(2)}) async-start(f32[8,16,128]{2,0,1:T(8,128)} %copy.292), calls=%async_computation | async-start | bytes 131072 | tf_op jit(solution)/shard_map/all_to_all | solution.py:214
where the time goes:
time: 118 us
  local copies, waits for them, and re-layouts  82.1 us (70%)
  starting transfers between devices  22.2 us (19%)
  other arithmetic  7.19 us (6%)
  waiting for transfers between devices  4.31 us (4%)
  between operations  1.32 us (1%)
    gather x2, local copies, waits for them, and re-layouts, body(): jnp.take(level_table, crystal_label_map, axis=1) * frozen_share_map[None]  62.2 us
    ppermute x6, starting transfers between devices, passed_along(): lax.ppermute(array, axis, [(i, (i + by) % count) for i in range(count)])  11.9 us
    gather x9, local copies, waits for them, and re-layouts, element_matrix(): columns[within, local][None, :]  6.86 us
    ppermute x2, starting transfers between devices, extended_2(): after = lax.ppermute(first, axis, down)  5.93 us
    all_to_all x1, waiting for transfers between devices, body(): lax.all_to_all(slab_cells, 'slab', split_axis=1, concat_axis=0, tiled=True)  4.29 us
    all_to_all x1, starting transfers between devices, body(): lax.all_to_all(slab_cells, 'slab', split_axis=1, concat_axis=0, tiled=True)  3.73 us
    div x1, local copies, waits for them, and re-layouts, body(): level_table = growth_reach_table.T.astype(jnp.float32) / 4.0  3.06 us
  transfers between devices with their start and end apart: 11, of which 1 were waited for; matrix products, arithmetic and copies ran while one was open for 76% of the time, Pallas kernels for 0%

commit v1 on v0

v1 whole, which is shorter than its diff:
```python
import functools

import jax
import jax.numpy as jnp
import numpy as np
from jax import lax
from jax.experimental import pallas as pl
from jax.experimental.pallas import tpu as pltpu
from jax.sharding import PartitionSpec as P

HEX_COUNT_LATER = 2
CPC = 8
LANES = 128
HIGHEST = lax.Precision.HIGHEST
STEP = 0.004
AXES = ("grp", "slab")
VMEM = pl.BlockSpec(memory_space=pltpu.VMEM)
PARAMS = pltpu.CompilerParams(vmem_limit_bytes=48 * 1024 * 1024)


def up_to(value, unit):
    return -(-value // unit) * unit


def split_index(value, by):
    if by & (by - 1) == 0:
        return value >> (by.bit_length() - 1), value & (by - 1)
    quotient = lax.div(value, jnp.full_like(value, by))
    return quotient, value - quotient * by


def pick_codes(table_ref, labels):
    half = table_ref.shape[0]
    tile, lane = labels >> 7, labels & (LANES - 1)
    upper = tile >= half
    row = jnp.where(upper, tile - half, tile)
    found = jnp.zeros(labels.shape, jnp.int32)
    for r in range(half):
        line = jnp.broadcast_to(table_ref[r : r + 1, :], labels.shape)
        here = jnp.take_along_axis(line, lane, axis=1, mode="promise_in_bounds")
        found = jnp.where(row == r, here, found)
    return jnp.where(upper, found >> 12, found) & 4095


def level(code, direction):
    return (((code >> (2 * direction)) & 3) + 1).astype(jnp.float32)


def cells_kernel(
    depth, flat, table_ref, label_ref, frozen_ref, slot_ref, seed_ref,
    packed_ref, gathered_ref, nucleation_ref, faces_ref, line_ref, code_ref,
):
    count = table_ref.shape[1]
    half = packed_ref.shape[0]
    edge_x, wide = frozen_ref.shape
    place = lax.broadcasted_iota(jnp.int32, table_ref.shape, 0)
    line_ref[...] = jnp.zeros(line_ref.shape, jnp.int32)
    word = jnp.sum((table_ref[...] - 1) << (2 * place), axis=0, keepdims=True)
    line_ref[0:1, 0:count] = word
    for r in range(half):
        low = line_ref[0:1, r * LANES : (r + 1) * LANES]
        high = line_ref[0:1, (r + half) * LANES : (r + half + 1) * LANES]
        packed_ref[r : r + 1, :] = low | (high << 12)

    def look_up(chunk, carry):
        rows = pl.ds(pl.multiple_of(chunk * 8, 8), 8)
        for t in range(wide // LANES):
            lanes = pl.ds(t * LANES, LANES)
            code_ref[rows, lanes] = pick_codes(packed_ref, label_ref[rows, lanes])
        return carry

    lax.fori_loop(0, edge_x // 8, look_up, 0, unroll=4)
    frozen = frozen_ref[...] * 0.25
    code = code_ref[...]
    shares = [frozen * level(code, d) for d in range(6)]
    line_x = lax.broadcasted_iota(jnp.int32, (edge_x, wide), 0)
    lane = lax.broadcasted_iota(jnp.int32, (edge_x, wide), 1)
    deep = lane % depth if depth & (depth - 1) else lane & (depth - 1)
    total = jnp.where(line_x == edge_x - 1, 0.0, pltpu.roll(shares[0], edge_x - 1, 0))
    total += jnp.where(line_x == 0, 0.0, pltpu.roll(shares[1], 1, 0))
    total += jnp.where(lane >= flat - depth, 0.0, pltpu.roll(shares[2], wide - depth, 1))
    total += jnp.where(lane < depth, 0.0, pltpu.roll(shares[3], depth, 1))
    total += jnp.where(
        deep == depth - 1, pltpu.roll(shares[4], depth - 1, 1), pltpu.roll(shares[4], wide - 1, 1)
    )
    total += jnp.where(
        deep == 0, pltpu.roll(shares[5], wide - (depth - 1), 1), pltpu.roll(shares[5], 1, 1)
    )
    gathered_ref[...] = total
    sides = jnp.transpose(jnp.where(lane < depth, shares[2], shares[3]))
    faces_ref[0:depth, :] = sides[0:depth]
    faces_ref[depth : 2 * depth, :] = sides[flat - depth : flat]
    sites = seed_ref.shape[0]
    codes = pick_codes(packed_ref, seed_ref[...])
    worth = sum(level(codes, d) for d in range(6))
    site_x, site_lane = split_index(slot_ref[...], flat)
    at_x = lax.broadcasted_iota(jnp.int32, (edge_x, LANES), 0)
    at_lane = lax.broadcasted_iota(jnp.int32, (wide, LANES), 0)
    added = jnp.zeros((edge_x, wide), jnp.float32)
    for r in range(sites):
        left = jnp.where(at_x == site_x[r : r + 1], worth[r : r + 1], 0.0).astype(jnp.bfloat16)
        right = jnp.where(at_lane == site_lane[r : r + 1], 1.0, 0.0).astype(jnp.bfloat16)
        added += lax.dot_general(
            left, right, (((1,), (1,)), ((), ())), preferred_element_type=jnp.float32
        )
    nucleation_ref[...] = added * (1.0 / 6.0)


def spread_tables(width, plane):
    rows_y, deep = width // plane, plane // 2
    along = np.zeros((rows_y // 2, rows_y), np.float32)
    down = np.zeros((deep, plane), np.float32)
    for table in (along, down):
        for element in range(table.shape[0]):
            for local, weight in enumerate((1, 4, 1)):
                table[element, (2 * element + local) % table.shape[1]] += weight
    first_y = np.zeros_like(along)
    first_z = np.zeros_like(down)
    first_y[np.arange(rows_y // 2), 2 * np.arange(rows_y // 2)] = 1
    first_z[np.arange(deep), 2 * np.arange(deep)] = 1
    full = [np.kron(along, down), np.kron(first_y, down), np.kron(along, first_z)]
    out = np.zeros((width, 3 * width), np.float32)
    out[: width // 4] = np.concatenate(full, 1)
    return out


def advance(plane, even, odd, heat_even, heat_odd, kappa, spread):
    rows, width = even.shape
    up = lambda v: pltpu.roll(v, rows - 1, 0)
    down = lambda v: pltpu.roll(v, 1, 0)
    turn = lambda v, by: pltpu.roll(v, by % width, 1)
    lane = lax.broadcasted_iota(jnp.int32, (rows, width), 1)
    row_y, deep = split_index(lane, plane)
    lines = jnp.dot(kappa, spread, precision=HIGHEST, preferred_element_type=jnp.float32)
    lines = lines * (1.0 / 108.0)
    along_x, along_y, along_z = (lines[:, i * width : (i + 1) * width] for i in range(3))
    y_even, y_odd = along_y + down(along_y), 4.0 * along_y
    z_even, z_odd = along_z + down(along_z), 4.0 * along_z
    inverse = 27.0 * jnp.where(row_y & 1 == 1, 0.5, 1.0) * jnp.where(deep & 1 == 1, 0.5, 1.0)
    scale_even, scale_odd = inverse, 0.5 * inverse

    def bend(first, second, third, coefficient):
        curve = (4.0 * coefficient) * (first - 2.0 * second + third)
        slope = (3.0 * coefficient) * (third - first)
        return curve - slope, -2.0 * curve, curve + slope

    def in_plane(values, along_y, along_z):
        a, b, c = bend(values, turn(values, -plane), turn(values, -2 * plane), along_y)
        result = a + turn(b, plane) + turn(c, 2 * plane)
        third = jnp.where(deep == plane - 2, turn(values, plane - 2), turn(values, -2))
        a, b, c = bend(values, turn(values, -1), third, along_z)
        return result + a + turn(b, 1) + jnp.where(deep == 0, turn(c, 2 - plane), turn(c, 2))

    def missing(v_even, v_odd):
        a, b, c = bend(v_even, v_odd, up(v_even), along_x)
        k_even = a + down(c) + in_plane(v_even, y_even, z_even)
        k_odd = b + in_plane(v_odd, y_odd, z_odd)
        return heat_even - k_even, heat_odd - k_odd

    one_even, one_odd = missing(even, odd)
    two_even, two_odd = missing(
        even + (STEP * scale_even) * one_even, odd + (STEP * scale_odd) * one_odd
    )
    return (
        even + (0.5 * STEP * scale_even) * (one_even + two_even),
        odd + (0.5 * STEP * scale_odd) * (one_odd + two_odd),
    )


def heat_kernel(plane, layers, first_row, state_ref, spread_ref, new_ref, even_ref, odd_ref):
    even, odd = advance(plane, *(state_ref[i] for i in range(5)), spread_ref[...])
    even_ref[...] = even
    odd_ref[...] = odd
    start = first_row()
    for layer in range(layers):
        new_ref[2 * layer : 2 * layer + 1, :] = even_ref[pl.ds(start + layer, 1), :]
        new_ref[2 * layer + 1 : 2 * layer + 2, :] = odd_ref[pl.ds(start + layer, 1), :]


def basis(step):
    point = (step.astype(jnp.float32) + 0.5) / CPC
    return (
        2.0 * (point - 0.5) * (point - 1.0),
        -4.0 * point * (point - 1.0),
        2.0 * point * (point - 0.5),
    )


def finish_kernel(
    plane, depth, flat, layers, first_row, cell_row, wraps,
    state_ref, spread_ref, weave_ref, packed_ref, edge_ref, behind_ref, ahead_ref,
    gathered_ref, nucleation_ref, frozen_ref, *refs,
):
    solid_ref, even_ref, odd_ref, side_ref, extra_ref = refs[-5:]
    edge_x, wide = frozen_ref.shape
    rows = state_ref.shape[1]
    even, odd = advance(plane, *(state_ref[i] for i in range(5)), spread_ref[...])
    if first_row is not None:
        new_ref = refs[0]
        even_ref[:, 0 : even.shape[1]] = even
        odd_ref[:, 0 : even.shape[1]] = odd
        start = first_row()
        for layer in range(layers):
            new_ref[2 * layer : 2 * layer + 1, :] = even_ref[pl.ds(start + layer, 1), 0 : even.shape[1]]
            new_ref[2 * layer + 1 : 2 * layer + 2, :] = odd_ref[pl.ds(start + layer, 1), 0 : even.shape[1]]
    side_ref[...] = jnp.zeros(side_ref.shape, jnp.float32)
    side_ref[0:depth, :] = behind_ref[...]
    side_ref[flat - depth : flat, :] = ahead_ref[...]
    extra_ref[...] = gathered_ref[...] + jnp.transpose(side_ref[...])
    for t in range(wide // LANES):
        lanes = slice(t * LANES, (t + 1) * LANES)
        rough = jnp.concatenate([edge_ref[:, lanes], jnp.zeros((4, LANES), jnp.float32)], 0)
        codes = pick_codes(packed_ref, rough.astype(jnp.int32))
        behind = rough[0:1] * level(codes[1:2], 1) * 0.25
        ahead = rough[2:3] * level(codes[3:4], 0) * 0.25
        extra_ref[0:1, lanes] += behind
        extra_ref[edge_x - 1 : edge_x, lanes] += ahead
    weave = weave_ref[...]
    even_ref[:, 0:wide] = jnp.dot(even, weave, precision=HIGHEST, preferred_element_type=jnp.float32)
    odd_ref[:, 0:wide] = jnp.dot(odd, weave, precision=HIGHEST, preferred_element_type=jnp.float32)
    first, middle, last = basis(lax.broadcasted_iota(jnp.int32, (CPC, wide), 0))
    base = cell_row()
    for a in range(edge_x // CPC):
        cells = slice(a * CPC, (a + 1) * CPC)
        later = base + (a + 1)
        if wraps:
            later = lax.rem(later, rows)
        temperature = (
            first * even_ref[pl.ds(base + a, 1), 0:wide]
            + middle * odd_ref[pl.ds(base + a, 1), 0:wide]
            + last * even_ref[pl.ds(later, 1), 0:wide]
        )
        under = jnp.maximum(-temperature, 0.0)
        rate = under * (under * extra_ref[cells, :] + nucleation_ref[cells, :])
        frozen = frozen_ref[cells, :]
        solid_ref[cells, :] = frozen + (1.0 - frozen) * (1.0 - jnp.exp(-rate))


def weave_table(width, plane, depth, edge_y, start_y, first_cell, rows_total):
    wide = up_to(edge_y * depth, LANES)
    node, cell = jnp.arange(width)[:, None], jnp.arange(wide)[None, :]
    cell_y, cell_z = first_cell + cell // depth, cell % depth
    step_y = jnp.remainder(start_y + node // plane - 2 * (cell_y // CPC), rows_total)
    step_z = jnp.remainder(node % plane - 2 * (cell_z // CPC), plane)
    take = lambda step, at: sum(jnp.where(step == i, v, 0.0) for i, v in enumerate(basis(at % CPC)))
    return jnp.where(cell < edge_y * depth, take(step_y, cell_y) * take(step_z, cell_z), 0.0)


def lines(values, width):
    flat = values.reshape(-1)
    return jnp.pad(flat, (0, -flat.shape[0] % width)).reshape(-1, width)


def body(
    thermal_state_values,
    thermal_kappa_values,
    nodal_heating_input,
    frozen_share_map,
    crystal_label_map,
    growth_reach_table,
    seed_site_slots,
    seed_crystal_label,
):
    groups, slabs = lax.axis_size("grp"), lax.axis_size("slab")
    devices = groups * slabs
    group, slab = lax.axis_index("grp"), lax.axis_index("slab")
    me = group * slabs + slab
    layers, elements = thermal_kappa_values.shape
    plane = 2 * HEX_COUNT_LATER
    depth = CPC * HEX_COUNT_LATER
    flat = thermal_state_values.shape[1]
    rows_y = flat // plane
    edge_x, flat_cells = frozen_share_map.shape
    edge_y = flat_cells // depth
    wide = up_to(flat_cells, LANES)
    all_layers = layers * devices

    def swapped(array, bit):
        return lax.ppermute(array, AXES, [(i, i ^ (1 << bit)) for i in range(devices)])

    def widened(array):
        return jnp.pad(array, ((0, 0), (0, wide - flat_cells)))

    unit = layers * flat
    held = jnp.concatenate(
        [
            jnp.swapaxes(thermal_state_values.reshape(layers, 2, flat), 0, 1).reshape(2, unit),
            jnp.swapaxes(nodal_heating_input.reshape(layers, 2, flat), 0, 1).reshape(2, unit),
            jnp.pad(thermal_kappa_values, ((0, 0), (0, flat - elements))).reshape(1, unit),
        ],
        0,
    )
    frozen, label = widened(frozen_share_map), widened(crystal_label_map)
    low_edge = jnp.stack([frozen[0], label[0].astype(jnp.float32)])
    high_edge = jnp.stack([frozen[-1], label[-1].astype(jnp.float32)])
    seeds = up_to(seed_site_slots.shape[0], LANES)
    short = seeds - seed_site_slots.shape[0]
    packed, gathered, nucleation, faces = pl.pallas_call(
        functools.partial(cells_kernel, depth, flat_cells),
        out_shape=(
            jax.ShapeDtypeStruct((up_to(growth_reach_table.shape[0], 2 * LANES) // (2 * LANES), LANES), jnp.int32),
            jax.ShapeDtypeStruct((edge_x, wide), jnp.float32),
            jax.ShapeDtypeStruct((edge_x, wide), jnp.float32),
            jax.ShapeDtypeStruct((2 * depth, edge_x), jnp.float32),
        ),
        in_specs=[VMEM] * 5,
        out_specs=[VMEM] * 4,
        scratch_shapes=[
            pltpu.VMEM((8, up_to(growth_reach_table.shape[0], 2 * LANES)), jnp.int32),
            pltpu.VMEM((edge_x, wide), jnp.int32),
        ],
        compiler_params=PARAMS,
        name="cells",
    )(
        growth_reach_table.T,
        label,
        frozen,
        jnp.pad(seed_site_slots, (0, short), constant_values=-1).reshape(-1, LANES),
        jnp.pad(seed_crystal_label, (0, short)).reshape(-1, LANES),
    )

    held = held[:, None]
    to_behind, to_ahead = faces[:depth], faces[depth:]
    behind = ahead = edges = None
    for bit in reversed(range(devices.bit_length() - 1)):
        sent = [lines(held, unit)]
        if groups == 2 and 1 << bit == slabs:
            sent.append(lines(jnp.concatenate([high_edge, low_edge]), unit))
        low = (1 << bit) - 1
        goes_on = (slab & low) == low
        if bit > 0 and 1 << bit < slabs:
            face = jnp.where(goes_on, to_ahead, to_behind)
            sent.append(lines(face, unit))
        if bit == 0:
            sent += [lines(to_ahead, unit), lines(to_behind, unit)]
        got = swapped(jnp.concatenate(sent, 0), bit)
        parts, at = [], 0
        for part in sent:
            parts.append(got[at : at + part.shape[0]])
            at += part.shape[0]
        theirs = parts[0].reshape(held.shape)
        upper = (me >> bit) & 1 == 1
        held = jnp.stack(
            [jnp.where(upper, theirs, held), jnp.where(upper, held, theirs)], 2
        ).reshape(held.shape[0], 2 * held.shape[1], unit)
        if groups == 2 and 1 << bit == slabs:
            edges = parts[1].reshape(-1)[: 4 * wide].reshape(4, wide)
        if bit > 0 and 1 << bit < slabs:
            face = parts[1].reshape(-1)[: depth * edge_x].reshape(depth, edge_x)
            to_ahead = jnp.where(goes_on, face, to_ahead)
            to_behind = jnp.where((slab & low) == 0, face, to_behind)
        if bit == 0:
            behind, ahead = (
                part.reshape(-1)[: depth * edge_x].reshape(depth, edge_x) for part in parts[1:]
            )
    if edges is None:
        ring = [(i, (i + 1) % groups) for i in range(groups)]
        edges = jnp.concatenate(
            [
                lax.ppermute(high_edge, "grp", ring),
                lax.ppermute(low_edge, "grp", [(j, i) for i, j in ring]),
            ]
        )
    held = held.reshape(5, all_layers, flat)

    def window(first_layer, need_layers, first_element, need_elements):
        rows, width = up_to(need_layers, 8), up_to(need_elements * 2 * plane, LANES)
        part, start_layer, start_y = held, 0, 0
        if 2 * rows <= all_layers:
            start_layer = first_layer
            part = lax.dynamic_slice_in_dim(
                jnp.concatenate([part, part[:, : rows]], 1),
                jnp.remainder(start_layer, all_layers), rows, 1,
            )
        if 2 * width <= flat:
            start_y = 2 * first_element
            shifted = lambda v, by, size: lax.dynamic_slice_in_dim(
                jnp.concatenate([v, v[..., :size]], -1), by, size, v.ndim - 1
            )
            start = jnp.remainder(first_element, rows_y // 2)
            part = jnp.concatenate(
                [
                    shifted(part[:4], start * 2 * plane, width),
                    jnp.pad(
                        shifted(part[4:, :, :elements], start * HEX_COUNT_LATER, width // 4),
                        ((0, 0), (0, 0), (0, width - width // 4)),
                    ),
                ],
                0,
            )
        return part, start_layer, start_y

    brick_layers = edge_x // CPC
    first_cell = slab * edge_y
    state, start_layer, start_y = window(
        group * brick_layers - 2,
        brick_layers + 5,
        first_cell // CPC - 2,
        (edge_y + CPC - 2) // CPC + 6,
    )
    width = state.shape[2]
    whole = state.shape == held.shape
    weave = weave_table(width, plane, depth, edge_y, start_y, first_cell, rows_y)

    def place(start, layer):
        if not isinstance(start, int):
            return lambda: 2
        return lambda: layer(lax.axis_index("grp"), lax.axis_index("slab"))

    own_layer = lambda g, s: (g * slabs + s) * layers
    cell_row = place(start_layer, lambda g, s: g * brick_layers)
    own_row = place(start_layer, own_layer)
    new_shape = jax.ShapeDtypeStruct((2 * layers, flat), jnp.float32)
    solid_shape = jax.ShapeDtypeStruct((edge_x, wide), jnp.float32)
    span = max(width, wide)
    results = pl.pallas_call(
        functools.partial(
            finish_kernel, plane, depth, flat_cells, layers,
            own_row if whole else None, cell_row, isinstance(start_layer, int),
        ),
        out_shape=(new_shape, solid_shape) if whole else (solid_shape,),
        in_specs=[VMEM] * 10,
        out_specs=(VMEM,) * (1 + whole),
        scratch_shapes=[
            pltpu.VMEM((state.shape[1], span), jnp.float32),
            pltpu.VMEM((state.shape[1], span), jnp.float32),
            pltpu.VMEM((wide, edge_x), jnp.float32),
            pltpu.VMEM((edge_x, wide), jnp.float32),
        ],
        compiler_params=PARAMS,
        name="finish",
    )(
        state, jnp.asarray(spread_tables(width, plane)), weave, packed, edges,
        behind, ahead, gathered, nucleation, frozen,
    )
    if whole:
        new_field, new_solid = results
    else:
        (new_solid,) = results
        state, start_layer, _ = window(me * layers - 2, layers + 4, 0, rows_y // 2)
        own_row = place(start_layer, own_layer)
        new_field = pl.pallas_call(
            functools.partial(heat_kernel, plane, layers, own_row),
            out_shape=new_shape,
            in_specs=[VMEM] * 2,
            out_specs=VMEM,
            scratch_shapes=[pltpu.VMEM(state.shape[1:], jnp.float32)] * 2,
            compiler_params=PARAMS,
            name="heat",
        )(state, jnp.asarray(spread_tables(flat, plane)))
    return new_field, new_solid[:, :flat_cells]


def solution(mesh):
    in_specs = (
        P(("grp", "slab"), None),
        P(("grp", "slab"), None),
        P(("grp", "slab"), None),
        P("grp", "slab"),
        P("grp", "slab"),
        P(),
        P(("grp", "slab")),
        P(("grp", "slab")),
    )
    out_specs = (P(("grp", "slab"), None), P("grp", "slab"))
    return jax.shard_map(body, mesh=mesh, in_specs=in_specs, out_specs=out_specs, check_vma=False)
```

time: 118 us -> 27.4 us (0.23)
  local copies, waits for them, and re-layouts: 82.1 us -> 5.74 us
  starting transfers between devices: 22.2 us -> 8.94 us
  other arithmetic: 7.19 us -> 1.09 us
  waiting for transfers between devices: 4.31 us -> 7.63 us
  Pallas kernels: 0 us -> 2.69 us
    gather x12 -> x0, local copies, waits for them, and re-layouts: 70.8 us -> none  [the longest x2 62.2 us: body(): jnp.take(level_table, crystal_label_map, axis=1) * frozen_share_map[None]]
    ppermute x10 -> x5, starting transfers between devices: 18.5 us -> 8.94 us  [swapped(): lax.ppermute(array, AXES, [(i, i ^ 1 << bit) for i in range(devices)])]
    ppermute x10 -> x5, waiting for transfers between devices: 0.03 us -> 7.63 us  [swapped(): lax.ppermute(array, AXES, [(i, i ^ 1 << bit) for i in range(devices)])]
    unnamed x16 -> x20, local copies, waits for them, and re-layouts: 0.2 us -> 4.83 us
    all_to_all x1 -> x0, waiting for transfers between devices: 4.29 us -> none  [body(): lax.all_to_all(slab_cells, 'slab', split_axis=1, concat_axis=0, tiled=True)]
    all_to_all x1 -> x0, starting transfers between devices: 3.73 us -> none  [body(): lax.all_to_all(slab_cells, 'slab', split_axis=1, concat_axis=0, tiled=True)]
    div x1 -> x0, local copies, waits for them, and re-layouts: 3.06 us -> none  [body(): level_table = growth_reach_table.T.astype(jnp.float32) / 4.0]
    mul x27 -> x0, local copies, waits for them, and re-layouts: 2.7 us -> none  [the longest x12 1.33 us: contract(): terms.append(WEIGHTS[point] * coefficient * slope)]
  transfers between devices with their start and end apart: 11 -> 5, of which waited for: 1 -> 4; matrix products, arithmetic and copies ran while one was open for 76% -> 1% of each run, Pallas kernels for 0% -> 5%
where the time goes in v1:
time: 27.4 us; the launch traced here: 27 us
  starting transfers between devices  8.94 us (33%)
  waiting for transfers between devices  7.63 us (28%)
  local copies, waits for them, and re-layouts  5.74 us (21%)
  Pallas kernels  2.69 us (10%)
  other arithmetic  1.09 us (4%)
  between operations  0.9 us (3%)
    ppermute x5, starting transfers between devices, swapped(): lax.ppermute(array, AXES, [(i, i ^ 1 << bit) for i in range(devices)])  8.94 us
    ppermute x5, waiting for transfers between devices, swapped(): lax.ppermute(array, AXES, [(i, i ^ 1 << bit) for i in range(devices)])  7.63 us
    unnamed x20, local copies, waits for them, and re-layouts  4.83 us
    pallas_call x1, Pallas kernels, body(): pl.pallas_call(functools.partial(finish_kernel, plane, depth, flat_cells,...  1.4 us
    pallas_call x1, Pallas kernels, body(): pl.pallas_call(functools.partial(cells_kernel, depth, flat_cells), out_sh...  1.29 us
    convert_element_type x1, other arithmetic, body(): low_edge = jnp.stack([frozen[0], label[0].astype(jnp.float32)])  0.72 us
    slice x1, local copies, waits for them, and re-layouts, body(): low_edge = jnp.stack([frozen[0], label[0].astype(jnp.float32)])  0.72 us
  transfers between devices with their start and end apart: 5, of which 4 were waited for; matrix products, arithmetic and copies ran while one was open for 1% of the time, Pallas kernels for 5%

profile of v1, /device:TPU:0, one launch (start us, length us, event | category | flops | bytes accessed | tf_op | source)
XLA Modules:
  0.0 27.0 jit_solution(16823709625511218230)
XLA Ops:
  0.6 0.7 %slice_convert_fusion = (f32[1,128]{1,0:T(1,128)S(1)}, f32[1,128]{1,0:T(1,128)S(1)}) fusion(s32[128,128]{1,0:T(8,128)} %label_ref.1), kind=kLoop, calls=%fused_computation.74 | loop fusion | flops 256 | bytes 2048 | tf_op jit(solution)/shard_map/convert_element_type | solution.py:294
  1.3 0.0 copy-start.9
  1.4 0.7 %fusion.11 = (f32[1,128]{1,0:T(1,128)S(1)}, f32[1,128]{1,0:T(1,128)S(1)}) fusion(f32[128,128]{1,0:T(8,128)} %frozen_ref.3), kind=kLoop, calls=%fused_computation.80 | loop fusion | bytes 2048 | tf_op jit(solution)/shard_map/slice | solution.py:294
  2.1 0.0 copy-done.9
  2.1 0.0 copy-start.8
  2.1 0.0 copy-start.7
  2.1 0.7 %copy-done.8 = f32[2,128]{1,0:T(2,128)S(1)} copy-done((f32[2,128]{1,0:T(2,128)S(1)}, f32[2,128]{1,0:T(2,128)}, u32[]{:S(2)}) %copy-start.8) | copy-done | bytes 1048
  2.8 0.0 copy-done.7
  2.8 3.0 %collective-permute-start = (f32[9,128]{1,0:T(8,128)S(1)}, f32[9,128]{1,0:T(8,128)S(1)}, u32[]{:S(2)}, u32[]{:S(2)}) collective-permute-start(f32[9,128]{1,0:T(8,128)S(1)} %concatenate.20), channel_id=1, source_target_pairs={{0,16},{1,17},{2,18},{3,19},{4,20},{5,21},{6,22},{7,23},{8,24},{9,... | collective-permute-start | bytes 13832 | tf_op jit(solution)/shard_map/ppermute | solution.py:279
  5.8 0.0 copy-start.6
  5.9 0.0 copy-start.5
  5.9 0.7 %copy-done.6 = s32[256]{0:T(256)S(1)} copy-done((s32[256]{0:T(256)S(1)}, s32[256]{0:T(256)}, u32[]{:S(2)}) %copy-start.6) | copy-done | bytes 1048
  6.5 0.0 copy-done.5
  6.5 0.0 copy-start
  6.5 0.8 %copy-done = f32[128,128]{1,0:T(8,128)S(1)} copy-done((f32[128,128]{1,0:T(8,128)S(1)}, f32[128,128]{1,0:T(8,128)}, u32[]{:S(2)}) %copy-start) | copy-done | bytes 65560
  7.4 0.0 copy-start.2
  7.4 0.9 %copy-done.2 = s32[8000,6]{0,1:T(8,128)S(1)} copy-done((s32[8000,6]{0,1:T(8,128)S(1)}, s32[8000,6]{0,1:T(8,128)}, u32[]{:S(2)}) %copy-start.2) | copy-done | bytes 192024
  8.3 0.0 copy-start.4
  8.3 0.8 %copy-done.4 = s32[128,128]{1,0:T(8,128)S(1)} copy-done((s32[128,128]{1,0:T(8,128)S(1)}, s32[128,128]{1,0:T(8,128)}, u32[]{:S(2)}) %copy-start.4) | copy-done | bytes 65560
  9.2 1.3 %cells.1 = (s32[32,128]{1,0:T(8,128)S(1)}, f32[128,128]{1,0:T(8,128)S(1)}, f32[128,128]{1,0:T(8,128)S(1)}, f32[32,128]{1,0:T(8,128)S(1)}) custom-call(s32[6,8000]{1,0:T(8,128)S(1)} %bitcast.26, s32[128,128]{1,0:T(8,128)S(1)} %copy-done.4, f32[128,128]{1,0:T(8,128)S(1)} %copy-done, s32[2,128]{1,0:T(2,128)S(1)} %bitcast.27, s32[2,128]{1,0:T(2,128)S(1)} %bitcast.28), custom_call_target="tpu_custom_call" | custom-call | tf_op jit(solution)/shard_map/cells/pallas_call | solution.py:298
  10.5 0.0 collective-permute-done
  10.6 2.7 %collective-permute-start.1 = (f32[26,128]{1,0:T(8,128)S(1)}, f32[26,128]{1,0:T(8,128)S(1)}, u32[]{:S(2)}, u32[]{:S(2)}) collective-permute-start(f32[26,128]{1,0:T(8,128)S(1)} %pad_maximum_fusion.6), channel_id=1, source_target_pairs={{0,8},{1,9},{2,10},{3,11},{4,12},{5,13},{6,14},{7,15},{8,0},{9,1},... | collective-permute-start | bytes 39944 | tf_op jit(solution)/shard_map/ppermute | solution.py:279
  13.2 2.0 %collective-permute-done.1 = f32[26,128]{1,0:T(8,128)S(1)} collective-permute-done((f32[26,128]{1,0:T(8,128)S(1)}, f32[26,128]{1,0:T(8,128)S(1)}, u32[]{:S(2)}, u32[]{:S(2)}) %collective-permute-start.1) | collective-permute-done | bytes 13344 | tf_op jit(solution)/shard_map/ppermute | solution.py:279
  15.4 1.6 %collective-permute-start.2 = (f32[36,128]{1,0:T(8,128)S(1)}, f32[36,128]{1,0:T(8,128)S(1)}, u32[]{:S(2)}, u32[]{:S(2)}) collective-permute-start(f32[36,128]{1,0:T(8,128)S(1)} %pad_maximum_fusion.4), channel_id=1, source_target_pairs={{0,4},{1,5},{2,6},{3,7},{4,0},{5,1},{6,2},{7,3},{8,12},{9,13},{10,... | collective-permute-start | bytes 55304 | tf_op jit(solution)/shard_map/ppermute | solution.py:279
  17.0 2.2 %collective-permute-done.2 = f32[36,128]{1,0:T(8,128)S(1)} collective-permute-done((f32[36,128]{1,0:T(8,128)S(1)}, f32[36,128]{1,0:T(8,128)S(1)}, u32[]{:S(2)}, u32[]{:S(2)}) %collective-permute-start.2) | collective-permute-done | bytes 18464 | tf_op jit(solution)/shard_map/ppermute | solution.py:279
  19.3 1.6 %collective-permute-start.3 = (f32[56,128]{1,0:T(8,128)S(1)}, f32[56,128]{1,0:T(8,128)S(1)}, u32[]{:S(2)}, u32[]{:S(2)}) collective-permute-start(f32[56,128]{1,0:T(8,128)S(1)} %pad_maximum_fusion.3), channel_id=1, source_target_pairs={{0,2},{1,3},{2,0},{3,1},{4,6},{5,7},{6,4},{7,5},{8,10},{9,11},{10,... | collective-permute-start | bytes 86024 | tf_op jit(solution)/shard_map/ppermute | solution.py:279
  20.9 2.3 %collective-permute-done.3 = f32[56,128]{1,0:T(8,128)S(1)} collective-permute-done((f32[56,128]{1,0:T(8,128)S(1)}, f32[56,128]{1,0:T(8,128)S(1)}, u32[]{:S(2)}, u32[]{:S(2)}) %collective-permute-start.3) | collective-permute-done | bytes 28704 | tf_op jit(solution)/shard_map/ppermute | solution.py:279
  23.3 0.1 collective-permute-start.4
  23.4 0.2 multiply_select_fusion.weave_ref
  23.6 1.0 %collective-permute-done.4 = f32[112,128]{1,0:T(8,128)S(1)} collective-permute-done((f32[112,128]{1,0:T(8,128)S(1)}, f32[112,128]{1,0:T(8,128)S(1)}, u32[]{:S(2)}, u32[]{:S(2)}) %collective-permute-start.4) | collective-permute-done | bytes 57376 | tf_op jit(solution)/shard_map/ppermute | solution.py:279
  24.7 0.0 copy-start.3
  24.7 0.0 copy-start.1
  24.8 0.8 %copy-done.3 = f32[128,384]{1,0:T(8,128)S(1)} copy-done((f32[128,384]{1,0:T(8,128)S(1)}, f32[128,384]{1,0:T(8,128)}, u32[]{:S(2)}) %copy-start.3) | copy-done | bytes 196632
  25.6 0.0 copy-done.1
  25.6 1.4 %finish.1 = (f32[2,128]{1,0:T(2,128)}, f32[128,128]{1,0:T(8,128)}) custom-call(f32[5,32,128]{2,1,0:T(8,128)S(1)} %bitcast.25, f32[128,384]{1,0:T(8,128)S(1)} %copy-done.3, f32[128,128]{1,0:T(8,128)S(1)} %multiply_select_fusion.weave_ref, s32[32,128]{1,0:T(8,128)S(1)} %get-tuple-element.7.packed_ref, f32[4,128]{1,0:T(4,128)S(1)} %slice.76.edge_ref, ...), custom_call_target="tpu_custom_call" | custom-call | tf_op jit(solution)/shard_map/finish/pallas_call | solution.py:416
  (40 shorter events, 0.4 us)
Async XLA Ops:
  1.3 0.7 %copy-start.9 = (f32[1,32]{1,0:T(1,128)S(1)}, f32[1,32]{1,0:T(1,128)}, u32[]{:S(2)}) copy-start(f32[1,32]{1,0:T(1,128)} %param.10) | copy-start | bytes 388
  2.1 0.7 %copy-start.8 = (f32[2,128]{1,0:T(2,128)S(1)}, f32[2,128]{1,0:T(2,128)}, u32[]{:S(2)}) copy-start(f32[2,128]{1,0:T(2,128)} %param.11) | copy-start | bytes 3076
  2.1 0.7 %copy-start.7 = (f32[2,128]{1,0:T(2,128)S(1)}, f32[2,128]{1,0:T(2,128)}, u32[]{:S(2)}) copy-start(f32[2,128]{1,0:T(2,128)} %param.9) | copy-start | bytes 3076
  2.8 7.7 %collective-permute-start = (f32[9,128]{1,0:T(8,128)S(1)}, f32[9,128]{1,0:T(8,128)S(1)}, u32[]{:S(2)}, u32[]{:S(2)}) collective-permute-start(f32[9,128]{1,0:T(8,128)S(1)} %concatenate.20), channel_id=1, source_target_pairs={{0,16},{1,17},{2,18},{3,19},{4,20},{5,21},{6,22},{7,23},{8,24},{9,... | collective-permute-start | bytes 13832 | tf_op jit(solution)/shard_map/ppermute | solution.py:279
  5.8 0.7 %copy-start.6 = (s32[256]{0:T(256)S(1)}, s32[256]{0:T(256)}, u32[]{:S(2)}) copy-start(s32[256]{0:T(256)} %param.16) | copy-start | bytes 3076
  5.9 0.7 %copy-start.5 = (s32[256]{0:T(256)S(1)}, s32[256]{0:T(256)}, u32[]{:S(2)}) copy-start(s32[256]{0:T(256)} %param.15) | copy-start | bytes 3076
  6.5 0.8 %copy-start = (f32[128,128]{1,0:T(8,128)S(1)}, f32[128,128]{1,0:T(8,128)}, u32[]{:S(2)}) copy-start(f32[128,128]{1,0:T(8,128)} %frozen_ref.3) | copy-start | bytes 196612
  7.4 0.9 %copy-start.2 = (s32[8000,6]{0,1:T(8,128)S(1)}, s32[8000,6]{0,1:T(8,128)}, u32[]{:S(2)}) copy-start(s32[8000,6]{0,1:T(8,128)} %param.14) | copy-start | bytes 576004
  8.3 0.8 %copy-start.4 = (s32[128,128]{1,0:T(8,128)S(1)}, s32[128,128]{1,0:T(8,128)}, u32[]{:S(2)}) copy-start(s32[128,128]{1,0:T(8,128)} %label_ref.1) | copy-start | bytes 196612
  10.6 4.7 %collective-permute-start.1 = (f32[26,128]{1,0:T(8,128)S(1)}, f32[26,128]{1,0:T(8,128)S(1)}, u32[]{:S(2)}, u32[]{:S(2)}) collective-permute-start(f32[26,128]{1,0:T(8,128)S(1)} %pad_maximum_fusion.6), channel_id=1, source_target_pairs={{0,8},{1,9},{2,10},{3,11},{4,12},{5,13},{6,14},{7,15},{8,0},{9,1},... | collective-permute-start | bytes 39944 | tf_op jit(solution)/shard_map/ppermute | solution.py:279
  15.4 3.8 %collective-permute-start.2 = (f32[36,128]{1,0:T(8,128)S(1)}, f32[36,128]{1,0:T(8,128)S(1)}, u32[]{:S(2)}, u32[]{:S(2)}) collective-permute-start(f32[36,128]{1,0:T(8,128)S(1)} %pad_maximum_fusion.4), channel_id=1, source_target_pairs={{0,4},{1,5},{2,6},{3,7},{4,0},{5,1},{6,2},{7,3},{8,12},{9,13},{10,... | collective-permute-start | bytes 55304 | tf_op jit(solution)/shard_map/ppermute | solution.py:279
  19.3 3.9 %collective-permute-start.3 = (f32[56,128]{1,0:T(8,128)S(1)}, f32[56,128]{1,0:T(8,128)S(1)}, u32[]{:S(2)}, u32[]{:S(2)}) collective-permute-start(f32[56,128]{1,0:T(8,128)S(1)} %pad_maximum_fusion.3), channel_id=1, source_target_pairs={{0,2},{1,3},{2,0},{3,1},{4,6},{5,7},{6,4},{7,5},{8,10},{9,11},{10,... | collective-permute-start | bytes 86024 | tf_op jit(solution)/shard_map/ppermute | solution.py:279
  23.3 1.3 %collective-permute-start.4 = (f32[112,128]{1,0:T(8,128)S(1)}, f32[112,128]{1,0:T(8,128)S(1)}, u32[]{:S(2)}, u32[]{:S(2)}) collective-permute-start(f32[112,128]{1,0:T(8,128)S(1)} %pad_maximum_fusion.1), channel_id=1, source_target_pairs={{0,1},{1,0},{2,3},{3,2},{4,5},{5,4},{6,7},{7,6},{8,9},{9,8},{10,11... | collective-permute-start | bytes 172040 | tf_op jit(solution)/shard_map/ppermute | solution.py:279
  24.7 0.9 %copy-start.3 = (f32[128,384]{1,0:T(8,128)S(1)}, f32[128,384]{1,0:T(8,128)}, u32[]{:S(2)}) copy-start(f32[128,384]{1,0:T(8,128)} %constant.161.clone.spread_ref) | copy-start | bytes 589828
  24.7 0.9 %copy-start.1 = (f32[128,128]{1,0:T(8,128)S(1)}, f32[128,128]{1,0:T(8,128)}, u32[]{:S(2)}) copy-start(f32[128,128]{1,0:T(8,128)} %frozen_ref.3) | copy-start | bytes 196612

commit v2 on v1

--- a/solution.py
+++ b/solution.py
@@ -15,6 +15,7 @@
 STEP = 0.004
 AXES = ("grp", "slab")
 VMEM = pl.BlockSpec(memory_space=pltpu.VMEM)
+HBM = pl.BlockSpec(memory_space=pltpu.HBM)
 PARAMS = pltpu.CompilerParams(vmem_limit_bytes=48 * 1024 * 1024)
 
 
@@ -27,6 +28,46 @@
         return value >> (by.bit_length() - 1), value & (by - 1)
     quotient = lax.div(value, jnp.full_like(value, by))
     return quotient, value - quotient * by
+
+
+def pack_kernel(
+    state_ref, heat_ref, kappa_ref, frozen_ref, label_ref, held_ref, edge_ref,
+    state, heat, kappa, frozen, label, sems,
+):
+    layers, elements = kappa.shape
+    flat = state.shape[1]
+    edge_x = frozen_ref.shape[0]
+    top, bottom = pl.ds(0, 8), pl.ds(edge_x - 8, 8)
+    copies = [
+        pltpu.make_async_copy(source, target, sems.at[i])
+        for i, (source, target) in enumerate(
+            [
+                (state_ref, state),
+                (heat_ref, heat),
+                (kappa_ref, kappa),
+                (frozen_ref.at[top, :], frozen.at[0]),
+                (frozen_ref.at[bottom, :], frozen.at[1]),
+                (label_ref.at[top, :], label.at[0]),
+                (label_ref.at[bottom, :], label.at[1]),
+            ]
+        )
+    ]
+    for copy in copies:
+        copy.start()
+    held_ref[4:5, :] = jnp.zeros((1, held_ref.shape[1]), jnp.float32)
+    for copy in copies:
+        copy.wait()
+    for layer in range(layers):
+        lanes = slice(layer * flat, (layer + 1) * flat)
+        for parity in range(2):
+            row = slice(2 * layer + parity, 2 * layer + parity + 1)
+            held_ref[parity : parity + 1, lanes] = state[row, :]
+            held_ref[2 + parity : 3 + parity, lanes] = heat[row, :]
+        held_ref[4:5, layer * flat : layer * flat + elements] = kappa[layer : layer + 1, :]
+    edge_ref[0:1, :] = frozen[1, 7:8, :]
+    edge_ref[1:2, :] = label[1, 7:8, :].astype(jnp.float32)
+    edge_ref[2:3, :] = frozen[0, 0:1, :]
+    edge_ref[3:4, :] = label[0, 0:1, :].astype(jnp.float32)
 
 
 def pick_codes(table_ref, labels):
@@ -47,14 +88,31 @@
 
 
 def cells_kernel(
-    depth, flat, table_ref, label_ref, frozen_ref, slot_ref, seed_ref,
-    packed_ref, gathered_ref, nucleation_ref, faces_ref, line_ref, code_ref,
+    depth, flat, table_hbm, label_hbm, frozen_hbm, slot_hbm, seed_hbm, spread_hbm,
+    packed_ref, gathered_ref, nucleation_ref, faces_ref, frozen_ref, spread_ref,
+    line_ref, code_ref, table_ref, label_ref, slot_ref, seed_ref, sems,
 ):
+    get_table, get_label, get_frozen, get_slot, get_seed, get_spread = [
+        pltpu.make_async_copy(source, target, sems.at[i])
+        for i, (source, target) in enumerate(
+            [
+                (table_hbm, table_ref),
+                (label_hbm, label_ref),
+                (frozen_hbm, frozen_ref),
+                (slot_hbm, slot_ref),
+                (seed_hbm, seed_ref),
+                (spread_hbm, spread_ref),
+            ]
+        )
+    ]
+    for copy in (get_table, get_label, get_frozen, get_slot, get_seed, get_spread):
+        copy.start()
     count = table_ref.shape[1]
     half = packed_ref.shape[0]
     edge_x, wide = frozen_ref.shape
     place = lax.broadcasted_iota(jnp.int32, table_ref.shape, 0)
     line_ref[...] = jnp.zeros(line_ref.shape, jnp.int32)
+    get_table.wait()
     word = jnp.sum((table_ref[...] - 1) << (2 * place), axis=0, keepdims=True)
     line_ref[0:1, 0:count] = word
     for r in range(half):
@@ -69,7 +127,9 @@
             code_ref[rows, lanes] = pick_codes(packed_ref, label_ref[rows, lanes])
         return carry
 
+    get_label.wait()
     lax.fori_loop(0, edge_x // 8, look_up, 0, unroll=4)
+    get_frozen.wait()
     frozen = frozen_ref[...] * 0.25
     code = code_ref[...]
     shares = [frozen * level(code, d) for d in range(6)]
@@ -90,6 +150,8 @@
     sides = jnp.transpose(jnp.where(lane < depth, shares[2], shares[3]))
     faces_ref[0:depth, :] = sides[0:depth]
     faces_ref[depth : 2 * depth, :] = sides[flat - depth : flat]
+    for copy in (get_slot, get_seed, get_spread):
+        copy.wait()
     sites = seed_ref.shape[0]
     codes = pick_codes(packed_ref, seed_ref[...])
     worth = sum(level(codes, d) for d in range(6))
@@ -275,39 +337,67 @@
     wide = up_to(flat_cells, LANES)
     all_layers = layers * devices
 
-    def swapped(array, bit):
-        return lax.ppermute(array, AXES, [(i, i ^ (1 << bit)) for i in range(devices)])
+    def exchanged(parts, flips):
+        sizes = np.cumsum([part.shape[0] for part in parts])
+        pairs = [(i, i ^ flips) for i in range(devices)]
+        got = lax.ppermute(jnp.concatenate(parts, 0), AXES, pairs)
+        return [got[end - part.shape[0] : end] for part, end in zip(parts, sizes)]
 
     def widened(array):
         return jnp.pad(array, ((0, 0), (0, wide - flat_cells)))
 
     unit = layers * flat
-    held = jnp.concatenate(
-        [
-            jnp.swapaxes(thermal_state_values.reshape(layers, 2, flat), 0, 1).reshape(2, unit),
-            jnp.swapaxes(nodal_heating_input.reshape(layers, 2, flat), 0, 1).reshape(2, unit),
-            jnp.pad(thermal_kappa_values, ((0, 0), (0, flat - elements))).reshape(1, unit),
+    count = growth_reach_table.shape[0]
+    frozen, label = widened(frozen_share_map), widened(crystal_label_map)
+    held, edge_rows = pl.pallas_call(
+        pack_kernel,
+        out_shape=(
+            jax.ShapeDtypeStruct((5, unit), jnp.float32),
+            jax.ShapeDtypeStruct((4, wide), jnp.float32),
+        ),
+        in_specs=[HBM] * 5,
+        out_specs=(VMEM, VMEM),
+        scratch_shapes=[
+            pltpu.VMEM(thermal_state_values.shape, jnp.float32),
+            pltpu.VMEM(nodal_heating_input.shape, jnp.float32),
+            pltpu.VMEM(thermal_kappa_values.shape, jnp.float32),
+            pltpu.VMEM((2, 8, wide), jnp.float32),
+            pltpu.VMEM((2, 8, wide), jnp.int32),
+            pltpu.SemaphoreType.DMA((7,)),
         ],
-        0,
-    )
-    frozen, label = widened(frozen_share_map), widened(crystal_label_map)
-    low_edge = jnp.stack([frozen[0], label[0].astype(jnp.float32)])
-    high_edge = jnp.stack([frozen[-1], label[-1].astype(jnp.float32)])
+        compiler_params=PARAMS,
+        name="pack",
+    )(thermal_state_values, nodal_heating_input, thermal_kappa_values, frozen, label)
+    high_edge, low_edge = edge_rows[:2], edge_rows[2:]
+
+    brick_layers = edge_x // CPC
+    need_y = (edge_y + CPC - 2) // CPC + 6
+    width = up_to(need_y * 2 * plane, LANES)
+    if 2 * width > flat:
+        width = flat
     seeds = up_to(seed_site_slots.shape[0], LANES)
     short = seeds - seed_site_slots.shape[0]
-    packed, gathered, nucleation, faces = pl.pallas_call(
+    table_lanes = up_to(count, 2 * LANES)
+    packed, gathered, nucleation, faces, frozen, spread = pl.pallas_call(
         functools.partial(cells_kernel, depth, flat_cells),
         out_shape=(
-            jax.ShapeDtypeStruct((up_to(growth_reach_table.shape[0], 2 * LANES) // (2 * LANES), LANES), jnp.int32),
+            jax.ShapeDtypeStruct((table_lanes // (2 * LANES), LANES), jnp.int32),
             jax.ShapeDtypeStruct((edge_x, wide), jnp.float32),
             jax.ShapeDtypeStruct((edge_x, wide), jnp.float32),
             jax.ShapeDtypeStruct((2 * depth, edge_x), jnp.float32),
+            jax.ShapeDtypeStruct((edge_x, wide), jnp.float32),
+            jax.ShapeDtypeStruct((width, 3 * width), jnp.float32),
         ),
-        in_specs=[VMEM] * 5,
-        out_specs=[VMEM] * 4,
+        in_specs=[HBM] * 6,
+        out_specs=[VMEM] * 6,
         scratch_shapes=[
-            pltpu.VMEM((8, up_to(growth_reach_table.shape[0], 2 * LANES)), jnp.int32),
+            pltpu.VMEM((8, table_lanes), jnp.int32),
             pltpu.VMEM((edge_x, wide), jnp.int32),
+            pltpu.VMEM((growth_reach_table.shape[1], count), jnp.int32),
+            pltpu.VMEM((edge_x, wide), jnp.int32),
+            pltpu.VMEM((seeds // LANES, LANES), jnp.int32),
+            pltpu.VMEM((seeds // LANES, LANES), jnp.int32),
+            pltpu.SemaphoreType.DMA((6,)),
         ],
         compiler_params=PARAMS,
         name="cells",
@@ -317,42 +407,58 @@
         frozen,
         jnp.pad(seed_site_slots, (0, short), constant_values=-1).reshape(-1, LANES),
         jnp.pad(seed_crystal_label, (0, short)).reshape(-1, LANES),
-    )
-
-    held = held[:, None]
+        jnp.asarray(spread_tables(width, plane)),
+    )
+
+    core, pair = me & 1, slab >> 1
     to_behind, to_ahead = faces[:depth], faces[depth:]
-    behind = ahead = edges = None
-    for bit in reversed(range(devices.bit_length() - 1)):
+    onward = jnp.where(core == 1, to_ahead, 0.0)
+    backward = jnp.where(core == 0, to_behind, 0.0)
+    held, edges = held[:, None], None
+    as_face = lambda part: part.reshape(-1)[: depth * edge_x].reshape(depth, edge_x)
+    for bit in reversed(range(1, devices.bit_length() - 1)):
         sent = [lines(held, unit)]
+        rides = 1 << bit < slabs
+        low = (1 << (bit - 1)) - 1
+        moves_on, moves_back = (pair & low) == low, (pair & low) == 0
         if groups == 2 and 1 << bit == slabs:
-            sent.append(lines(jnp.concatenate([high_edge, low_edge]), unit))
-        low = (1 << bit) - 1
-        goes_on = (slab & low) == low
-        if bit > 0 and 1 << bit < slabs:
-            face = jnp.where(goes_on, to_ahead, to_behind)
-            sent.append(lines(face, unit))
-        if bit == 0:
-            sent += [lines(to_ahead, unit), lines(to_behind, unit)]
-        got = swapped(jnp.concatenate(sent, 0), bit)
-        parts, at = [], 0
-        for part in sent:
-            parts.append(got[at : at + part.shape[0]])
-            at += part.shape[0]
-        theirs = parts[0].reshape(held.shape)
+            sent.append(lines(edge_rows, unit))
+        elif rides and low:
+            sent.append(lines(jnp.where(moves_on, onward, backward), unit))
+        elif rides:
+            sent += [lines(onward, unit), lines(backward, unit)]
+        theirs, *parts = exchanged(sent, (1 << bit) | 1)
+        theirs = theirs.reshape(held.shape)
         upper = (me >> bit) & 1 == 1
         held = jnp.stack(
             [jnp.where(upper, theirs, held), jnp.where(upper, held, theirs)], 2
         ).reshape(held.shape[0], 2 * held.shape[1], unit)
         if groups == 2 and 1 << bit == slabs:
-            edges = parts[1].reshape(-1)[: 4 * wide].reshape(4, wide)
-        if bit > 0 and 1 << bit < slabs:
-            face = parts[1].reshape(-1)[: depth * edge_x].reshape(depth, edge_x)
-            to_ahead = jnp.where(goes_on, face, to_ahead)
-            to_behind = jnp.where((slab & low) == 0, face, to_behind)
-        if bit == 0:
-            behind, ahead = (
-                part.reshape(-1)[: depth * edge_x].reshape(depth, edge_x) for part in parts[1:]
-            )
+            edges = parts[0].reshape(-1)[: 4 * wide].reshape(4, wide)
+        elif rides and low:
+            onward = jnp.where(moves_on, as_face(parts[0]), onward)
+            backward = jnp.where(moves_back, as_face(parts[0]), backward)
+        elif rides:
+            onward, backward = as_face(parts[0]), as_face(parts[1])
+    across = jnp.where(core == 0, to_ahead, to_behind)
+    passing = jnp.where(core == 1, onward, backward)
+    sent = [lines(held, unit), lines(across, unit), lines(passing, unit)]
+    if edges is not None:
+        sent.append(lines(edges, unit))
+    theirs, *parts = exchanged(sent, 1)
+    across = as_face(parts[0])
+    passing = as_face(parts[1]) + jnp.where(core == 0, onward, backward)
+    behind = jnp.where(core == 0, passing, across)
+    ahead = jnp.where(core == 0, across, passing)
+    if edges is not None:
+        edges = parts[2].reshape(-1)[: 4 * wide].reshape(4, wide)
+    odd_count = np.array([bin(i).count("1") & 1 for i in range(devices // 2)], np.int32)
+    mine = sum((me >> bit) & 1 for bit in range(devices.bit_length() - 1)) & 1
+    even_first = (jnp.asarray(odd_count) == mine)[None, :, None]
+    theirs = theirs.reshape(held.shape)
+    held = jnp.stack(
+        [jnp.where(even_first, held, theirs), jnp.where(even_first, theirs, held)], 2
+    )
     if edges is None:
         ring = [(i, (i + 1) % groups) for i in range(groups)]
         edges = jnp.concatenate(
@@ -390,15 +496,13 @@
             )
         return part, start_layer, start_y
 
-    brick_layers = edge_x // CPC
     first_cell = slab * edge_y
     state, start_layer, start_y = window(
         group * brick_layers - 2,
         brick_layers + 5,
         first_cell // CPC - 2,
-        (edge_y + CPC - 2) // CPC + 6,
-    )
-    width = state.shape[2]
+        need_y,
+    )
     whole = state.shape == held.shape
     weave = weave_table(width, plane, depth, edge_y, start_y, first_cell, rows_y)
 
@@ -430,7 +534,7 @@
         compiler_params=PARAMS,
         name="finish",
     )(
-        state, jnp.asarray(spread_tables(width, plane)), weave, packed, edges,
+        state, spread, weave, packed, edges,
         behind, ahead, gathered, nucleation, frozen,
     )
     if whole:

time: 27.4 us -> 26.6 us (0.971)
  waiting for transfers between devices: 7.63 us -> 5.41 us
  Pallas kernels: 2.69 us -> 3.79 us
  local copies, waits for them, and re-layouts: 5.74 us -> 6.5 us
  other arithmetic: 1.09 us -> 0.45 us
    ppermute x5, waiting for transfers between devices: 7.63 us -> 5.41 us  [exchanged(): got = lax.ppermute(jnp.concatenate(parts, 0), AXES, pairs)]
    unnamed x20 -> x24, local copies, waits for them, and re-layouts: 4.83 us -> 6.35 us
    pallas_call x1, Pallas kernels: 1.29 us -> 2.29 us  [body(): pl.pallas_call(functools.partial(cells_kernel, depth, flat_cells), out_sh...]
    convert_element_type x1 -> x0, other arithmetic: 0.72 us -> none  [body(): low_edge = jnp.stack([frozen[0], label[0].astype(jnp.float32)])]
    slice x6 -> x5, local copies, waits for them, and re-layouts: 0.73 us -> 0.01 us  [exchanged(): return [got[end - part.shape[0]:end] for part, end in zip(parts, sizes)]]
  transfers between devices with their start and end apart: 5 -> 5, of which waited for: 4 -> 4; matrix products, arithmetic and copies ran while one was open for 1% -> 1% of each run, Pallas kernels for 5% -> 9%
where the time goes in v2:
time: 26.6 us; the launch traced here: 26.3 us
  starting transfers between devices  9.21 us (35%)
  local copies, waits for them, and re-layouts  6.5 us (24%)
  waiting for transfers between devices  5.41 us (20%)
  Pallas kernels  3.79 us (14%)
  between operations  0.95 us (4%)
  other arithmetic  0.45 us (2%)
    ppermute x5, starting transfers between devices, exchanged(): got = lax.ppermute(jnp.concatenate(parts, 0), AXES, pairs)  9.21 us
    unnamed x24, local copies, waits for them, and re-layouts  6.35 us
    ppermute x5, waiting for transfers between devices, exchanged(): got = lax.ppermute(jnp.concatenate(parts, 0), AXES, pairs)  5.41 us
    pallas_call x1, Pallas kernels, body(): pl.pallas_call(functools.partial(cells_kernel, depth, flat_cells), out_sh...  2.29 us
    pallas_call x1, Pallas kernels, body(): pl.pallas_call(functools.partial(finish_kernel, plane, depth, flat_cells,...  1.41 us
  transfers between devices with their start and end apart: 5, of which 4 were waited for; matrix products, arithmetic and copies ran while one was open for 1% of the time, Pallas kernels for 9%

profile of v2, /device:TPU:0, one launch (start us, length us, event | category | flops | bytes accessed | tf_op | source)
XLA Modules:
  0.0 26.3 jit_solution(7741679127925841057)
XLA Ops:
  0.6 0.0 copy-start
  0.6 0.8 %copy-done = s32[128,128]{1,0:T(8,128)S(1)} copy-done((s32[128,128]{1,0:T(8,128)S(1)}, s32[128,128]{1,0:T(8,128)}, u32[]{:S(2)}) %copy-start) | copy-done | bytes 65560
  1.5 0.0 copy-start.2
  1.5 0.8 %copy-done.2 = f32[128,128]{1,0:T(8,128)S(1)} copy-done((f32[128,128]{1,0:T(8,128)S(1)}, f32[128,128]{1,0:T(8,128)}, u32[]{:S(2)}) %copy-start.2) | copy-done | bytes 65560
  2.3 0.0 copy-start.6
  2.3 0.7 %copy-done.6 = f32[2,128]{1,0:T(2,128)S(1)} copy-done((f32[2,128]{1,0:T(2,128)S(1)}, f32[2,128]{1,0:T(2,128)}, u32[]{:S(2)}) %copy-start.6) | copy-done | bytes 1048
  3.0 0.0 copy-start.7
  3.0 0.7 %copy-done.7 = f32[2,128]{1,0:T(2,128)S(1)} copy-done((f32[2,128]{1,0:T(2,128)S(1)}, f32[2,128]{1,0:T(2,128)}, u32[]{:S(2)}) %copy-start.7) | copy-done | bytes 1048
  3.7 0.0 copy-start.10
  3.7 0.7 %copy-done.10 = f32[1,32]{1,0:T(1,128)S(1)} copy-done((f32[1,32]{1,0:T(1,128)S(1)}, f32[1,32]{1,0:T(1,128)}, u32[]{:S(2)}) %copy-start.10) | copy-done | bytes 152
  4.3 0.0 copy-start.1
  4.3 0.0 copy-start.3
  4.3 0.1 pack.1
  4.5 2.4 %collective-permute-start = (f32[9,128]{1,0:T(8,128)S(1)}, f32[9,128]{1,0:T(8,128)S(1)}, u32[]{:S(2)}, u32[]{:S(2)}) collective-permute-start(f32[9,128]{1,0:T(8,128)S(1)} %pad_maximum_fusion.8), channel_id=1, source_target_pairs={{0,17},{1,16},{2,19},{3,18},{4,21},{5,20},{6,23},{7,22},{8,25},{9,... | collective-permute-start | bytes 13832 | tf_op jit(solution)/shard_map/ppermute | solution.py:343
  7.0 0.0 copy-start.9
  7.0 0.0 copy-start.8
  7.0 0.0 copy-done.1
  7.0 0.0 copy-done.3
  7.0 0.6 %copy-done.9 = s32[256]{0:T(256)S(1)} copy-done((s32[256]{0:T(256)S(1)}, s32[256]{0:T(256)}, u32[]{:S(2)}) %copy-start.9) | copy-done | bytes 1048
  7.6 0.0 copy-done.8
  7.7 0.0 copy-start.4
  7.7 0.9 %copy-done.4 = s32[8000,6]{0,1:T(8,128)S(1)} copy-done((s32[8000,6]{0,1:T(8,128)S(1)}, s32[8000,6]{0,1:T(8,128)}, u32[]{:S(2)}) %copy-start.4) | copy-done | bytes 192024
  8.6 0.0 copy-start.5
  8.6 0.9 %copy-done.5 = f32[128,384]{1,0:T(8,128)S(1)} copy-done((f32[128,384]{1,0:T(8,128)S(1)}, f32[128,384]{1,0:T(8,128)}, u32[]{:S(2)}) %copy-start.5) | copy-done | bytes 196632
  9.5 2.3 %cells.1 = (s32[32,128]{1,0:T(8,128)S(1)}, f32[128,128]{1,0:T(8,128)S(1)}, f32[128,128]{1,0:T(8,128)S(1)}, f32[32,128]{1,0:T(8,128)S(1)}, f32[128,128]{1,0:T(8,128)S(1)}, /*index=5*/f32[128,384]{1,0:T(8,128)S(1)}) custom-call(s32[6,8000]{1,0:T(8,128)S(1)} %bitcast.26, s32[128,128]{1,0:T(8,128)S(1)} %copy-done.1, f32[128,128]{1,0:T(8,128)S(1)} %copy-done.3, ...), custom_call_target="tpu_custom_call" | custom-call | tf_op jit(solution)/shard_map/cells/pallas_call | solution.py:381
  11.9 0.0 collective-permute-done
  11.9 2.9 %collective-permute-start.1 = (f32[26,128]{1,0:T(8,128)S(1)}, f32[26,128]{1,0:T(8,128)S(1)}, u32[]{:S(2)}, u32[]{:S(2)}) collective-permute-start(f32[26,128]{1,0:T(8,128)S(1)} %pad_maximum_fusion.6), channel_id=1, source_target_pairs={{0,9},{1,8},{2,11},{3,10},{4,13},{5,12},{6,15},{7,14},{8,1},{9,0},... | collective-permute-start | bytes 39944 | tf_op jit(solution)/shard_map/ppermute | solution.py:343
  14.9 1.4 %collective-permute-done.1 = f32[26,128]{1,0:T(8,128)S(1)} collective-permute-done((f32[26,128]{1,0:T(8,128)S(1)}, f32[26,128]{1,0:T(8,128)S(1)}, u32[]{:S(2)}, u32[]{:S(2)}) %collective-permute-start.1) | collective-permute-done | bytes 13344 | tf_op jit(solution)/shard_map/ppermute | solution.py:343
  16.4 1.7 %collective-permute-start.2 = (f32[36,128]{1,0:T(8,128)S(1)}, f32[36,128]{1,0:T(8,128)S(1)}, u32[]{:S(2)}, u32[]{:S(2)}) collective-permute-start(f32[36,128]{1,0:T(8,128)S(1)} %pad_maximum_fusion.4), channel_id=1, source_target_pairs={{0,5},{1,4},{2,7},{3,6},{4,1},{5,0},{6,3},{7,2},{8,13},{9,12},{10,... | collective-permute-start | bytes 55304 | tf_op jit(solution)/shard_map/ppermute | solution.py:343
  18.1 1.6 %collective-permute-done.2 = f32[36,128]{1,0:T(8,128)S(1)} collective-permute-done((f32[36,128]{1,0:T(8,128)S(1)}, f32[36,128]{1,0:T(8,128)S(1)}, u32[]{:S(2)}, u32[]{:S(2)}) %collective-permute-start.2) | collective-permute-done | bytes 18464 | tf_op jit(solution)/shard_map/ppermute | solution.py:343
  19.8 1.6 %collective-permute-start.3 = (f32[72,128]{1,0:T(8,128)S(1)}, f32[72,128]{1,0:T(8,128)S(1)}, u32[]{:S(2)}, u32[]{:S(2)}) collective-permute-start(f32[72,128]{1,0:T(8,128)S(1)} %pad_maximum_fusion.3), channel_id=1, source_target_pairs={{0,3},{1,2},{2,1},{3,0},{4,7},{5,6},{6,5},{7,4},{8,11},{9,10},{10,... | collective-permute-start | bytes 110600 | tf_op jit(solution)/shard_map/ppermute | solution.py:343
  21.4 0.2 multiply_select_fusion.weave_ref
  21.6 1.6 %collective-permute-done.3 = f32[72,128]{1,0:T(8,128)S(1)} collective-permute-done((f32[72,128]{1,0:T(8,128)S(1)}, f32[72,128]{1,0:T(8,128)S(1)}, u32[]{:S(2)}, u32[]{:S(2)}) %collective-permute-start.3) | collective-permute-done | bytes 36896 | tf_op jit(solution)/shard_map/ppermute | solution.py:343
  23.3 0.0 copy-start.11
  23.3 0.5 %collective-permute-start.4 = (f32[116,128]{1,0:T(8,128)S(1)}, f32[116,128]{1,0:T(8,128)S(1)}, u32[]{:S(2)}, u32[]{:S(2)}) collective-permute-start(f32[116,128]{1,0:T(8,128)S(1)} %pad_maximum_fusion.1), channel_id=1, source_target_pairs={{0,1},{1,0},{2,3},{3,2},{4,5},{5,4},{6,7},{7,6},{8,9},{9,8},{10,11... | collective-permute-start | bytes 178184 | tf_op jit(solution)/shard_map/ppermute | solution.py:343
  23.8 0.1 copy-done.11
  24.0 0.8 %collective-permute-done.4 = f32[116,128]{1,0:T(8,128)S(1)} collective-permute-done((f32[116,128]{1,0:T(8,128)S(1)}, f32[116,128]{1,0:T(8,128)S(1)}, u32[]{:S(2)}, u32[]{:S(2)}) %collective-permute-start.4) | collective-permute-done | bytes 59424 | tf_op jit(solution)/shard_map/ppermute | solution.py:343
  24.7 0.1 broadcast_select_fusion.1
  24.9 1.4 %finish.1 = (f32[2,128]{1,0:T(2,128)}, f32[128,128]{1,0:T(8,128)}) custom-call(f32[5,32,128]{2,1,0:T(8,128)S(1)} %bitcast.25, f32[128,384]{1,0:T(8,128)S(1)} %get-tuple-element.13.spread_ref, f32[128,128]{1,0:T(8,128)S(1)} %multiply_select_fusion.weave_ref, s32[32,128]{1,0:T(8,128)S(1)} %get-tuple-element.14.packed_ref, f32[4,128]{1,0:T(4,128)S(1)} %slice.70.edge_ref, ...), custom_call_target="tpu_custom_call" | custom-call | tf_op jit(solution)/shard_map/finish/pallas_call | solution.py:520
  (40 shorter events, 0.4 us)
Async XLA Ops:
  0.6 0.8 %copy-start = (s32[128,128]{1,0:T(8,128)S(1)}, s32[128,128]{1,0:T(8,128)}, u32[]{:S(2)}) copy-start(s32[128,128]{1,0:T(8,128)} %label_hbm.1) | copy-start | bytes 196612
  1.5 0.8 %copy-start.2 = (f32[128,128]{1,0:T(8,128)S(1)}, f32[128,128]{1,0:T(8,128)}, u32[]{:S(2)}) copy-start(f32[128,128]{1,0:T(8,128)} %frozen_hbm.1) | copy-start | bytes 196612
  2.3 0.7 %copy-start.6 = (f32[2,128]{1,0:T(2,128)S(1)}, f32[2,128]{1,0:T(2,128)}, u32[]{:S(2)}) copy-start(f32[2,128]{1,0:T(2,128)} %state_ref.1) | copy-start | bytes 3076
  3.0 0.7 %copy-start.7 = (f32[2,128]{1,0:T(2,128)S(1)}, f32[2,128]{1,0:T(2,128)}, u32[]{:S(2)}) copy-start(f32[2,128]{1,0:T(2,128)} %heat_ref.1) | copy-start | bytes 3076
  3.7 0.7 %copy-start.10 = (f32[1,32]{1,0:T(1,128)S(1)}, f32[1,32]{1,0:T(1,128)}, u32[]{:S(2)}) copy-start(f32[1,32]{1,0:T(1,128)} %kappa_ref.1) | copy-start | bytes 388
  4.3 2.7 %copy-start.1 = (s32[128,128]{1,0:T(8,128)S(1)}, s32[128,128]{1,0:T(8,128)}, u32[]{:S(2)}) copy-start(s32[128,128]{1,0:T(8,128)} %label_hbm.1) | copy-start | bytes 196612
  4.3 2.7 %copy-start.3 = (f32[128,128]{1,0:T(8,128)S(1)}, f32[128,128]{1,0:T(8,128)}, u32[]{:S(2)}) copy-start(f32[128,128]{1,0:T(8,128)} %frozen_hbm.1) | copy-start | bytes 196612
  4.5 7.4 %collective-permute-start = (f32[9,128]{1,0:T(8,128)S(1)}, f32[9,128]{1,0:T(8,128)S(1)}, u32[]{:S(2)}, u32[]{:S(2)}) collective-permute-start(f32[9,128]{1,0:T(8,128)S(1)} %pad_maximum_fusion.8), channel_id=1, source_target_pairs={{0,17},{1,16},{2,19},{3,18},{4,21},{5,20},{6,23},{7,22},{8,25},{9,... | collective-permute-start | bytes 13832 | tf_op jit(solution)/shard_map/ppermute | solution.py:343
  7.0 0.7 %copy-start.9 = (s32[256]{0:T(256)S(1)}, s32[256]{0:T(256)}, u32[]{:S(2)}) copy-start(s32[256]{0:T(256)} %param.17) | copy-start | bytes 3076
  7.0 0.7 %copy-start.8 = (s32[256]{0:T(256)S(1)}, s32[256]{0:T(256)}, u32[]{:S(2)}) copy-start(s32[256]{0:T(256)} %param.16) | copy-start | bytes 3076
  7.7 0.9 %copy-start.4 = (s32[8000,6]{0,1:T(8,128)S(1)}, s32[8000,6]{0,1:T(8,128)}, u32[]{:S(2)}) copy-start(s32[8000,6]{0,1:T(8,128)} %param.15) | copy-start | bytes 576004
  8.6 0.9 %copy-start.5 = (f32[128,384]{1,0:T(8,128)S(1)}, f32[128,384]{1,0:T(8,128)}, u32[]{:S(2)}) copy-start(f32[128,384]{1,0:T(8,128)} %constant.161.clone.spread_hbm) | copy-start | bytes 589828
  11.9 4.4 %collective-permute-start.1 = (f32[26,128]{1,0:T(8,128)S(1)}, f32[26,128]{1,0:T(8,128)S(1)}, u32[]{:S(2)}, u32[]{:S(2)}) collective-permute-start(f32[26,128]{1,0:T(8,128)S(1)} %pad_maximum_fusion.6), channel_id=1, source_target_pairs={{0,9},{1,8},{2,11},{3,10},{4,13},{5,12},{6,15},{7,14},{8,1},{9,0},... | collective-permute-start | bytes 39944 | tf_op jit(solution)/shard_map/ppermute | solution.py:343
  16.4 3.3 %collective-permute-start.2 = (f32[36,128]{1,0:T(8,128)S(1)}, f32[36,128]{1,0:T(8,128)S(1)}, u32[]{:S(2)}, u32[]{:S(2)}) collective-permute-start(f32[36,128]{1,0:T(8,128)S(1)} %pad_maximum_fusion.4), channel_id=1, source_target_pairs={{0,5},{1,4},{2,7},{3,6},{4,1},{5,0},{6,3},{7,2},{8,13},{9,12},{10,... | collective-permute-start | bytes 55304 | tf_op jit(solution)/shard_map/ppermute | solution.py:343
  19.8 3.4 %collective-permute-start.3 = (f32[72,128]{1,0:T(8,128)S(1)}, f32[72,128]{1,0:T(8,128)S(1)}, u32[]{:S(2)}, u32[]{:S(2)}) collective-permute-start(f32[72,128]{1,0:T(8,128)S(1)} %pad_maximum_fusion.3), channel_id=1, source_target_pairs={{0,3},{1,2},{2,1},{3,0},{4,7},{5,6},{6,5},{7,4},{8,11},{9,10},{10,... | collective-permute-start | bytes 110600 | tf_op jit(solution)/shard_map/ppermute | solution.py:343
  23.3 0.7 %copy-start.11 = (s32[16]{0:T(128)S(1)}, s32[16]{0:T(128)}, u32[]{:S(2)}) copy-start(s32[16]{0:T(128)} %constant.162.clone) | copy-start | bytes 196
  23.3 1.4 %collective-permute-start.4 = (f32[116,128]{1,0:T(8,128)S(1)}, f32[116,128]{1,0:T(8,128)S(1)}, u32[]{:S(2)}, u32[]{:S(2)}) collective-permute-start(f32[116,128]{1,0:T(8,128)S(1)} %pad_maximum_fusion.1), channel_id=1, source_target_pairs={{0,1},{1,0},{2,3},{3,2},{4,5},{5,4},{6,7},{7,6},{8,9},{9,8},{10,11... | collective-permute-start | bytes 178184 | tf_op jit(solution)/shard_map/ppermute | solution.py:343

commit v3 on v2

--- a/solution.py
+++ b/solution.py
@@ -17,6 +17,10 @@
 VMEM = pl.BlockSpec(memory_space=pltpu.VMEM)
 HBM = pl.BlockSpec(memory_space=pltpu.HBM)
 PARAMS = pltpu.CompilerParams(vmem_limit_bytes=48 * 1024 * 1024)
+
+
+def in_hbm(array):
+    return pltpu.with_memory_space_constraint(array, pltpu.HBM)
 
 
 def up_to(value, unit):
@@ -367,7 +371,7 @@
         ],
         compiler_params=PARAMS,
         name="pack",
-    )(thermal_state_values, nodal_heating_input, thermal_kappa_values, frozen, label)
+    )(*map(in_hbm, (thermal_state_values, nodal_heating_input, thermal_kappa_values, frozen, label)))
     high_edge, low_edge = edge_rows[:2], edge_rows[2:]
 
     brick_layers = edge_x // CPC
@@ -402,12 +406,12 @@
         compiler_params=PARAMS,
         name="cells",
     )(
-        growth_reach_table.T,
-        label,
-        frozen,
-        jnp.pad(seed_site_slots, (0, short), constant_values=-1).reshape(-1, LANES),
-        jnp.pad(seed_crystal_label, (0, short)).reshape(-1, LANES),
-        jnp.asarray(spread_tables(width, plane)),
+        in_hbm(growth_reach_table.T),
+        in_hbm(label),
+        in_hbm(frozen),
+        in_hbm(jnp.pad(seed_site_slots, (0, short), constant_values=-1).reshape(-1, LANES)),
+        in_hbm(jnp.pad(seed_crystal_label, (0, short)).reshape(-1, LANES)),
+        in_hbm(jnp.asarray(spread_tables(width, plane))),
     )
 
     core, pair = me & 1, slab >> 1
@@ -452,9 +456,9 @@
     ahead = jnp.where(core == 0, across, passing)
     if edges is not None:
         edges = parts[2].reshape(-1)[: 4 * wide].reshape(4, wide)
-    odd_count = np.array([bin(i).count("1") & 1 for i in range(devices // 2)], np.int32)
-    mine = sum((me >> bit) & 1 for bit in range(devices.bit_length() - 1)) & 1
-    even_first = (jnp.asarray(odd_count) == mine)[None, :, None]
+    odd_count = lambda number: lax.population_count(number) & 1
+    pairs_held = jnp.arange(devices // 2, dtype=jnp.int32)
+    even_first = (odd_count(pairs_held) == odd_count(me))[None, :, None]
     theirs = theirs.reshape(held.shape)
     held = jnp.stack(
         [jnp.where(even_first, held, theirs), jnp.where(even_first, theirs, held)], 2

time: 26.6 us -> 21.2 us (0.80)
  local copies, waits for them, and re-layouts: 6.5 us -> 0.15 us
  Pallas kernels: 3.79 us -> 4.77 us
    unnamed x24 -> x0, local copies, waits for them, and re-layouts: 6.35 us -> none
    pallas_call x1, Pallas kernels: 0.1 us -> 0.85 us  [body(): pl.pallas_call(pack_kernel, out_shape=(jax.ShapeDtypeStruct((5, unit), jn...]
  transfers between devices with their start and end apart: 5 -> 5, of which waited for: 4 -> 4; matrix products, arithmetic and copies ran while one was open for 1% -> 1% of each run, Pallas kernels for 9% -> 12%
where the time goes in v3:
time: 21.2 us; the launch traced here: 21 us
  starting transfers between devices  9.2 us (43%)
  waiting for transfers between devices  5.53 us (26%)
  Pallas kernels  4.77 us (22%)
  between operations  0.88 us (4%)
  other arithmetic  0.45 us (2%)
    ppermute x5, starting transfers between devices, exchanged(): got = lax.ppermute(jnp.concatenate(parts, 0), AXES, pairs)  9.2 us
    ppermute x5, waiting for transfers between devices, exchanged(): got = lax.ppermute(jnp.concatenate(parts, 0), AXES, pairs)  5.53 us
    pallas_call x1, Pallas kernels, body(): pl.pallas_call(functools.partial(cells_kernel, depth, flat_cells), out_sh...  2.51 us
    pallas_call x1, Pallas kernels, body(): pl.pallas_call(functools.partial(finish_kernel, plane, depth, flat_cells,...  1.41 us
    pallas_call x1, Pallas kernels, body(): pl.pallas_call(pack_kernel, out_shape=(jax.ShapeDtypeStruct((5, unit), jn...  0.85 us
  transfers between devices with their start and end apart: 5, of which 4 were waited for; matrix products, arithmetic and copies ran while one was open for 1% of the time, Pallas kernels for 12%

profile of v3, /device:TPU:0, one launch (start us, length us, event | category | flops | bytes accessed | tf_op | source)
XLA Modules:
  0.0 21.0 jit_solution(10448823415636847368)
XLA Ops:
  0.6 0.8 %pack.1 = (f32[5,128]{1,0:T(8,128)S(1)}, f32[4,128]{1,0:T(4,128)S(1)}) custom-call(f32[2,128]{1,0:T(2,128)} %state_ref.1, f32[2,128]{1,0:T(2,128)} %heat_ref.1, f32[1,32]{1,0:T(1,128)} %kappa_ref.1, f32[128,128]{1,0:T(8,128)} %frozen_hbm.1, s32[128,128]{1,0:T(8,128)} %label_hbm.1), custom_call_target="tpu_custom_call" | custom-call | tf_op jit(solution)/shard_map/pack/pallas_call | solution.py:356
  1.5 2.4 %collective-permute-start = (f32[9,128]{1,0:T(8,128)S(1)}, f32[9,128]{1,0:T(8,128)S(1)}, u32[]{:S(2)}, u32[]{:S(2)}) collective-permute-start(f32[9,128]{1,0:T(8,128)S(1)} %pad_maximum_fusion.8), channel_id=1, source_target_pairs={{0,17},{1,16},{2,19},{3,18},{4,21},{5,20},{6,23},{7,22},{8,25},{9,... | collective-permute-start | bytes 13832 | tf_op jit(solution)/shard_map/ppermute | solution.py:347
  4.0 2.5 %cells.1 = (s32[32,128]{1,0:T(8,128)S(1)}, f32[128,128]{1,0:T(8,128)S(1)}, f32[128,128]{1,0:T(8,128)S(1)}, f32[32,128]{1,0:T(8,128)S(1)}, f32[128,128]{1,0:T(8,128)S(1)}, /*index=5*/f32[128,384]{1,0:T(8,128)S(1)}) custom-call(s32[6,8000]{1,0:T(8,128)} %bitcast.28, s32[128,128]{1,0:T(8,128)} %label_hbm.1, f32[128,128]{1,0:T(8,128)} %frozen_hbm.1, ...), custom_call_target="tpu_custom_call" | custom-call | tf_op jit(solution)/shard_map/cells/pallas_call | solution.py:385
  6.6 0.0 collective-permute-done
  6.6 2.9 %collective-permute-start.1 = (f32[26,128]{1,0:T(8,128)S(1)}, f32[26,128]{1,0:T(8,128)S(1)}, u32[]{:S(2)}, u32[]{:S(2)}) collective-permute-start(f32[26,128]{1,0:T(8,128)S(1)} %pad_maximum_fusion.6), channel_id=1, source_target_pairs={{0,9},{1,8},{2,11},{3,10},{4,13},{5,12},{6,15},{7,14},{8,1},{9,0},... | collective-permute-start | bytes 39944 | tf_op jit(solution)/shard_map/ppermute | solution.py:347
  9.6 1.4 %collective-permute-done.1 = f32[26,128]{1,0:T(8,128)S(1)} collective-permute-done((f32[26,128]{1,0:T(8,128)S(1)}, f32[26,128]{1,0:T(8,128)S(1)}, u32[]{:S(2)}, u32[]{:S(2)}) %collective-permute-start.1) | collective-permute-done | bytes 13344 | tf_op jit(solution)/shard_map/ppermute | solution.py:347
  11.1 1.7 %collective-permute-start.2 = (f32[36,128]{1,0:T(8,128)S(1)}, f32[36,128]{1,0:T(8,128)S(1)}, u32[]{:S(2)}, u32[]{:S(2)}) collective-permute-start(f32[36,128]{1,0:T(8,128)S(1)} %pad_maximum_fusion.4), channel_id=1, source_target_pairs={{0,5},{1,4},{2,7},{3,6},{4,1},{5,0},{6,3},{7,2},{8,13},{9,12},{10,... | collective-permute-start | bytes 55304 | tf_op jit(solution)/shard_map/ppermute | solution.py:347
  12.8 1.6 %collective-permute-done.2 = f32[36,128]{1,0:T(8,128)S(1)} collective-permute-done((f32[36,128]{1,0:T(8,128)S(1)}, f32[36,128]{1,0:T(8,128)S(1)}, u32[]{:S(2)}, u32[]{:S(2)}) %collective-permute-start.2) | collective-permute-done | bytes 18464 | tf_op jit(solution)/shard_map/ppermute | solution.py:347
  14.5 1.6 %collective-permute-start.3 = (f32[72,128]{1,0:T(8,128)S(1)}, f32[72,128]{1,0:T(8,128)S(1)}, u32[]{:S(2)}, u32[]{:S(2)}) collective-permute-start(f32[72,128]{1,0:T(8,128)S(1)} %pad_maximum_fusion.3), channel_id=1, source_target_pairs={{0,3},{1,2},{2,1},{3,0},{4,7},{5,6},{6,5},{7,4},{8,11},{9,10},{10,... | collective-permute-start | bytes 110600 | tf_op jit(solution)/shard_map/ppermute | solution.py:347
  16.1 0.2 multiply_select_fusion.weave_ref
  16.3 1.6 %collective-permute-done.3 = f32[72,128]{1,0:T(8,128)S(1)} collective-permute-done((f32[72,128]{1,0:T(8,128)S(1)}, f32[72,128]{1,0:T(8,128)S(1)}, u32[]{:S(2)}, u32[]{:S(2)}) %collective-permute-start.3) | collective-permute-done | bytes 36896 | tf_op jit(solution)/shard_map/ppermute | solution.py:347
  18.0 0.5 %collective-permute-start.4 = (f32[116,128]{1,0:T(8,128)S(1)}, f32[116,128]{1,0:T(8,128)S(1)}, u32[]{:S(2)}, u32[]{:S(2)}) collective-permute-start(f32[116,128]{1,0:T(8,128)S(1)} %pad_maximum_fusion.1), channel_id=1, source_target_pairs={{0,1},{1,0},{2,3},{3,2},{4,5},{5,4},{6,7},{7,6},{8,9},{9,8},{10,11... | collective-permute-start | bytes 178184 | tf_op jit(solution)/shard_map/ppermute | solution.py:347
  18.5 0.9 %collective-permute-done.4 = f32[116,128]{1,0:T(8,128)S(1)} collective-permute-done((f32[116,128]{1,0:T(8,128)S(1)}, f32[116,128]{1,0:T(8,128)S(1)}, u32[]{:S(2)}, u32[]{:S(2)}) %collective-permute-start.4) | collective-permute-done | bytes 59424 | tf_op jit(solution)/shard_map/ppermute | solution.py:347
  19.4 0.1 broadcast_select_fusion.1
  19.6 1.4 %finish.1 = (f32[2,128]{1,0:T(2,128)}, f32[128,128]{1,0:T(8,128)}) custom-call(f32[5,32,128]{2,1,0:T(8,128)S(1)} %bitcast.25, f32[128,384]{1,0:T(8,128)S(1)} %get-tuple-element.13.spread_ref, f32[128,128]{1,0:T(8,128)S(1)} %multiply_select_fusion.weave_ref, s32[32,128]{1,0:T(8,128)S(1)} %get-tuple-element.14.packed_ref, f32[4,128]{1,0:T(4,128)S(1)} %slice.70.edge_ref, ...), custom_call_target="tpu_custom_call" | custom-call | tf_op jit(solution)/shard_map/finish/pallas_call | solution.py:524
  (40 shorter events, 0.4 us)
Async XLA Ops:
  1.5 5.1 %collective-permute-start = (f32[9,128]{1,0:T(8,128)S(1)}, f32[9,128]{1,0:T(8,128)S(1)}, u32[]{:S(2)}, u32[]{:S(2)}) collective-permute-start(f32[9,128]{1,0:T(8,128)S(1)} %pad_maximum_fusion.8), channel_id=1, source_target_pairs={{0,17},{1,16},{2,19},{3,18},{4,21},{5,20},{6,23},{7,22},{8,25},{9,... | collective-permute-start | bytes 13832 | tf_op jit(solution)/shard_map/ppermute | solution.py:347
  6.6 4.4 %collective-permute-start.1 = (f32[26,128]{1,0:T(8,128)S(1)}, f32[26,128]{1,0:T(8,128)S(1)}, u32[]{:S(2)}, u32[]{:S(2)}) collective-permute-start(f32[26,128]{1,0:T(8,128)S(1)} %pad_maximum_fusion.6), channel_id=1, source_target_pairs={{0,9},{1,8},{2,11},{3,10},{4,13},{5,12},{6,15},{7,14},{8,1},{9,0},... | collective-permute-start | bytes 39944 | tf_op jit(solution)/shard_map/ppermute | solution.py:347
  11.1 3.3 %collective-permute-start.2 = (f32[36,128]{1,0:T(8,128)S(1)}, f32[36,128]{1,0:T(8,128)S(1)}, u32[]{:S(2)}, u32[]{:S(2)}) collective-permute-start(f32[36,128]{1,0:T(8,128)S(1)} %pad_maximum_fusion.4), channel_id=1, source_target_pairs={{0,5},{1,4},{2,7},{3,6},{4,1},{5,0},{6,3},{7,2},{8,13},{9,12},{10,... | collective-permute-start | bytes 55304 | tf_op jit(solution)/shard_map/ppermute | solution.py:347
  14.5 3.4 %collective-permute-start.3 = (f32[72,128]{1,0:T(8,128)S(1)}, f32[72,128]{1,0:T(8,128)S(1)}, u32[]{:S(2)}, u32[]{:S(2)}) collective-permute-start(f32[72,128]{1,0:T(8,128)S(1)} %pad_maximum_fusion.3), channel_id=1, source_target_pairs={{0,3},{1,2},{2,1},{3,0},{4,7},{5,6},{6,5},{7,4},{8,11},{9,10},{10,... | collective-permute-start | bytes 110600 | tf_op jit(solution)/shard_map/ppermute | solution.py:347
  18.0 1.4 %collective-permute-start.4 = (f32[116,128]{1,0:T(8,128)S(1)}, f32[116,128]{1,0:T(8,128)S(1)}, u32[]{:S(2)}, u32[]{:S(2)}) collective-permute-start(f32[116,128]{1,0:T(8,128)S(1)} %pad_maximum_fusion.1), channel_id=1, source_target_pairs={{0,1},{1,0},{2,3},{3,2},{4,5},{5,4},{6,7},{7,6},{8,9},{9,8},{10,11... | collective-permute-start | bytes 178184 | tf_op jit(solution)/shard_map/ppermute | solution.py:347

commit v4 on v3

--- a/solution.py
+++ b/solution.py
@@ -42,22 +42,18 @@
     flat = state.shape[1]
     edge_x = frozen_ref.shape[0]
     top, bottom = pl.ds(0, 8), pl.ds(edge_x - 8, 8)
-    copies = [
-        pltpu.make_async_copy(source, target, sems.at[i])
-        for i, (source, target) in enumerate(
-            [
-                (state_ref, state),
-                (heat_ref, heat),
-                (kappa_ref, kappa),
-                (frozen_ref.at[top, :], frozen.at[0]),
-                (frozen_ref.at[bottom, :], frozen.at[1]),
-                (label_ref.at[top, :], label.at[0]),
-                (label_ref.at[bottom, :], label.at[1]),
-            ]
-        )
-    ]
-    for copy in copies:
-        copy.start()
+    copies = started(
+        [
+            (state_ref, state),
+            (heat_ref, heat),
+            (kappa_ref, kappa),
+            (frozen_ref.at[top, :], frozen.at[0]),
+            (frozen_ref.at[bottom, :], frozen.at[1]),
+            (label_ref.at[top, :], label.at[0]),
+            (label_ref.at[bottom, :], label.at[1]),
+        ],
+        sems,
+    )
     held_ref[4:5, :] = jnp.zeros((1, held_ref.shape[1]), jnp.float32)
     for copy in copies:
         copy.wait()
@@ -91,31 +87,31 @@
     return (((code >> (2 * direction)) & 3) + 1).astype(jnp.float32)
 
 
-def cells_kernel(
-    depth, flat, table_hbm, label_hbm, frozen_hbm, slot_hbm, seed_hbm, spread_hbm,
-    packed_ref, gathered_ref, nucleation_ref, faces_ref, frozen_ref, spread_ref,
-    line_ref, code_ref, table_ref, label_ref, slot_ref, seed_ref, sems,
+def started(pairs, sems):
+    copies = [pltpu.make_async_copy(*pair, sems.at[i]) for i, pair in enumerate(pairs)]
+    for copy in copies:
+        copy.start()
+    return copies
+
+
+def faces_kernel(
+    depth, flat, table_hbm, label_hbm, frozen_hbm,
+    packed_ref, label_ref, frozen_ref, faces_ref, line_ref, table_ref, sems,
 ):
-    get_table, get_label, get_frozen, get_slot, get_seed, get_spread = [
-        pltpu.make_async_copy(source, target, sems.at[i])
-        for i, (source, target) in enumerate(
-            [
-                (table_hbm, table_ref),
-                (label_hbm, label_ref),
-                (frozen_hbm, frozen_ref),
-                (slot_hbm, slot_ref),
-                (seed_hbm, seed_ref),
-                (spread_hbm, spread_ref),
-            ]
-        )
-    ]
-    for copy in (get_table, get_label, get_frozen, get_slot, get_seed, get_spread):
-        copy.start()
+    get_table, get_label, get_frozen = started(
+        [(table_hbm, table_ref), (label_hbm, label_ref), (frozen_hbm, frozen_ref)], sems
+    )
     count = table_ref.shape[1]
     half = packed_ref.shape[0]
-    edge_x, wide = frozen_ref.shape
+    edge_x = frozen_ref.shape[0]
     place = lax.broadcasted_iota(jnp.int32, table_ref.shape, 0)
     line_ref[...] = jnp.zeros(line_ref.shape, jnp.int32)
+    get_label.wait()
+    get_frozen.wait()
+    label = jnp.transpose(label_ref[...])
+    label = jnp.concatenate([label[0:depth], label[flat - depth : flat]], 0)
+    frozen = jnp.transpose(frozen_ref[...])
+    frozen = 0.25 * jnp.concatenate([frozen[0:depth], frozen[flat - depth : flat]], 0)
     get_table.wait()
     word = jnp.sum((table_ref[...] - 1) << (2 * place), axis=0, keepdims=True)
     line_ref[0:1, 0:count] = word
@@ -123,6 +119,20 @@
         low = line_ref[0:1, r * LANES : (r + 1) * LANES]
         high = line_ref[0:1, (r + half) * LANES : (r + half + 1) * LANES]
         packed_ref[r : r + 1, :] = low | (high << 12)
+    for t in range(edge_x // LANES):
+        lanes = slice(t * LANES, (t + 1) * LANES)
+        for part in range(2 * depth // 8):
+            rows = slice(part * 8, part * 8 + 8)
+            code = pick_codes(packed_ref, label[rows, lanes])
+            faces_ref[rows, lanes] = frozen[rows, lanes] * level(code, 2 if part * 8 < depth else 3)
+
+
+def cells_kernel(
+    depth, flat, packed_ref, label_ref, frozen_ref, slot_hbm, seed_hbm, spread_hbm,
+    gathered_ref, nucleation_ref, spread_ref, code_ref, slot_ref, seed_ref, sems,
+):
+    copies = started([(slot_hbm, slot_ref), (seed_hbm, seed_ref), (spread_hbm, spread_ref)], sems)
+    edge_x, wide = frozen_ref.shape
 
     def look_up(chunk, carry):
         rows = pl.ds(pl.multiple_of(chunk * 8, 8), 8)
@@ -131,15 +141,13 @@
             code_ref[rows, lanes] = pick_codes(packed_ref, label_ref[rows, lanes])
         return carry
 
-    get_label.wait()
-    lax.fori_loop(0, edge_x // 8, look_up, 0, unroll=4)
-    get_frozen.wait()
+    lax.fori_loop(0, edge_x // 8, look_up, 0, unroll=16)
     frozen = frozen_ref[...] * 0.25
     code = code_ref[...]
     shares = [frozen * level(code, d) for d in range(6)]
     line_x = lax.broadcasted_iota(jnp.int32, (edge_x, wide), 0)
     lane = lax.broadcasted_iota(jnp.int32, (edge_x, wide), 1)
-    deep = lane % depth if depth & (depth - 1) else lane & (depth - 1)
+    deep = split_index(lane, depth)[1]
     total = jnp.where(line_x == edge_x - 1, 0.0, pltpu.roll(shares[0], edge_x - 1, 0))
     total += jnp.where(line_x == 0, 0.0, pltpu.roll(shares[1], 1, 0))
     total += jnp.where(lane >= flat - depth, 0.0, pltpu.roll(shares[2], wide - depth, 1))
@@ -151,10 +159,7 @@
         deep == 0, pltpu.roll(shares[5], wide - (depth - 1), 1), pltpu.roll(shares[5], 1, 1)
     )
     gathered_ref[...] = total
-    sides = jnp.transpose(jnp.where(lane < depth, shares[2], shares[3]))
-    faces_ref[0:depth, :] = sides[0:depth]
-    faces_ref[depth : 2 * depth, :] = sides[flat - depth : flat]
-    for copy in (get_slot, get_seed, get_spread):
+    for copy in copies:
         copy.wait()
     sites = seed_ref.shape[0]
     codes = pick_codes(packed_ref, seed_ref[...])
@@ -185,8 +190,16 @@
     first_y[np.arange(rows_y // 2), 2 * np.arange(rows_y // 2)] = 1
     first_z[np.arange(deep), 2 * np.arange(deep)] = 1
     full = [np.kron(along, down), np.kron(first_y, down), np.kron(along, first_z)]
-    out = np.zeros((width, 3 * width), np.float32)
-    out[: width // 4] = np.concatenate(full, 1)
+    out = np.zeros((width, 3 * width), jnp.bfloat16)
+    out[: 3 * (width // 4)] = np.concatenate([np.concatenate(full, 1)] * 3, 0)
+    return out
+
+
+def pieces(values):
+    out = []
+    for _ in range(3):
+        out.append(values.astype(jnp.bfloat16).astype(jnp.float32))
+        values = values - out[-1]
     return out
 
 
@@ -197,7 +210,9 @@
     turn = lambda v, by: pltpu.roll(v, by % width, 1)
     lane = lax.broadcasted_iota(jnp.int32, (rows, width), 1)
     row_y, deep = split_index(lane, plane)
-    lines = jnp.dot(kappa, spread, precision=HIGHEST, preferred_element_type=jnp.float32)
+    first, second, third = pieces(kappa)
+    joined = first + turn(second, width // 4) + turn(third, 2 * (width // 4))
+    lines = jnp.dot(joined.astype(jnp.bfloat16), spread, preferred_element_type=jnp.float32)
     lines = lines * (1.0 / 108.0)
     along_x, along_y, along_z = (lines[:, i * width : (i + 1) * width] for i in range(3))
     y_even, y_odd = along_y + down(along_y), 4.0 * along_y
@@ -253,37 +268,70 @@
 
 
 def finish_kernel(
-    plane, depth, flat, layers, first_row, cell_row, wraps,
-    state_ref, spread_ref, weave_ref, packed_ref, edge_ref, behind_ref, ahead_ref,
-    gathered_ref, nucleation_ref, frozen_ref, *refs,
+    plane, depth, flat, layers, group_lanes, sizes, first_row, cell_row, first_lane, wraps,
+    mine_ref, theirs_ref, across_ref, passing_ref, edge_ref, kept_ref, spread_ref, weave_ref,
+    packed_ref, gathered_ref, nucleation_ref, frozen_ref, *refs,
 ):
-    solid_ref, even_ref, odd_ref, side_ref, extra_ref = refs[-5:]
+    solid_ref, state_ref, even_ref, odd_ref, side_ref, extra_ref = refs[-6:]
     edge_x, wide = frozen_ref.shape
-    rows = state_ref.shape[1]
-    even, odd = advance(plane, *(state_ref[i] for i in range(5)), spread_ref[...])
-    if first_row is not None:
-        new_ref = refs[0]
-        even_ref[:, 0 : even.shape[1]] = even
-        odd_ref[:, 0 : even.shape[1]] = odd
-        start = first_row()
-        for layer in range(layers):
-            new_ref[2 * layer : 2 * layer + 1, :] = even_ref[pl.ds(start + layer, 1), 0 : even.shape[1]]
-            new_ref[2 * layer + 1 : 2 * layer + 2, :] = odd_ref[pl.ds(start + layer, 1), 0 : even.shape[1]]
+    _, rows, width = state_ref.shape
+    heat_rows, across_row, passing_row, edge_row, devices = sizes
+    core = lax.axis_index("slab") & 1
+    if heat_rows:
+        me = lax.axis_index("grp") * lax.axis_size("slab") + lax.axis_index("slab")
+        for p, off in enumerate(arrival_order(devices)):
+            source, block = (mine_ref, p) if p < devices // 2 else (theirs_ref, p - devices // 2)
+            for c in range(5):
+                for layer in range(layers):
+                    state_ref[c, pl.ds((me ^ off) * layers + layer, 1), :] = source[
+                        block * 5 + c : block * 5 + c + 1, layer * width : (layer + 1) * width
+                    ]
+        state = [state_ref[i] for i in range(5)]
+    else:
+        state = [mine_ref[i] for i in range(5)]
     side_ref[...] = jnp.zeros(side_ref.shape, jnp.float32)
-    side_ref[0:depth, :] = behind_ref[...]
-    side_ref[flat - depth : flat, :] = ahead_ref[...]
+    there = jnp.where(core == 0, 0, flat - depth)
+    side_ref[pl.ds(pl.multiple_of(there, 8), depth), :] = (
+        kept_ref[...] + passing_ref[passing_row : passing_row + depth, :]
+    )
+    side_ref[pl.ds(pl.multiple_of(flat - depth - there, 8), depth), :] = across_ref[
+        across_row : across_row + depth, :
+    ]
     extra_ref[...] = gathered_ref[...] + jnp.transpose(side_ref[...])
     for t in range(wide // LANES):
         lanes = slice(t * LANES, (t + 1) * LANES)
-        rough = jnp.concatenate([edge_ref[:, lanes], jnp.zeros((4, LANES), jnp.float32)], 0)
+        rough = jnp.concatenate(
+            [edge_ref[edge_row : edge_row + 4, lanes], jnp.zeros((4, LANES), jnp.float32)], 0
+        )
         codes = pick_codes(packed_ref, rough.astype(jnp.int32))
         behind = rough[0:1] * level(codes[1:2], 1) * 0.25
         ahead = rough[2:3] * level(codes[3:4], 0) * 0.25
         extra_ref[0:1, lanes] += behind
         extra_ref[edge_x - 1 : edge_x, lanes] += ahead
-    weave = weave_ref[...]
-    even_ref[:, 0:wide] = jnp.dot(even, weave, precision=HIGHEST, preferred_element_type=jnp.float32)
-    odd_ref[:, 0:wide] = jnp.dot(odd, weave, precision=HIGHEST, preferred_element_type=jnp.float32)
+    even, odd = advance(plane, *state, spread_ref[...])
+    if first_row is not None:
+        new_ref = refs[0]
+        even_ref[:, 0:width] = even
+        odd_ref[:, 0:width] = odd
+        start = first_row()
+        for layer in range(layers):
+            new_ref[2 * layer : 2 * layer + 1, :] = even_ref[pl.ds(start + layer, 1), 0:width]
+            new_ref[2 * layer + 1 : 2 * layer + 2, :] = odd_ref[pl.ds(start + layer, 1), 0:width]
+    both = jnp.concatenate([even, odd], 0)
+    both = pltpu.roll(both, first_lane(), 1)
+    span = weave_ref.shape[0]
+    if span > width:
+        both = jnp.concatenate([both, jnp.zeros((2 * rows, span - width), jnp.float32)], 1)
+    lane = lax.broadcasted_iota(jnp.int32, both.shape, 1)
+    first, second, third = pieces(jnp.where(lane < group_lanes, both, 0.0))
+    joined = first
+    for i, piece in enumerate((second, third, first, second)):
+        joined = joined + pltpu.roll(piece, (i + 1) * group_lanes, 1)
+    woven = jnp.dot(
+        joined.astype(jnp.bfloat16), weave_ref[...], preferred_element_type=jnp.float32
+    )
+    even_ref[:, 0:wide] = woven[:rows]
+    odd_ref[:, 0:wide] = woven[rows:]
     first, middle, last = basis(lax.broadcasted_iota(jnp.int32, (CPC, wide), 0))
     base = cell_row()
     for a in range(edge_x // CPC):
@@ -302,14 +350,24 @@
         solid_ref[cells, :] = frozen + (1.0 - frozen) * (1.0 - jnp.exp(-rate))
 
 
-def weave_table(width, plane, depth, edge_y, start_y, first_cell, rows_total):
-    wide = up_to(edge_y * depth, LANES)
-    node, cell = jnp.arange(width)[:, None], jnp.arange(wide)[None, :]
-    cell_y, cell_z = first_cell + cell // depth, cell % depth
-    step_y = jnp.remainder(start_y + node // plane - 2 * (cell_y // CPC), rows_total)
+def weave_table(group_lanes, plane, depth, edge_y, first_step, wide):
+    node, cell = jnp.arange(group_lanes)[:, None], jnp.arange(wide)[None, :]
+    cell_y, cell_z = first_step + cell // depth, cell % depth
+    step_y = node // plane - 2 * (cell_y // CPC)
     step_z = jnp.remainder(node % plane - 2 * (cell_z // CPC), plane)
     take = lambda step, at: sum(jnp.where(step == i, v, 0.0) for i, v in enumerate(basis(at % CPC)))
-    return jnp.where(cell < edge_y * depth, take(step_y, cell_y) * take(step_z, cell_z), 0.0)
+    full = jnp.where(cell < edge_y * depth, take(step_y, cell_y) * take(step_z, cell_z), 0.0)
+    high = jnp.floor(full * 128.0) * (1.0 / 128.0)
+    both = jnp.stack([high, high, high, full - high, full - high]).reshape(5 * group_lanes, wide)
+    short = up_to(5 * group_lanes, LANES) - 5 * group_lanes
+    return jnp.pad(both, ((0, short), (0, 0))).astype(jnp.bfloat16)
+
+
+def arrival_order(devices):
+    offs = [0]
+    for bit in reversed(range(1, devices.bit_length() - 1)):
+        offs += [off ^ (1 << bit) ^ 1 for off in offs]
+    return offs + [off ^ 1 for off in offs]
 
 
 def lines(values, width):
@@ -342,10 +400,11 @@
     all_layers = layers * devices
 
     def exchanged(parts, flips):
-        sizes = np.cumsum([part.shape[0] for part in parts])
-        pairs = [(i, i ^ flips) for i in range(devices)]
-        got = lax.ppermute(jnp.concatenate(parts, 0), AXES, pairs)
-        return [got[end - part.shape[0] : end] for part, end in zip(parts, sizes)]
+        at = [0]
+        for part in parts[:-1]:
+            at.append(at[-1] + part.shape[0])
+        sent = jnp.concatenate(parts, 0) if len(parts) > 1 else parts[0]
+        return sent, lax.ppermute(sent, AXES, [(i, i ^ flips) for i in range(devices)]), at
 
     def widened(array):
         return jnp.pad(array, ((0, 0), (0, wide - flat_cells)))
@@ -379,36 +438,48 @@
     width = up_to(need_y * 2 * plane, LANES)
     if 2 * width > flat:
         width = flat
+    table_lanes = up_to(count, 2 * LANES)
+    packed, label, frozen, faces = pl.pallas_call(
+        functools.partial(faces_kernel, depth, flat_cells),
+        out_shape=(
+            jax.ShapeDtypeStruct((table_lanes // (2 * LANES), LANES), jnp.int32),
+            jax.ShapeDtypeStruct((edge_x, wide), jnp.int32),
+            jax.ShapeDtypeStruct((edge_x, wide), jnp.float32),
+            jax.ShapeDtypeStruct((2 * depth, edge_x), jnp.float32),
+        ),
+        in_specs=[HBM] * 3,
+        out_specs=[VMEM] * 4,
+        scratch_shapes=[
+            pltpu.VMEM((8, table_lanes), jnp.int32),
+            pltpu.VMEM((growth_reach_table.shape[1], count), jnp.int32),
+            pltpu.SemaphoreType.DMA((3,)),
+        ],
+        compiler_params=PARAMS,
+        name="faces",
+    )(in_hbm(growth_reach_table.T), in_hbm(label), in_hbm(frozen))
     seeds = up_to(seed_site_slots.shape[0], LANES)
     short = seeds - seed_site_slots.shape[0]
-    table_lanes = up_to(count, 2 * LANES)
-    packed, gathered, nucleation, faces, frozen, spread = pl.pallas_call(
+    gathered, nucleation, spread = pl.pallas_call(
         functools.partial(cells_kernel, depth, flat_cells),
         out_shape=(
-            jax.ShapeDtypeStruct((table_lanes // (2 * LANES), LANES), jnp.int32),
             jax.ShapeDtypeStruct((edge_x, wide), jnp.float32),
             jax.ShapeDtypeStruct((edge_x, wide), jnp.float32),
-            jax.ShapeDtypeStruct((2 * depth, edge_x), jnp.float32),
-            jax.ShapeDtypeStruct((edge_x, wide), jnp.float32),
-            jax.ShapeDtypeStruct((width, 3 * width), jnp.float32),
+            jax.ShapeDtypeStruct((width, 3 * width), jnp.bfloat16),
         ),
-        in_specs=[HBM] * 6,
-        out_specs=[VMEM] * 6,
+        in_specs=[VMEM] * 3 + [HBM] * 3,
+        out_specs=[VMEM] * 3,
         scratch_shapes=[
-            pltpu.VMEM((8, table_lanes), jnp.int32),
-            pltpu.VMEM((edge_x, wide), jnp.int32),
-            pltpu.VMEM((growth_reach_table.shape[1], count), jnp.int32),
             pltpu.VMEM((edge_x, wide), jnp.int32),
             pltpu.VMEM((seeds // LANES, LANES), jnp.int32),
             pltpu.VMEM((seeds // LANES, LANES), jnp.int32),
-            pltpu.SemaphoreType.DMA((6,)),
+            pltpu.SemaphoreType.DMA((3,)),
         ],
         compiler_params=PARAMS,
         name="cells",
     )(
-        in_hbm(growth_reach_table.T),
-        in_hbm(label),
-        in_hbm(frozen),
+        packed,
+        label,
+        frozen,
         in_hbm(jnp.pad(seed_site_slots, (0, short), constant_values=-1).reshape(-1, LANES)),
         in_hbm(jnp.pad(seed_crystal_label, (0, short)).reshape(-1, LANES)),
         in_hbm(jnp.asarray(spread_tables(width, plane))),
@@ -418,25 +489,23 @@
     to_behind, to_ahead = faces[:depth], faces[depth:]
     onward = jnp.where(core == 1, to_ahead, 0.0)
     backward = jnp.where(core == 0, to_behind, 0.0)
-    held, edges = held[:, None], None
+    heat, edges = [held], None
     as_face = lambda part: part.reshape(-1)[: depth * edge_x].reshape(depth, edge_x)
     for bit in reversed(range(1, devices.bit_length() - 1)):
-        sent = [lines(held, unit)]
         rides = 1 << bit < slabs
         low = (1 << (bit - 1)) - 1
         moves_on, moves_back = (pair & low) == low, (pair & low) == 0
+        extra = []
         if groups == 2 and 1 << bit == slabs:
-            sent.append(lines(edge_rows, unit))
+            extra = [lines(edge_rows, unit)]
         elif rides and low:
-            sent.append(lines(jnp.where(moves_on, onward, backward), unit))
+            extra = [lines(jnp.where(moves_on, onward, backward), unit)]
         elif rides:
-            sent += [lines(onward, unit), lines(backward, unit)]
-        theirs, *parts = exchanged(sent, (1 << bit) | 1)
-        theirs = theirs.reshape(held.shape)
-        upper = (me >> bit) & 1 == 1
-        held = jnp.stack(
-            [jnp.where(upper, theirs, held), jnp.where(upper, held, theirs)], 2
-        ).reshape(held.shape[0], 2 * held.shape[1], unit)
+            extra = [lines(onward, unit), lines(backward, unit)]
+        sent, got, at = exchanged(heat + extra, (1 << bit) | 1)
+        heat_rows = sum(part.shape[0] for part in heat)
+        heat = [sent[:heat_rows], got[:heat_rows]]
+        parts = [got[row : row + part.shape[0]] for row, part in zip(at[len(at) - len(extra) :], extra)]
         if groups == 2 and 1 << bit == slabs:
             edges = parts[0].reshape(-1)[: 4 * wide].reshape(4, wide)
         elif rides and low:
@@ -444,25 +513,19 @@
             backward = jnp.where(moves_back, as_face(parts[0]), backward)
         elif rides:
             onward, backward = as_face(parts[0]), as_face(parts[1])
-    across = jnp.where(core == 0, to_ahead, to_behind)
-    passing = jnp.where(core == 1, onward, backward)
-    sent = [lines(held, unit), lines(across, unit), lines(passing, unit)]
+    extra = [
+        lines(jnp.where(core == 0, to_ahead, to_behind), unit),
+        lines(jnp.where(core == 1, onward, backward), unit),
+    ]
     if edges is not None:
-        sent.append(lines(edges, unit))
-    theirs, *parts = exchanged(sent, 1)
-    across = as_face(parts[0])
-    passing = as_face(parts[1]) + jnp.where(core == 0, onward, backward)
-    behind = jnp.where(core == 0, passing, across)
-    ahead = jnp.where(core == 0, across, passing)
+        extra.append(lines(edges, unit))
+    kept = jnp.where(core == 0, onward, backward)
+    sent, got, at = exchanged(heat + extra, 1)
+    heat_rows = sum(part.shape[0] for part in heat)
+    at = at[len(heat) :]
+    across, passing = (as_face(got[row : row + part.shape[0]]) for row, part in zip(at, extra[:2]))
     if edges is not None:
-        edges = parts[2].reshape(-1)[: 4 * wide].reshape(4, wide)
-    odd_count = lambda number: lax.population_count(number) & 1
-    pairs_held = jnp.arange(devices // 2, dtype=jnp.int32)
-    even_first = (odd_count(pairs_held) == odd_count(me))[None, :, None]
-    theirs = theirs.reshape(held.shape)
-    held = jnp.stack(
-        [jnp.where(even_first, held, theirs), jnp.where(even_first, theirs, held)], 2
-    )
+        edges = got[at[2] : at[2] + extra[2].shape[0]].reshape(-1)[: 4 * wide].reshape(4, wide)
     if edges is None:
         ring = [(i, (i + 1) % groups) for i in range(groups)]
         edges = jnp.concatenate(
@@ -471,44 +534,60 @@
                 lax.ppermute(low_edge, "grp", [(j, i) for i, j in ring]),
             ]
         )
-    held = held.reshape(5, all_layers, flat)
-
-    def window(first_layer, need_layers, first_element, need_elements):
-        rows, width = up_to(need_layers, 8), up_to(need_elements * 2 * plane, LANES)
-        part, start_layer, start_y = held, 0, 0
-        if 2 * rows <= all_layers:
-            start_layer = first_layer
-            part = lax.dynamic_slice_in_dim(
-                jnp.concatenate([part, part[:, : rows]], 1),
-                jnp.remainder(start_layer, all_layers), rows, 1,
-            )
-        if 2 * width <= flat:
-            start_y = 2 * first_element
-            shifted = lambda v, by, size: lax.dynamic_slice_in_dim(
-                jnp.concatenate([v, v[..., :size]], -1), by, size, v.ndim - 1
-            )
-            start = jnp.remainder(first_element, rows_y // 2)
-            part = jnp.concatenate(
-                [
-                    shifted(part[:4], start * 2 * plane, width),
-                    jnp.pad(
-                        shifted(part[4:, :, :elements], start * HEX_COUNT_LATER, width // 4),
-                        ((0, 0), (0, 0), (0, width - width // 4)),
-                    ),
-                ],
-                0,
-            )
-        return part, start_layer, start_y
-
+    brick_layers = edge_x // CPC
     first_cell = slab * edge_y
-    state, start_layer, start_y = window(
-        group * brick_layers - 2,
-        brick_layers + 5,
-        first_cell // CPC - 2,
-        need_y,
-    )
-    whole = state.shape == held.shape
-    weave = weave_table(width, plane, depth, edge_y, start_y, first_cell, rows_y)
+    first_element = first_cell // CPC
+    need_layers = brick_layers + 5
+    whole = width == flat and 2 * up_to(need_layers, 8) > all_layers
+    direct = whole and edge_x == unit and wide == unit and groups == 2
+    if direct:
+        inputs = (sent, got, got, got, got)
+        sizes = (heat_rows, *at, devices)
+        start_layer = start_y = 0
+    else:
+        order = np.argsort(arrival_order(devices))
+        blocks = jnp.concatenate([sent[:heat_rows], got[:heat_rows]], 0).reshape(devices, 5, layers, flat)
+        blocks = jnp.take(blocks, jnp.asarray(order)[jnp.arange(devices) ^ me], axis=0)
+        held = jnp.moveaxis(blocks, 1, 0).reshape(5, all_layers, flat)
+
+        def window(first_layer, need_layers, first_element, need_elements):
+            rows, lanes = up_to(need_layers, 8), up_to(need_elements * 2 * plane, LANES)
+            part, start_layer, start_y = held, 0, 0
+            if 2 * rows <= all_layers:
+                start_layer = first_layer
+                part = lax.dynamic_slice_in_dim(
+                    jnp.concatenate([part, part[:, :rows]], 1),
+                    jnp.remainder(start_layer, all_layers), rows, 1,
+                )
+            if 2 * lanes <= flat:
+                start_y = 2 * first_element
+                shifted = lambda v, by, size: lax.dynamic_slice_in_dim(
+                    jnp.concatenate([v, v[..., :size]], -1), by, size, v.ndim - 1
+                )
+                start = jnp.remainder(first_element, rows_y // 2)
+                part = jnp.concatenate(
+                    [
+                        shifted(part[:4], start * 2 * plane, lanes),
+                        jnp.pad(
+                            shifted(part[4:, :, :elements], start * HEX_COUNT_LATER, lanes // 4),
+                            ((0, 0), (0, 0), (0, lanes - lanes // 4)),
+                        ),
+                    ],
+                    0,
+                )
+            return part, start_layer, start_y
+
+        state, start_layer, start_y = window(
+            group * brick_layers - 2, need_layers, first_element - 2, need_y
+        )
+        inputs = (state, state, across, passing, edges)
+        sizes = (0, 0, 0, 0, devices)
+    if edge_y % CPC == 0 or CPC % edge_y == 0:
+        covered = max(edge_y // CPC, 1)
+    else:
+        covered = (edge_y + CPC - 2) // CPC + 1
+    group_lanes = up_to((2 * covered + 1) * plane, 16)
+    weave = weave_table(group_lanes, plane, depth, edge_y, first_cell % CPC, wide)
 
     def place(start, layer):
         if not isinstance(start, int):
@@ -518,29 +597,34 @@
     own_layer = lambda g, s: (g * slabs + s) * layers
     cell_row = place(start_layer, lambda g, s: g * brick_layers)
     own_row = place(start_layer, own_layer)
+    if isinstance(start_y, int):
+        first_lane = lambda: lax.rem(
+            width - (lax.axis_index("slab") * edge_y // CPC) * 2 * plane, width
+        )
+    else:
+        first_lane = lambda: width - 4 * plane
+    rows = all_layers if direct else state.shape[1]
     new_shape = jax.ShapeDtypeStruct((2 * layers, flat), jnp.float32)
     solid_shape = jax.ShapeDtypeStruct((edge_x, wide), jnp.float32)
     span = max(width, wide)
     results = pl.pallas_call(
         functools.partial(
-            finish_kernel, plane, depth, flat_cells, layers,
-            own_row if whole else None, cell_row, isinstance(start_layer, int),
+            finish_kernel, plane, depth, flat_cells, layers, group_lanes, sizes,
+            own_row if whole else None, cell_row, first_lane, isinstance(start_layer, int),
         ),
         out_shape=(new_shape, solid_shape) if whole else (solid_shape,),
-        in_specs=[VMEM] * 10,
+        in_specs=[VMEM] * 12,
         out_specs=(VMEM,) * (1 + whole),
         scratch_shapes=[
-            pltpu.VMEM((state.shape[1], span), jnp.float32),
-            pltpu.VMEM((state.shape[1], span), jnp.float32),
+            pltpu.VMEM((5, rows, width), jnp.float32),
+            pltpu.VMEM((rows, span), jnp.float32),
+            pltpu.VMEM((rows, span), jnp.float32),
             pltpu.VMEM((wide, edge_x), jnp.float32),
             pltpu.VMEM((edge_x, wide), jnp.float32),
         ],
         compiler_params=PARAMS,
         name="finish",
-    )(
-        state, spread, weave, packed, edges,
-        behind, ahead, gathered, nucleation, frozen,
-    )
+    )(*inputs, kept, spread, weave, packed, gathered, nucleation, frozen)
     if whole:
         new_field, new_solid = results
     else:

time: 21.2 us -> 21.6 us (1.019)
  waiting for transfers between devices: 5.53 us -> 4.58 us
  Pallas kernels: 4.77 us -> 5.58 us
  local copies, waits for them, and re-layouts: 0.15 us -> 0.71 us
    pallas_call x0 -> x1, Pallas kernels: none -> 1.46 us  [body(): pl.pallas_call(functools.partial(faces_kernel, depth, flat_cells), out_sh...]
    ppermute x5, waiting for transfers between devices: 5.53 us -> 4.58 us  [exchanged(): lax.ppermute(sent, AXES, [(i, i ^ flips) for i in range(devices)])]
    pallas_call x1, Pallas kernels: 2.51 us -> 1.71 us  [body(): pl.pallas_call(functools.partial(cells_kernel, depth, flat_cells), out_sh...]
    concatenate x0 -> x2, local copies, waits for them, and re-layouts: none -> 0.69 us  [exchanged(): sent = jnp.concatenate(parts, 0) if len(parts) > 1 else parts[0]]
    unnamed x0 -> x4, other arithmetic: none -> 0.37 us
    select_n x10 -> x4, other arithmetic: 0.3 us -> 0.02 us  [the longest x2 0.01 us: body(): extra = [lines(jnp.where(moves_on, onward, backward), unit)]]
  transfers between devices with their start and end apart: 5 -> 5, of which waited for: 4 -> 3; matrix products, arithmetic and copies ran while one was open for 1% -> 3% of each run, Pallas kernels for 12% -> 15%
where the time goes in v4:
time: 21.6 us; the launch traced here: 21.4 us
  starting transfers between devices  9.17 us (42%)
  Pallas kernels  5.58 us (26%)
  waiting for transfers between devices  4.58 us (21%)
  between operations  0.77 us (4%)
  local copies, waits for them, and re-layouts  0.71 us (3%)
  other arithmetic  0.59 us (3%)
    ppermute x5, starting transfers between devices, exchanged(): lax.ppermute(sent, AXES, [(i, i ^ flips) for i in range(devices)])  9.17 us
    ppermute x5, waiting for transfers between devices, exchanged(): lax.ppermute(sent, AXES, [(i, i ^ flips) for i in range(devices)])  4.58 us
    pallas_call x1, Pallas kernels, body(): pl.pallas_call(functools.partial(cells_kernel, depth, flat_cells), out_sh...  1.71 us
    pallas_call x1, Pallas kernels, body(): pl.pallas_call(functools.partial(finish_kernel, plane, depth, flat_cells,...  1.56 us
    pallas_call x1, Pallas kernels, body(): pl.pallas_call(functools.partial(faces_kernel, depth, flat_cells), out_sh...  1.46 us
    pallas_call x1, Pallas kernels, body(): pl.pallas_call(pack_kernel, out_shape=(jax.ShapeDtypeStruct((5, unit), jn...  0.85 us
    concatenate x2, local copies, waits for them, and re-layouts, exchanged(): sent = jnp.concatenate(parts, 0) if len(parts) > 1 else parts[0]  0.69 us
  transfers between devices with their start and end apart: 5, of which 3 were waited for; matrix products, arithmetic and copies ran while one was open for 3% of the time, Pallas kernels for 15%

profile of v4, /device:TPU:0, one launch (start us, length us, event | category | flops | bytes accessed | tf_op | source)
XLA Modules:
  0.0 21.4 jit_solution(18033641472699134638)
XLA Ops:
  0.6 0.8 %pack.1 = (f32[5,128]{1,0:T(8,128)S(1)}, f32[4,128]{1,0:T(4,128)S(1)}) custom-call(f32[2,128]{1,0:T(2,128)} %state_ref.1, f32[2,128]{1,0:T(2,128)} %heat_ref.1, f32[1,32]{1,0:T(1,128)} %kappa_ref.1, f32[128,128]{1,0:T(8,128)} %frozen_hbm.1, s32[128,128]{1,0:T(8,128)} %label_hbm.1), custom_call_target="tpu_custom_call" | custom-call | tf_op jit(solution)/shard_map/pack/pallas_call | solution.py:415
  1.5 2.4 %collective-permute-start = (f32[9,128]{1,0:T(8,128)S(1)}, f32[9,128]{1,0:T(8,128)S(1)}, u32[]{:S(2)}, u32[]{:S(2)}) collective-permute-start(f32[9,128]{1,0:T(8,128)S(1)} %pad_maximum_fusion.2), channel_id=1, source_target_pairs={{0,17},{1,16},{2,19},{3,18},{4,21},{5,20},{6,23},{7,22},{8,25},{9,... | collective-permute-start | bytes 13832 | tf_op jit(solution)/shard_map/ppermute | solution.py:407
  4.0 1.5 %faces.1 = (s32[32,128]{1,0:T(8,128)S(1)}, s32[128,128]{1,0:T(8,128)S(1)}, f32[128,128]{1,0:T(8,128)S(1)}, f32[32,128]{1,0:T(8,128)S(1)}) custom-call(s32[6,8000]{1,0:T(8,128)} %bitcast.4, s32[128,128]{1,0:T(8,128)} %label_hbm.1, f32[128,128]{1,0:T(8,128)} %frozen_hbm.1), custom_call_target="tpu_custom_call" | custom-call | tf_op jit(solution)/shard_map/faces/pallas_call | solution.py:442
  5.5 0.1 constant_dynamic-update-slice_fusion.4
  5.6 0.0 collective-permute-done
  5.6 2.9 %collective-permute-start.1 = (f32[26,128]{1,0:T(8,128)S(1)}, f32[26,128]{1,0:T(8,128)S(1)}, u32[]{:S(2)}, u32[]{:S(2)}) collective-permute-start(f32[26,128]{1,0:T(8,128)S(1)} %pad_maximum_fusion.1), channel_id=1, source_target_pairs={{0,9},{1,8},{2,11},{3,10},{4,13},{5,12},{6,15},{7,14},{8,1},{9,0},... | collective-permute-start | bytes 39944 | tf_op jit(solution)/shard_map/ppermute | solution.py:407
  8.6 0.1 constant_dynamic-update-slice_fusion.3
  8.7 1.3 %collective-permute-done.1 = f32[26,128]{1,0:T(8,128)S(1)} collective-permute-done((f32[26,128]{1,0:T(8,128)S(1)}, f32[26,128]{1,0:T(8,128)S(1)}, u32[]{:S(2)}, u32[]{:S(2)}) %collective-permute-start.1) | collective-permute-done | bytes 13344 | tf_op jit(solution)/shard_map/ppermute | solution.py:407
  10.1 1.7 %collective-permute-start.2 = (f32[36,128]{1,0:T(8,128)S(1)}, f32[36,128]{1,0:T(8,128)S(1)}, u32[]{:S(2)}, u32[]{:S(2)}) collective-permute-start(f32[36,128]{1,0:T(8,128)S(1)} %pad_maximum_fusion), channel_id=1, source_target_pairs={{0,5},{1,4},{2,7},{3,6},{4,1},{5,0},{6,3},{7,2},{8,13},{9,12},{10,... | collective-permute-start | bytes 55304 | tf_op jit(solution)/shard_map/ppermute | solution.py:407
  11.7 0.1 constant_dynamic-update-slice_fusion.2
  11.8 1.5 %collective-permute-done.2 = f32[36,128]{1,0:T(8,128)S(1)} collective-permute-done((f32[36,128]{1,0:T(8,128)S(1)}, f32[36,128]{1,0:T(8,128)S(1)}, u32[]{:S(2)}, u32[]{:S(2)}) %collective-permute-start.2) | collective-permute-done | bytes 18464 | tf_op jit(solution)/shard_map/ppermute | solution.py:407
  13.3 0.3 %concatenate.26 = f32[72,128]{1,0:T(8,128)S(1)} concatenate(f32[5,128]{1,0:T(8,128)S(1)} %get-tuple-element.11, f32[5,128]{1,0:T(8,128)S(1)} %slice.50, f32[10,128]{1,0:T(8,128)S(1)} %slice.51, f32[20,128]{1,0:T(8,128)S(1)} %slice.53, f32[16,128]{1,0:T(8,128)S(1)} %get-tuple-element.21, f32[16,128]{1,0:T(8,128)S(1)} %get-tuple-element.20), dimensions={0} | concatenate | bytes 73728 | tf_op jit(solution)/shard_map/concatenate | solution.py:406
  13.7 1.6 %collective-permute-start.3 = (f32[72,128]{1,0:T(8,128)S(1)}, f32[72,128]{1,0:T(8,128)S(1)}, u32[]{:S(2)}, u32[]{:S(2)}) collective-permute-start(f32[72,128]{1,0:T(8,128)S(1)} %concatenate.26), channel_id=1, source_target_pairs={{0,3},{1,2},{2,1},{3,0},{4,7},{5,6},{6,5},{7,4},{8,11},{9,10},{10,... | collective-permute-start | bytes 110600 | tf_op jit(solution)/shard_map/ppermute | solution.py:407
  15.3 0.1 constant_dynamic-update-slice_fusion.1
  15.4 1.7 %collective-permute-done.3 = f32[72,128]{1,0:T(8,128)S(1)} collective-permute-done((f32[72,128]{1,0:T(8,128)S(1)}, f32[72,128]{1,0:T(8,128)S(1)}, u32[]{:S(2)}, u32[]{:S(2)}) %collective-permute-start.3) | collective-permute-done | bytes 36896 | tf_op jit(solution)/shard_map/ppermute | solution.py:407
  17.1 0.3 %concatenate.27.mine_ref = f32[116,128]{1,0:T(8,128)S(1)} concatenate(f32[5,128]{1,0:T(8,128)S(1)} %get-tuple-element.11, f32[5,128]{1,0:T(8,128)S(1)} %slice.50, f32[10,128]{1,0:T(8,128)S(1)} %slice.51, f32[20,128]{1,0:T(8,128)S(1)} %slice.53, f32[40,128]{1,0:T(8,128)S(1)} %slice.55, f32[16,128]{1,0:T(8,128)S(1)} %get-tuple-element.24, f32[16,128]{1,0:T(8,128)S(1)} %get-tuple-element.23, ...), dimensions={0} | concatenate | bytes 118784 | tf_op jit(solution)/shard_map/concatenate | solution.py:406
  17.5 0.5 %collective-permute-start.4 = (f32[116,128]{1,0:T(8,128)S(1)}, f32[116,128]{1,0:T(8,128)S(1)}, u32[]{:S(2)}, u32[]{:S(2)}) collective-permute-start(f32[116,128]{1,0:T(8,128)S(1)} %concatenate.27.mine_ref), channel_id=1, source_target_pairs={{0,1},{1,0},{2,3},{3,2},{4,5},{5,4},{6,7},{7,6},{8,9},{9,8},{10,11... | collective-permute-start | bytes 178184 | tf_op jit(solution)/shard_map/ppermute | solution.py:407
  18.0 0.1 constant_dynamic-update-slice_fusion
  18.1 1.7 %cells.1 = (f32[128,128]{1,0:T(8,128)S(1)}, f32[128,128]{1,0:T(8,128)S(1)}, bf16[128,384]{1,0:T(8,128)(2,1)S(1)}) custom-call(s32[32,128]{1,0:T(8,128)S(1)} %get-tuple-element.14.packed_ref, s32[128,128]{1,0:T(8,128)S(1)} %get-tuple-element.15.label_ref, f32[128,128]{1,0:T(8,128)S(1)} %get-tuple-element.16.frozen_ref, s32[2,128]{1,0:T(2,128)} %bitcast.6, ...), custom_call_target="tpu_custom_call" | custom-call | tf_op jit(solution)/shard_map/cells/pallas_call | solution.py:462
  19.8 0.0 collective-permute-done.4.theirs_ref.across_ref.passing_ref.edge_ref
  19.8 1.6 %finish.1 = (f32[2,128]{1,0:T(2,128)}, f32[128,128]{1,0:T(8,128)}) custom-call(f32[116,128]{1,0:T(8,128)S(1)} %concatenate.27.mine_ref, f32[116,128]{1,0:T(8,128)S(1)} %collective-permute-done.4.theirs_ref.across_ref.passing_ref.edge_ref, f32[116,128]{1,0:T(8,128)S(1)} %collective-permute-done.4.theirs_ref.across_ref.passing_ref.edge_ref, ...), custom_call_target="tpu_custom_call" | custom-call | tf_op jit(solution)/shard_map/finish/pallas_call | solution.py:610
  (19 shorter events, 0.1 us)
Async XLA Ops:
  1.5 4.1 %collective-permute-start = (f32[9,128]{1,0:T(8,128)S(1)}, f32[9,128]{1,0:T(8,128)S(1)}, u32[]{:S(2)}, u32[]{:S(2)}) collective-permute-start(f32[9,128]{1,0:T(8,128)S(1)} %pad_maximum_fusion.2), channel_id=1, source_target_pairs={{0,17},{1,16},{2,19},{3,18},{4,21},{5,20},{6,23},{7,22},{8,25},{9,... | collective-permute-start | bytes 13832 | tf_op jit(solution)/shard_map/ppermute | solution.py:407
  5.6 4.4 %collective-permute-start.1 = (f32[26,128]{1,0:T(8,128)S(1)}, f32[26,128]{1,0:T(8,128)S(1)}, u32[]{:S(2)}, u32[]{:S(2)}) collective-permute-start(f32[26,128]{1,0:T(8,128)S(1)} %pad_maximum_fusion.1), channel_id=1, source_target_pairs={{0,9},{1,8},{2,11},{3,10},{4,13},{5,12},{6,15},{7,14},{8,1},{9,0},... | collective-permute-start | bytes 39944 | tf_op jit(solution)/shard_map/ppermute | solution.py:407
  10.1 3.3 %collective-permute-start.2 = (f32[36,128]{1,0:T(8,128)S(1)}, f32[36,128]{1,0:T(8,128)S(1)}, u32[]{:S(2)}, u32[]{:S(2)}) collective-permute-start(f32[36,128]{1,0:T(8,128)S(1)} %pad_maximum_fusion), channel_id=1, source_target_pairs={{0,5},{1,4},{2,7},{3,6},{4,1},{5,0},{6,3},{7,2},{8,13},{9,12},{10,... | collective-permute-start | bytes 55304 | tf_op jit(solution)/shard_map/ppermute | solution.py:407
  13.7 3.4 %collective-permute-start.3 = (f32[72,128]{1,0:T(8,128)S(1)}, f32[72,128]{1,0:T(8,128)S(1)}, u32[]{:S(2)}, u32[]{:S(2)}) collective-permute-start(f32[72,128]{1,0:T(8,128)S(1)} %concatenate.26), channel_id=1, source_target_pairs={{0,3},{1,2},{2,1},{3,0},{4,7},{5,6},{6,5},{7,4},{8,11},{9,10},{10,... | collective-permute-start | bytes 110600 | tf_op jit(solution)/shard_map/ppermute | solution.py:407
  17.5 2.3 %collective-permute-start.4 = (f32[116,128]{1,0:T(8,128)S(1)}, f32[116,128]{1,0:T(8,128)S(1)}, u32[]{:S(2)}, u32[]{:S(2)}) collective-permute-start(f32[116,128]{1,0:T(8,128)S(1)} %concatenate.27.mine_ref), channel_id=1, source_target_pairs={{0,1},{1,0},{2,3},{3,2},{4,5},{5,4},{6,7},{7,6},{8,9},{9,8},{10,11... | collective-permute-start | bytes 178184 | tf_op jit(solution)/shard_map/ppermute | solution.py:407

commit v5 on v4

--- a/solution.py
+++ b/solution.py
@@ -11,6 +11,7 @@
 HEX_COUNT_LATER = 2
 CPC = 8
 LANES = 128
+CHUNKS = 4
 HIGHEST = lax.Precision.HIGHEST
 STEP = 0.004
 AXES = ("grp", "slab")
@@ -128,10 +129,9 @@
 
 
 def cells_kernel(
-    depth, flat, packed_ref, label_ref, frozen_ref, slot_hbm, seed_hbm, spread_hbm,
-    gathered_ref, nucleation_ref, spread_ref, code_ref, slot_ref, seed_ref, sems,
+    depth, flat, packed_ref, label_ref, frozen_ref, faces_ref, gathered_ref, onward_ref, code_ref
 ):
-    copies = started([(slot_hbm, slot_ref), (seed_hbm, seed_ref), (spread_hbm, spread_ref)], sems)
+    onward_ref[...] = faces_ref[...]
     edge_x, wide = frozen_ref.shape
 
     def look_up(chunk, carry):
@@ -159,6 +159,21 @@
         deep == 0, pltpu.roll(shares[5], wide - (depth - 1), 1), pltpu.roll(shares[5], 1, 1)
     )
     gathered_ref[...] = total
+
+
+def sites_kernel(
+    flat, packed_ref, edge_ref, faces_ref, slot_hbm, seed_hbm, spread_hbm,
+    nucleation_ref, ends_ref, spread_ref, onward_ref, slot_ref, seed_ref, sems,
+):
+    copies = started([(slot_hbm, slot_ref), (seed_hbm, seed_ref), (spread_hbm, spread_ref)], sems)
+    onward_ref[...] = faces_ref[...]
+    edge_x, wide = nucleation_ref.shape
+    for t in range(wide // LANES):
+        lanes = slice(t * LANES, (t + 1) * LANES)
+        rough = jnp.concatenate([edge_ref[:, lanes], jnp.zeros((4, LANES), jnp.float32)], 0)
+        codes = pick_codes(packed_ref, rough.astype(jnp.int32))
+        ends_ref[0:1, lanes] = rough[0:1] * level(codes[1:2], 1) * 0.25
+        ends_ref[1:2, lanes] = rough[2:3] * level(codes[3:4], 0) * 0.25
     for copy in copies:
         copy.wait()
     sites = seed_ref.shape[0]
@@ -268,25 +283,27 @@
 
 
 def finish_kernel(
-    plane, depth, flat, layers, group_lanes, sizes, first_row, cell_row, first_lane, wraps,
-    mine_ref, theirs_ref, across_ref, passing_ref, edge_ref, kept_ref, spread_ref, weave_ref,
+    plane, depth, flat, layers, group_lanes, sizes, first_layer, first_row, cell_row, first_lane,
+    wraps, mine_ref, theirs_ref, across_ref, passing_ref, edge_ref, kept_ref, spread_ref, weave_ref,
     packed_ref, gathered_ref, nucleation_ref, frozen_ref, *refs,
 ):
-    solid_ref, state_ref, even_ref, odd_ref, side_ref, extra_ref = refs[-6:]
+    solid_out, state_ref, even_ref, odd_ref, side_ref, extra_ref, solid_ref, new_ref, sems = refs[-9:]
     edge_x, wide = frozen_ref.shape
-    _, rows, width = state_ref.shape
+    _, all_rows, width = state_ref.shape
+    rows = even_ref.shape[0]
     heat_rows, across_row, passing_row, edge_row, devices = sizes
     core = lax.axis_index("slab") & 1
     if heat_rows:
         me = lax.axis_index("grp") * lax.axis_size("slab") + lax.axis_index("slab")
         for p, off in enumerate(arrival_order(devices)):
             source, block = (mine_ref, p) if p < devices // 2 else (theirs_ref, p - devices // 2)
+            row = lax.rem((me ^ off) * layers + (all_rows - first_layer()), all_rows)
             for c in range(5):
                 for layer in range(layers):
-                    state_ref[c, pl.ds((me ^ off) * layers + layer, 1), :] = source[
+                    state_ref[c, pl.ds(row + layer, 1), :] = source[
                         block * 5 + c : block * 5 + c + 1, layer * width : (layer + 1) * width
                     ]
-        state = [state_ref[i] for i in range(5)]
+        state = [state_ref[i, 0:rows, :] for i in range(5)]
     else:
         state = [mine_ref[i] for i in range(5)]
     side_ref[...] = jnp.zeros(side_ref.shape, jnp.float32)
@@ -298,25 +315,18 @@
         across_row : across_row + depth, :
     ]
     extra_ref[...] = gathered_ref[...] + jnp.transpose(side_ref[...])
-    for t in range(wide // LANES):
-        lanes = slice(t * LANES, (t + 1) * LANES)
-        rough = jnp.concatenate(
-            [edge_ref[edge_row : edge_row + 4, lanes], jnp.zeros((4, LANES), jnp.float32)], 0
-        )
-        codes = pick_codes(packed_ref, rough.astype(jnp.int32))
-        behind = rough[0:1] * level(codes[1:2], 1) * 0.25
-        ahead = rough[2:3] * level(codes[3:4], 0) * 0.25
-        extra_ref[0:1, lanes] += behind
-        extra_ref[edge_x - 1 : edge_x, lanes] += ahead
+    extra_ref[0:1, :] += edge_ref[edge_row : edge_row + 1, 0:wide]
+    extra_ref[edge_x - 1 : edge_x, :] += edge_ref[edge_row + 1 : edge_row + 2, 0:wide]
     even, odd = advance(plane, *state, spread_ref[...])
     if first_row is not None:
-        new_ref = refs[0]
         even_ref[:, 0:width] = even
         odd_ref[:, 0:width] = odd
         start = first_row()
         for layer in range(layers):
             new_ref[2 * layer : 2 * layer + 1, :] = even_ref[pl.ds(start + layer, 1), 0:width]
             new_ref[2 * layer + 1 : 2 * layer + 2, :] = odd_ref[pl.ds(start + layer, 1), 0:width]
+        new_copy = pltpu.make_async_copy(new_ref, refs[0], sems.at[CHUNKS])
+        new_copy.start()
     both = jnp.concatenate([even, odd], 0)
     both = pltpu.roll(both, first_lane(), 1)
     span = weave_ref.shape[0]
@@ -334,7 +344,9 @@
     odd_ref[:, 0:wide] = woven[rows:]
     first, middle, last = basis(lax.broadcasted_iota(jnp.int32, (CPC, wide), 0))
     base = cell_row()
-    for a in range(edge_x // CPC):
+    elements = edge_x // CPC
+    copies = []
+    for a in range(elements):
         cells = slice(a * CPC, (a + 1) * CPC)
         later = base + (a + 1)
         if wraps:
@@ -348,6 +360,19 @@
         rate = under * (under * extra_ref[cells, :] + nucleation_ref[cells, :])
         frozen = frozen_ref[cells, :]
         solid_ref[cells, :] = frozen + (1.0 - frozen) * (1.0 - jnp.exp(-rate))
+        done = (a + 1) * CHUNKS // elements
+        if done > len(copies):
+            low = copies[-1][1] if copies else 0
+            part = pl.ds(low, (a + 1) * CPC - low)
+            copy = pltpu.make_async_copy(
+                solid_ref.at[part, :], solid_out.at[part, :], sems.at[len(copies)]
+            )
+            copy.start()
+            copies.append((copy, (a + 1) * CPC))
+    for copy, _ in copies:
+        copy.wait()
+    if first_row is not None:
+        new_copy.wait()
 
 
 def weave_table(group_lanes, plane, depth, edge_y, first_step, wide):
@@ -403,7 +428,11 @@
         at = [0]
         for part in parts[:-1]:
             at.append(at[-1] + part.shape[0])
-        sent = jnp.concatenate(parts, 0) if len(parts) > 1 else parts[0]
+        total = at[-1] + parts[-1].shape[0]
+        sent = sum(
+            jnp.pad(part, ((row, total - row - part.shape[0]), (0, 0)))
+            for row, part in zip(at, parts)
+        )
         return sent, lax.ppermute(sent, AXES, [(i, i ^ flips) for i in range(devices)]), at
 
     def widened(array):
@@ -457,39 +486,64 @@
         compiler_params=PARAMS,
         name="faces",
     )(in_hbm(growth_reach_table.T), in_hbm(label), in_hbm(frozen))
-    seeds = up_to(seed_site_slots.shape[0], LANES)
-    short = seeds - seed_site_slots.shape[0]
-    gathered, nucleation, spread = pl.pallas_call(
+    gathered, faces_later = pl.pallas_call(
         functools.partial(cells_kernel, depth, flat_cells),
         out_shape=(
             jax.ShapeDtypeStruct((edge_x, wide), jnp.float32),
-            jax.ShapeDtypeStruct((edge_x, wide), jnp.float32),
-            jax.ShapeDtypeStruct((width, 3 * width), jnp.bfloat16),
+            jax.ShapeDtypeStruct((2 * depth, edge_x), jnp.float32),
         ),
-        in_specs=[VMEM] * 3 + [HBM] * 3,
-        out_specs=[VMEM] * 3,
-        scratch_shapes=[
-            pltpu.VMEM((edge_x, wide), jnp.int32),
-            pltpu.VMEM((seeds // LANES, LANES), jnp.int32),
-            pltpu.VMEM((seeds // LANES, LANES), jnp.int32),
-            pltpu.SemaphoreType.DMA((3,)),
-        ],
+        in_specs=[VMEM] * 4,
+        out_specs=[VMEM] * 2,
+        scratch_shapes=[pltpu.VMEM((edge_x, wide), jnp.int32)],
         compiler_params=PARAMS,
         name="cells",
-    )(
-        packed,
-        label,
-        frozen,
-        in_hbm(jnp.pad(seed_site_slots, (0, short), constant_values=-1).reshape(-1, LANES)),
-        in_hbm(jnp.pad(seed_crystal_label, (0, short)).reshape(-1, LANES)),
-        in_hbm(jnp.asarray(spread_tables(width, plane))),
-    )
+    )(packed, label, frozen, faces)
+    seeds = up_to(seed_site_slots.shape[0], LANES)
+    short = seeds - seed_site_slots.shape[0]
+
+    def sites(edges):
+        return pl.pallas_call(
+            functools.partial(sites_kernel, flat_cells),
+            out_shape=(
+                jax.ShapeDtypeStruct((edge_x, wide), jnp.float32),
+                jax.ShapeDtypeStruct((2, wide), jnp.float32),
+                jax.ShapeDtypeStruct((width, 3 * width), jnp.bfloat16),
+                jax.ShapeDtypeStruct((2 * depth, edge_x), jnp.float32),
+            ),
+            in_specs=[VMEM] * 3 + [HBM] * 3,
+            out_specs=[VMEM] * 4,
+            scratch_shapes=[
+                pltpu.VMEM((seeds // LANES, LANES), jnp.int32),
+                pltpu.VMEM((seeds // LANES, LANES), jnp.int32),
+                pltpu.SemaphoreType.DMA((3,)),
+            ],
+            compiler_params=PARAMS,
+            name="sites",
+        )(
+            packed,
+            edges,
+            faces_later,
+            in_hbm(jnp.pad(seed_site_slots, (0, short), constant_values=-1).reshape(-1, LANES)),
+            in_hbm(jnp.pad(seed_crystal_label, (0, short)).reshape(-1, LANES)),
+            in_hbm(jnp.asarray(spread_tables(width, plane))),
+        )
 
     core, pair = me & 1, slab >> 1
-    to_behind, to_ahead = faces[:depth], faces[depth:]
-    onward = jnp.where(core == 1, to_ahead, 0.0)
-    backward = jnp.where(core == 0, to_behind, 0.0)
+
+    def packets(faces):
+        return jnp.where(core == 1, faces[depth:], 0.0), jnp.where(core == 0, faces[:depth], 0.0)
+
+    onward, backward = packets(faces)
     heat, edges = [held], None
+    if groups > 2:
+        ring = [(i, (i + 1) % groups) for i in range(groups)]
+        edges = jnp.concatenate(
+            [
+                lax.ppermute(high_edge, "grp", ring),
+                lax.ppermute(low_edge, "grp", [(j, i) for i, j in ring]),
+            ]
+        )
+    moved, ends = 0, None
     as_face = lambda part: part.reshape(-1)[: depth * edge_x].reshape(depth, edge_x)
     for bit in reversed(range(1, devices.bit_length() - 1)):
         rides = 1 << bit < slabs
@@ -509,31 +563,28 @@
         if groups == 2 and 1 << bit == slabs:
             edges = parts[0].reshape(-1)[: 4 * wide].reshape(4, wide)
         elif rides and low:
+            if moved == 0:
+                onward, backward = packets(faces_later)
             onward = jnp.where(moves_on, as_face(parts[0]), onward)
             backward = jnp.where(moves_back, as_face(parts[0]), backward)
+            moved += 1
         elif rides:
             onward, backward = as_face(parts[0]), as_face(parts[1])
+        if edges is not None and ends is None:
+            nucleation, ends, spread, faces_last = sites(edges)
     extra = [
-        lines(jnp.where(core == 0, to_ahead, to_behind), unit),
+        lines(jnp.where(core == 0, faces_last[depth:], faces_last[:depth]), unit),
         lines(jnp.where(core == 1, onward, backward), unit),
     ]
-    if edges is not None:
-        extra.append(lines(edges, unit))
+    if groups == 2:
+        extra.append(lines(ends, unit))
     kept = jnp.where(core == 0, onward, backward)
     sent, got, at = exchanged(heat + extra, 1)
     heat_rows = sum(part.shape[0] for part in heat)
     at = at[len(heat) :]
     across, passing = (as_face(got[row : row + part.shape[0]]) for row, part in zip(at, extra[:2]))
-    if edges is not None:
-        edges = got[at[2] : at[2] + extra[2].shape[0]].reshape(-1)[: 4 * wide].reshape(4, wide)
-    if edges is None:
-        ring = [(i, (i + 1) % groups) for i in range(groups)]
-        edges = jnp.concatenate(
-            [
-                lax.ppermute(high_edge, "grp", ring),
-                lax.ppermute(low_edge, "grp", [(j, i) for i, j in ring]),
-            ]
-        )
+    if groups == 2:
+        ends = got[at[2] : at[2] + extra[2].shape[0]].reshape(-1)[: 2 * wide].reshape(2, wide)
     brick_layers = edge_x // CPC
     first_cell = slab * edge_y
     first_element = first_cell // CPC
@@ -543,7 +594,8 @@
     if direct:
         inputs = (sent, got, got, got, got)
         sizes = (heat_rows, *at, devices)
-        start_layer = start_y = 0
+        start_layer, start_y = group * brick_layers - 2, 0
+        rows = min(up_to(need_layers, 8), all_layers)
     else:
         order = np.argsort(arrival_order(devices))
         blocks = jnp.concatenate([sent[:heat_rows], got[:heat_rows]], 0).reshape(devices, 5, layers, flat)
@@ -580,8 +632,9 @@
         state, start_layer, start_y = window(
             group * brick_layers - 2, need_layers, first_element - 2, need_y
         )
-        inputs = (state, state, across, passing, edges)
+        inputs = (state, state, across, passing, ends)
         sizes = (0, 0, 0, 0, devices)
+        rows = state.shape[1]
     if edge_y % CPC == 0 or CPC % edge_y == 0:
         covered = max(edge_y // CPC, 1)
     else:
@@ -594,33 +647,41 @@
             return lambda: 2
         return lambda: layer(lax.axis_index("grp"), lax.axis_index("slab"))
 
+    def first_layer():
+        return lax.rem(lax.axis_index("grp") * brick_layers + (all_layers - 2), all_layers)
+
     own_layer = lambda g, s: (g * slabs + s) * layers
     cell_row = place(start_layer, lambda g, s: g * brick_layers)
     own_row = place(start_layer, own_layer)
+    if direct:
+        own_row = lambda: lax.axis_index("slab") * layers + 2
     if isinstance(start_y, int):
         first_lane = lambda: lax.rem(
             width - (lax.axis_index("slab") * edge_y // CPC) * 2 * plane, width
         )
     else:
         first_lane = lambda: width - 4 * plane
-    rows = all_layers if direct else state.shape[1]
     new_shape = jax.ShapeDtypeStruct((2 * layers, flat), jnp.float32)
     solid_shape = jax.ShapeDtypeStruct((edge_x, wide), jnp.float32)
     span = max(width, wide)
     results = pl.pallas_call(
         functools.partial(
             finish_kernel, plane, depth, flat_cells, layers, group_lanes, sizes,
-            own_row if whole else None, cell_row, first_lane, isinstance(start_layer, int),
+            first_layer, own_row if whole else None, cell_row, first_lane,
+            isinstance(start_layer, int),
         ),
         out_shape=(new_shape, solid_shape) if whole else (solid_shape,),
         in_specs=[VMEM] * 12,
-        out_specs=(VMEM,) * (1 + whole),
+        out_specs=(HBM,) * (1 + whole),
         scratch_shapes=[
-            pltpu.VMEM((5, rows, width), jnp.float32),
+            pltpu.VMEM((5, all_layers if direct else rows, width), jnp.float32),
             pltpu.VMEM((rows, span), jnp.float32),
             pltpu.VMEM((rows, span), jnp.float32),
             pltpu.VMEM((wide, edge_x), jnp.float32),
             pltpu.VMEM((edge_x, wide), jnp.float32),
+            pltpu.VMEM((edge_x, wide), jnp.float32),
+            pltpu.VMEM(new_shape.shape, jnp.float32),
+            pltpu.SemaphoreType.DMA((CHUNKS + 1,)),
         ],
         compiler_params=PARAMS,
         name="finish",

time: 21.6 us -> 20.1 us (0.931)
  waiting for transfers between devices: 4.58 us -> 3.39 us
  local copies, waits for them, and re-layouts: 0.71 us -> 0.03 us
  Pallas kernels: 5.58 us -> 5.88 us
    pallas_call x0 -> x1, Pallas kernels: none -> 1.22 us  [sites(): pl.pallas_call(functools.partial(sites_kernel, flat_cells), out_shape=(ja...]
    ppermute x5, waiting for transfers between devices: 4.58 us -> 3.39 us  [exchanged(): lax.ppermute(sent, AXES, [(i, i ^ flips) for i in range(devices)])]
    pallas_call x1, Pallas kernels: 1.71 us -> 0.81 us  [body(): pl.pallas_call(functools.partial(cells_kernel, depth, flat_cells), out_sh...]
    concatenate x2 -> x0, local copies, waits for them, and re-layouts: 0.69 us -> none  [exchanged(): sent = jnp.concatenate(parts, 0) if len(parts) > 1 else parts[0]]
  transfers between devices with their start and end apart: 5 -> 5, of which waited for: 3 -> 4; matrix products, arithmetic and copies ran while one was open for 3% -> 3% of each run, Pallas kernels for 15% -> 18%
where the time goes in v5:
time: 20.1 us; the launch traced here: 19.9 us
  starting transfers between devices  9.17 us (46%)
  Pallas kernels  5.88 us (29%)
  waiting for transfers between devices  3.39 us (17%)
  between operations  0.8 us (4%)
  other arithmetic  0.62 us (3%)
    ppermute x5, starting transfers between devices, exchanged(): lax.ppermute(sent, AXES, [(i, i ^ flips) for i in range(devices)])  9.17 us
    ppermute x5, waiting for transfers between devices, exchanged(): lax.ppermute(sent, AXES, [(i, i ^ flips) for i in range(devices)])  3.39 us
    pallas_call x1, Pallas kernels, body(): pl.pallas_call(functools.partial(finish_kernel, plane, depth, flat_cells,...  1.55 us
    pallas_call x1, Pallas kernels, body(): pl.pallas_call(functools.partial(faces_kernel, depth, flat_cells), out_sh...  1.45 us
    pallas_call x1, Pallas kernels, sites(): pl.pallas_call(functools.partial(sites_kernel, flat_cells), out_shape=(ja...  1.22 us
    pallas_call x1, Pallas kernels, body(): pl.pallas_call(pack_kernel, out_shape=(jax.ShapeDtypeStruct((5, unit), jn...  0.85 us
    pallas_call x1, Pallas kernels, body(): pl.pallas_call(functools.partial(cells_kernel, depth, flat_cells), out_sh...  0.81 us
  transfers between devices with their start and end apart: 5, of which 4 were waited for; matrix products, arithmetic and copies ran while one was open for 3% of the time, Pallas kernels for 18%

profile of v5, /device:TPU:0, one launch (start us, length us, event | category | flops | bytes accessed | tf_op | source)
XLA Modules:
  0.0 19.9 jit_solution(17601316867656379989)
XLA Ops:
  0.6 0.8 %pack.1 = (f32[5,128]{1,0:T(8,128)S(1)}, f32[4,128]{1,0:T(4,128)S(1)}) custom-call(f32[2,128]{1,0:T(2,128)} %state_ref.1, f32[2,128]{1,0:T(2,128)} %heat_ref.1, f32[1,32]{1,0:T(1,128)} %kappa_ref.1, f32[128,128]{1,0:T(8,128)} %frozen_hbm.1, s32[128,128]{1,0:T(8,128)} %label_hbm.1), custom_call_target="tpu_custom_call" | custom-call | tf_op jit(solution)/shard_map/pack/pallas_call | solution.py:444
  1.5 2.4 %collective-permute-start = (f32[9,128]{1,0:T(8,128)S(1)}, f32[9,128]{1,0:T(8,128)S(1)}, u32[]{:S(2)}, u32[]{:S(2)}) collective-permute-start(f32[9,128]{1,0:T(8,128)S(1)} %pad_add_fusion.4), channel_id=1, source_target_pairs={{0,17},{1,16},{2,19},{3,18},{4,21},{5,20},{6,23},{7,22},{8,25},{9,... | collective-permute-start | bytes 13832 | tf_op jit(solution)/shard_map/ppermute | solution.py:436
  4.0 0.1 constant_dynamic-update-slice_fusion.4
  4.1 0.1 constant_dynamic-update-slice_fusion.3
  4.2 1.5 %faces.1 = (s32[32,128]{1,0:T(8,128)S(1)}, s32[128,128]{1,0:T(8,128)S(1)}, f32[128,128]{1,0:T(8,128)S(1)}, f32[32,128]{1,0:T(8,128)S(1)}) custom-call(s32[6,8000]{1,0:T(8,128)} %bitcast.4, s32[128,128]{1,0:T(8,128)} %label_hbm.1, f32[128,128]{1,0:T(8,128)} %frozen_hbm.1), custom_call_target="tpu_custom_call" | custom-call | tf_op jit(solution)/shard_map/faces/pallas_call | solution.py:471
  5.7 0.0 collective-permute-done
  5.8 2.9 %collective-permute-start.1 = (f32[26,128]{1,0:T(8,128)S(1)}, f32[26,128]{1,0:T(8,128)S(1)}, u32[]{:S(2)}, u32[]{:S(2)}) collective-permute-start(f32[26,128]{1,0:T(8,128)S(1)} %pad_add_fusion.3), channel_id=1, source_target_pairs={{0,9},{1,8},{2,11},{3,10},{4,13},{5,12},{6,15},{7,14},{8,1},{9,0},... | collective-permute-start | bytes 39944 | tf_op jit(solution)/shard_map/ppermute | solution.py:436
  8.7 0.1 constant_dynamic-update-slice_fusion.2
  8.8 0.8 %cells.1 = (f32[128,128]{1,0:T(8,128)S(1)}, f32[32,128]{1,0:T(8,128)S(1)}) custom-call(s32[32,128]{1,0:T(8,128)S(1)} %get-tuple-element.17.packed_ref, s32[128,128]{1,0:T(8,128)S(1)} %get-tuple-element.18.label_ref, f32[128,128]{1,0:T(8,128)S(1)} %get-tuple-element.19.frozen_ref, f32[32,128]{1,0:T(8,128)S(1)} %get-tuple-element.16.faces_ref), custom_call_target="tpu_custom_call" | custom-call | tf_op jit(solution)/shard_map/cells/pallas_call | solution.py:489
  9.6 0.5 %collective-permute-done.1 = f32[26,128]{1,0:T(8,128)S(1)} collective-permute-done((f32[26,128]{1,0:T(8,128)S(1)}, f32[26,128]{1,0:T(8,128)S(1)}, u32[]{:S(2)}, u32[]{:S(2)}) %collective-permute-start.1) | collective-permute-done | bytes 13344 | tf_op jit(solution)/shard_map/ppermute | solution.py:436
  10.2 1.7 %collective-permute-start.2 = (f32[36,128]{1,0:T(8,128)S(1)}, f32[36,128]{1,0:T(8,128)S(1)}, u32[]{:S(2)}, u32[]{:S(2)}) collective-permute-start(f32[36,128]{1,0:T(8,128)S(1)} %pad_add_fusion.2), channel_id=1, source_target_pairs={{0,5},{1,4},{2,7},{3,6},{4,1},{5,0},{6,3},{7,2},{8,13},{9,12},{10,... | collective-permute-start | bytes 55304 | tf_op jit(solution)/shard_map/ppermute | solution.py:436
  11.8 0.1 constant_dynamic-update-slice_fusion.1
  11.9 1.2 %sites.1 = (f32[128,128]{1,0:T(8,128)S(1)}, f32[2,128]{1,0:T(2,128)S(1)}, bf16[128,384]{1,0:T(8,128)(2,1)S(1)}, f32[32,128]{1,0:T(8,128)S(1)}) custom-call(s32[32,128]{1,0:T(8,128)S(1)} %get-tuple-element.17.packed_ref, f32[4,128]{1,0:T(4,128)S(1)} %slice.87.edge_ref, f32[32,128]{1,0:T(8,128)S(1)} %get-tuple-element.20.faces_ref, s32[2,128]{1,0:T(2,128)} %bitcast.6, ...), custom_call_target="tpu_custom_call" | custom-call | tf_op jit(solution)/shard_map/sites/pallas_call | solution.py:505
  13.2 0.3 %collective-permute-done.2 = f32[36,128]{1,0:T(8,128)S(1)} collective-permute-done((f32[36,128]{1,0:T(8,128)S(1)}, f32[36,128]{1,0:T(8,128)S(1)}, u32[]{:S(2)}, u32[]{:S(2)}) %collective-permute-start.2) | collective-permute-done | bytes 18464 | tf_op jit(solution)/shard_map/ppermute | solution.py:436
  13.5 1.6 %collective-permute-start.3 = (f32[72,128]{1,0:T(8,128)S(1)}, f32[72,128]{1,0:T(8,128)S(1)}, u32[]{:S(2)}, u32[]{:S(2)}) collective-permute-start(f32[72,128]{1,0:T(8,128)S(1)} %pad_add_fusion.1), channel_id=1, source_target_pairs={{0,3},{1,2},{2,1},{3,0},{4,7},{5,6},{6,5},{7,4},{8,11},{9,10},{10,... | collective-permute-start | bytes 110600 | tf_op jit(solution)/shard_map/ppermute | solution.py:436
  15.1 1.8 %collective-permute-done.3 = f32[72,128]{1,0:T(8,128)S(1)} collective-permute-done((f32[72,128]{1,0:T(8,128)S(1)}, f32[72,128]{1,0:T(8,128)S(1)}, u32[]{:S(2)}, u32[]{:S(2)}) %collective-permute-start.3) | collective-permute-done | bytes 36896 | tf_op jit(solution)/shard_map/ppermute | solution.py:436
  16.9 0.5 %collective-permute-start.4 = (f32[114,128]{1,0:T(8,128)S(1)}, f32[114,128]{1,0:T(8,128)S(1)}, u32[]{:S(2)}, u32[]{:S(2)}) collective-permute-start(f32[114,128]{1,0:T(8,128)S(1)} %pad_add_fusion.mine_ref), channel_id=1, source_target_pairs={{0,1},{1,0},{2,3},{3,2},{4,5},{5,4},{6,7},{7,6},{8,9},{9,8},{10,11... | collective-permute-start | bytes 175112 | tf_op jit(solution)/shard_map/ppermute | solution.py:436
  17.4 0.1 constant_dynamic-update-slice_fusion
  17.5 0.8 %collective-permute-done.4.theirs_ref.across_ref.passing_ref.edge_ref = f32[114,128]{1,0:T(8,128)S(1)} collective-permute-done((f32[114,128]{1,0:T(8,128)S(1)}, f32[114,128]{1,0:T(8,128)S(1)}, u32[]{:S(2)}, u32[]{:S(2)}) %collective-permute-start.4) | collective-permute-done | bytes 58400 | tf_op jit(solution)/shard_map/ppermute | solution.py:436
  18.3 1.6 %finish.1 = (f32[2,128]{1,0:T(2,128)}, f32[128,128]{1,0:T(8,128)}) custom-call(f32[114,128]{1,0:T(8,128)S(1)} %pad_add_fusion.mine_ref, f32[114,128]{1,0:T(8,128)S(1)} %collective-permute-done.4.theirs_ref.across_ref.passing_ref.edge_ref, f32[114,128]{1,0:T(8,128)S(1)} %collective-permute-done.4.theirs_ref.across_ref.passing_ref.edge_ref, ...), custom_call_target="tpu_custom_call" | custom-call | tf_op jit(solution)/shard_map/finish/pallas_call | solution.py:667
  (26 shorter events, 0.2 us)
Async XLA Ops:
  1.5 4.2 %collective-permute-start = (f32[9,128]{1,0:T(8,128)S(1)}, f32[9,128]{1,0:T(8,128)S(1)}, u32[]{:S(2)}, u32[]{:S(2)}) collective-permute-start(f32[9,128]{1,0:T(8,128)S(1)} %pad_add_fusion.4), channel_id=1, source_target_pairs={{0,17},{1,16},{2,19},{3,18},{4,21},{5,20},{6,23},{7,22},{8,25},{9,... | collective-permute-start | bytes 13832 | tf_op jit(solution)/shard_map/ppermute | solution.py:436
  5.8 4.4 %collective-permute-start.1 = (f32[26,128]{1,0:T(8,128)S(1)}, f32[26,128]{1,0:T(8,128)S(1)}, u32[]{:S(2)}, u32[]{:S(2)}) collective-permute-start(f32[26,128]{1,0:T(8,128)S(1)} %pad_add_fusion.3), channel_id=1, source_target_pairs={{0,9},{1,8},{2,11},{3,10},{4,13},{5,12},{6,15},{7,14},{8,1},{9,0},... | collective-permute-start | bytes 39944 | tf_op jit(solution)/shard_map/ppermute | solution.py:436
  10.2 3.3 %collective-permute-start.2 = (f32[36,128]{1,0:T(8,128)S(1)}, f32[36,128]{1,0:T(8,128)S(1)}, u32[]{:S(2)}, u32[]{:S(2)}) collective-permute-start(f32[36,128]{1,0:T(8,128)S(1)} %pad_add_fusion.2), channel_id=1, source_target_pairs={{0,5},{1,4},{2,7},{3,6},{4,1},{5,0},{6,3},{7,2},{8,13},{9,12},{10,... | collective-permute-start | bytes 55304 | tf_op jit(solution)/shard_map/ppermute | solution.py:436
  13.5 3.4 %collective-permute-start.3 = (f32[72,128]{1,0:T(8,128)S(1)}, f32[72,128]{1,0:T(8,128)S(1)}, u32[]{:S(2)}, u32[]{:S(2)}) collective-permute-start(f32[72,128]{1,0:T(8,128)S(1)} %pad_add_fusion.1), channel_id=1, source_target_pairs={{0,3},{1,2},{2,1},{3,0},{4,7},{5,6},{6,5},{7,4},{8,11},{9,10},{10,... | collective-permute-start | bytes 110600 | tf_op jit(solution)/shard_map/ppermute | solution.py:436
  16.9 1.4 %collective-permute-start.4 = (f32[114,128]{1,0:T(8,128)S(1)}, f32[114,128]{1,0:T(8,128)S(1)}, u32[]{:S(2)}, u32[]{:S(2)}) collective-permute-start(f32[114,128]{1,0:T(8,128)S(1)} %pad_add_fusion.mine_ref), channel_id=1, source_target_pairs={{0,1},{1,0},{2,3},{3,2},{4,5},{5,4},{6,7},{7,6},{8,9},{9,8},{10,11... | collective-permute-start | bytes 175112 | tf_op jit(solution)/shard_map/ppermute | solution.py:436

commit v6 on v5

--- a/solution.py
+++ b/solution.py
@@ -36,9 +36,10 @@
 
 
 def pack_kernel(
-    state_ref, heat_ref, kappa_ref, frozen_ref, label_ref, held_ref, edge_ref,
-    state, heat, kappa, frozen, label, sems,
+    state_ref, heat_ref, kappa_ref, frozen_ref, label_ref, held_ref, *refs
 ):
+    state, heat, kappa, frozen, label, sems = refs[-6:]
+    edge_ref = refs[0] if len(refs) > 6 else held_ref.at[5:9, :]
     layers, elements = kappa.shape
     flat = state.shape[1]
     edge_x = frozen_ref.shape[0]
@@ -194,19 +195,30 @@
 
 def spread_tables(width, plane):
     rows_y, deep = width // plane, plane // 2
-    along = np.zeros((rows_y // 2, rows_y), np.float32)
-    down = np.zeros((deep, plane), np.float32)
-    for table in (along, down):
-        for element in range(table.shape[0]):
+
+    def tables(count):
+        spread, after, before = (np.zeros((count // 2, count), np.float32) for _ in range(3))
+        for element in range(count // 2):
             for local, weight in enumerate((1, 4, 1)):
-                table[element, (2 * element + local) % table.shape[1]] += weight
-    first_y = np.zeros_like(along)
-    first_z = np.zeros_like(down)
-    first_y[np.arange(rows_y // 2), 2 * np.arange(rows_y // 2)] = 1
-    first_z[np.arange(deep), 2 * np.arange(deep)] = 1
-    full = [np.kron(along, down), np.kron(first_y, down), np.kron(along, first_z)]
-    out = np.zeros((width, 3 * width), jnp.bfloat16)
-    out[: 3 * (width // 4)] = np.concatenate([np.concatenate(full, 1)] * 3, 0)
+                spread[element, (2 * element + local) % count] += weight
+            for local in range(2):
+                after[element, (2 * element + local) % count] += 1
+                before[element, (2 * element + local + 1) % count] += 1
+        return spread, after, before
+
+    spread_y, after_y, before_y = tables(rows_y)
+    spread_z, after_z, before_z = tables(plane)
+    full = [
+        np.kron(spread_y, spread_z),
+        np.kron(after_y, spread_z),
+        np.kron(before_y, spread_z),
+        np.kron(spread_y, after_z),
+        np.kron(spread_y, before_z),
+    ]
+    half = lambda count: np.where(np.arange(count) % 2 == 1, 0.5, 1.0)
+    inverse = 27.0 * np.kron(half(rows_y), half(plane))
+    out = np.zeros((width, 5 * width), jnp.bfloat16)
+    out[: 3 * (width // 4)] = np.concatenate([np.concatenate([t * inverse for t in full], 1)] * 3, 0)
     return out
 
 
@@ -225,42 +237,57 @@
     turn = lambda v, by: pltpu.roll(v, by % width, 1)
     lane = lax.broadcasted_iota(jnp.int32, (rows, width), 1)
     row_y, deep = split_index(lane, plane)
+    even_y, even_z = row_y & 1 == 0, deep & 1 == 0
     first, second, third = pieces(kappa)
     joined = first + turn(second, width // 4) + turn(third, 2 * (width // 4))
     lines = jnp.dot(joined.astype(jnp.bfloat16), spread, preferred_element_type=jnp.float32)
-    lines = lines * (1.0 / 108.0)
-    along_x, along_y, along_z = (lines[:, i * width : (i + 1) * width] for i in range(3))
-    y_even, y_odd = along_y + down(along_y), 4.0 * along_y
-    z_even, z_odd = along_z + down(along_z), 4.0 * along_z
-    inverse = 27.0 * jnp.where(row_y & 1 == 1, 0.5, 1.0) * jnp.where(deep & 1 == 1, 0.5, 1.0)
-    scale_even, scale_odd = inverse, 0.5 * inverse
-
-    def bend(first, second, third, coefficient):
-        curve = (4.0 * coefficient) * (first - 2.0 * second + third)
-        slope = (3.0 * coefficient) * (third - first)
-        return curve - slope, -2.0 * curve, curve + slope
-
-    def in_plane(values, along_y, along_z):
-        a, b, c = bend(values, turn(values, -plane), turn(values, -2 * plane), along_y)
-        result = a + turn(b, plane) + turn(c, 2 * plane)
-        third = jnp.where(deep == plane - 2, turn(values, plane - 2), turn(values, -2))
-        a, b, c = bend(values, turn(values, -1), third, along_z)
-        return result + a + turn(b, 1) + jnp.where(deep == 0, turn(c, 2 - plane), turn(c, 2))
-
-    def missing(v_even, v_odd):
-        a, b, c = bend(v_even, v_odd, up(v_even), along_x)
-        k_even = a + down(c) + in_plane(v_even, y_even, z_even)
-        k_odd = b + in_plane(v_odd, y_odd, z_odd)
+    lines = lines * (STEP / 108.0)
+    along_x, *others = (lines[:, i * width : (i + 1) * width] for i in range(5))
+    behind_x = down(along_x)
+    scale = STEP * 27.0 * jnp.where(even_y, 1.0, 0.5) * jnp.where(even_z, 1.0, 0.5)
+    heat_even, heat_odd = scale * heat_even, (0.5 * scale) * heat_odd
+
+    def in_plane(parts):
+        after_y, before_y, after_z, before_z = parts
+        own = jnp.where(even_y, 7.0 * (after_y + before_y), 16.0 * after_y)
+        own = own + jnp.where(even_z, 7.0 * (after_z + before_z), 16.0 * after_z)
+        far = [jnp.where(even_y, v, 0.0) for v in parts[:2]] + [
+            jnp.where(even_z, v, 0.0) for v in parts[2:]
+        ]
+        return own, [-8.0 * v for v in parts], far
+
+    own_even, near_even, far_even = in_plane([v + down(v) for v in others])
+    own_odd, near_odd, far_odd = in_plane([2.0 * v for v in others])
+    own_even = own_even + 7.0 * (along_x + behind_x)
+    own_odd = own_odd + 8.0 * along_x
+    near_x, near_behind, near_odd_x = -8.0 * along_x, -8.0 * behind_x, -4.0 * along_x
+
+    def moved(values, by):
+        if by > 0:
+            return jnp.where(deep + by >= plane, turn(values, plane - by), turn(values, -by))
+        return jnp.where(deep + by < 0, turn(values, -by - plane), turn(values, -by))
+
+    def neighbours(values, near, far):
+        ahead_y, back_y = turn(values, -plane), turn(values, plane)
+        total = near[0] * ahead_y + near[1] * back_y
+        total += near[2] * moved(values, 1) + near[3] * moved(values, -1)
+        total += far[0] * turn(values, -2 * plane) + far[1] * turn(values, 2 * plane)
+        if plane == 4:
+            return total + (far[2] + far[3]) * moved(values, 2)
+        return total + far[2] * moved(values, 2) + far[3] * moved(values, -2)
+
+    def change(v_even, v_odd):
+        following = up(v_even)
+        k_even = own_even * v_even + along_x * following + behind_x * down(v_even)
+        k_even += near_x * v_odd + near_behind * down(v_odd)
+        k_odd = own_odd * v_odd + near_odd_x * (v_even + following)
+        k_even += neighbours(v_even, near_even, far_even)
+        k_odd += neighbours(v_odd, near_odd, far_odd)
         return heat_even - k_even, heat_odd - k_odd
 
-    one_even, one_odd = missing(even, odd)
-    two_even, two_odd = missing(
-        even + (STEP * scale_even) * one_even, odd + (STEP * scale_odd) * one_odd
-    )
-    return (
-        even + (0.5 * STEP * scale_even) * (one_even + two_even),
-        odd + (0.5 * STEP * scale_odd) * (one_odd + two_odd),
-    )
+    one_even, one_odd = change(even, odd)
+    two_even, two_odd = change(even + one_even, odd + one_odd)
+    return even + 0.5 * (one_even + two_even), odd + 0.5 * (one_odd + two_odd)
 
 
 def heat_kernel(plane, layers, first_row, state_ref, spread_ref, new_ref, even_ref, odd_ref):
@@ -328,15 +355,18 @@
         new_copy = pltpu.make_async_copy(new_ref, refs[0], sems.at[CHUNKS])
         new_copy.start()
     both = jnp.concatenate([even, odd], 0)
-    both = pltpu.roll(both, first_lane(), 1)
-    span = weave_ref.shape[0]
-    if span > width:
-        both = jnp.concatenate([both, jnp.zeros((2 * rows, span - width), jnp.float32)], 1)
-    lane = lax.broadcasted_iota(jnp.int32, both.shape, 1)
-    first, second, third = pieces(jnp.where(lane < group_lanes, both, 0.0))
-    joined = first
-    for i, piece in enumerate((second, third, first, second)):
-        joined = joined + pltpu.roll(piece, (i + 1) * group_lanes, 1)
+    if group_lanes:
+        lane = lax.broadcasted_iota(jnp.int32, both.shape, 1)
+        first_node = first_lane()
+        inside = (lane >= first_node) & (lane < first_node + group_lanes)
+        inside |= lane + width < first_node + group_lanes
+        first, second, third = pieces(jnp.where(inside, both, 0.0))
+        joined = first
+        for i, piece in enumerate((second, third, first, second)):
+            joined = joined + pltpu.roll(piece, (i + 1) * group_lanes, 1)
+    else:
+        first, second, third = pieces(both)
+        joined = jnp.concatenate([first, second, third, first, second], 1)
     woven = jnp.dot(
         joined.astype(jnp.bfloat16), weave_ref[...], preferred_element_type=jnp.float32
     )
@@ -375,17 +405,23 @@
         new_copy.wait()
 
 
-def weave_table(group_lanes, plane, depth, edge_y, first_step, wide):
-    node, cell = jnp.arange(group_lanes)[:, None], jnp.arange(wide)[None, :]
+def weave_table(group_lanes, width, plane, depth, edge_y, first_step, first_node, wide):
+    span = group_lanes or width
+    row = jnp.arange(width if group_lanes else 5 * width)[:, None]
+    cell = jnp.arange(wide)[None, :]
+    if group_lanes:
+        row = (row - first_node) % width
+        copy, node = row // span, row % span
+    else:
+        copy, node = row // span, (row % span - first_node) % width
     cell_y, cell_z = first_step + cell // depth, cell % depth
     step_y = node // plane - 2 * (cell_y // CPC)
-    step_z = jnp.remainder(node % plane - 2 * (cell_z // CPC), plane)
+    step_z = (node % plane - 2 * (cell_z // CPC)) % plane
     take = lambda step, at: sum(jnp.where(step == i, v, 0.0) for i, v in enumerate(basis(at % CPC)))
-    full = jnp.where(cell < edge_y * depth, take(step_y, cell_y) * take(step_z, cell_z), 0.0)
+    full = take(step_y, cell_y) * take(step_z, cell_z)
     high = jnp.floor(full * 128.0) * (1.0 / 128.0)
-    both = jnp.stack([high, high, high, full - high, full - high]).reshape(5 * group_lanes, wide)
-    short = up_to(5 * group_lanes, LANES) - 5 * group_lanes
-    return jnp.pad(both, ((0, short), (0, 0))).astype(jnp.bfloat16)
+    part = jnp.where(copy < 3, high, full - high)
+    return jnp.where((copy < 5) & (cell < edge_y * depth), part, 0.0).astype(jnp.bfloat16)
 
 
 def arrival_order(devices):
@@ -424,15 +460,16 @@
     wide = up_to(flat_cells, LANES)
     all_layers = layers * devices
 
-    def exchanged(parts, flips):
+    def exchanged(parts, flips, sent=None):
         at = [0]
         for part in parts[:-1]:
             at.append(at[-1] + part.shape[0])
         total = at[-1] + parts[-1].shape[0]
-        sent = sum(
-            jnp.pad(part, ((row, total - row - part.shape[0]), (0, 0)))
-            for row, part in zip(at, parts)
-        )
+        if sent is None:
+            sent = sum(
+                jnp.pad(part, ((row, total - row - part.shape[0]), (0, 0)))
+                for row, part in zip(at, parts)
+            )
         return sent, lax.ppermute(sent, AXES, [(i, i ^ flips) for i in range(devices)]), at
 
     def widened(array):
@@ -441,14 +478,17 @@
     unit = layers * flat
     count = growth_reach_table.shape[0]
     frozen, label = widened(frozen_share_map), widened(crystal_label_map)
-    held, edge_rows = pl.pallas_call(
+    joined = groups == 2 and wide == unit
+    packed_rows = pl.pallas_call(
         pack_kernel,
-        out_shape=(
+        out_shape=[jax.ShapeDtypeStruct((9, unit), jnp.float32)]
+        if joined
+        else [
             jax.ShapeDtypeStruct((5, unit), jnp.float32),
             jax.ShapeDtypeStruct((4, wide), jnp.float32),
-        ),
+        ],
         in_specs=[HBM] * 5,
-        out_specs=(VMEM, VMEM),
+        out_specs=[VMEM] * (1 if joined else 2),
         scratch_shapes=[
             pltpu.VMEM(thermal_state_values.shape, jnp.float32),
             pltpu.VMEM(nodal_heating_input.shape, jnp.float32),
@@ -460,6 +500,7 @@
         compiler_params=PARAMS,
         name="pack",
     )(*map(in_hbm, (thermal_state_values, nodal_heating_input, thermal_kappa_values, frozen, label)))
+    held, edge_rows = packed_rows[0][:5], packed_rows[0][5:] if joined else packed_rows[1]
     high_edge, low_edge = edge_rows[:2], edge_rows[2:]
 
     brick_layers = edge_x // CPC
@@ -507,7 +548,7 @@
             out_shape=(
                 jax.ShapeDtypeStruct((edge_x, wide), jnp.float32),
                 jax.ShapeDtypeStruct((2, wide), jnp.float32),
-                jax.ShapeDtypeStruct((width, 3 * width), jnp.bfloat16),
+                jax.ShapeDtypeStruct((width, 5 * width), jnp.bfloat16),
                 jax.ShapeDtypeStruct((2 * depth, edge_x), jnp.float32),
             ),
             in_specs=[VMEM] * 3 + [HBM] * 3,
@@ -556,9 +597,10 @@
             extra = [lines(jnp.where(moves_on, onward, backward), unit)]
         elif rides:
             extra = [lines(onward, unit), lines(backward, unit)]
-        sent, got, at = exchanged(heat + extra, (1 << bit) | 1)
+        first_sent = packed_rows[0] if joined and 1 << bit == slabs else None
+        sent, got, at = exchanged(heat + extra, (1 << bit) | 1, first_sent)
         heat_rows = sum(part.shape[0] for part in heat)
-        heat = [sent[:heat_rows], got[:heat_rows]]
+        heat = heat + [got[:heat_rows]]
         parts = [got[row : row + part.shape[0]] for row, part in zip(at[len(at) - len(extra) :], extra)]
         if groups == 2 and 1 << bit == slabs:
             edges = parts[0].reshape(-1)[: 4 * wide].reshape(4, wide)
@@ -640,7 +682,17 @@
     else:
         covered = (edge_y + CPC - 2) // CPC + 1
     group_lanes = up_to((2 * covered + 1) * plane, 16)
-    weave = weave_table(group_lanes, plane, depth, edge_y, first_cell % CPC, wide)
+    if 5 * group_lanes > width:
+        group_lanes = 0
+    if isinstance(start_y, int):
+        first_lane = lambda: lax.rem(
+            lax.div(lax.axis_index("slab") * edge_y, CPC) * (2 * plane), width
+        )
+    else:
+        first_lane = lambda: 4 * plane
+    weave = weave_table(
+        group_lanes, width, plane, depth, edge_y, first_cell % CPC, first_lane(), wide
+    )
 
     def place(start, layer):
         if not isinstance(start, int):
@@ -655,12 +707,6 @@
     own_row = place(start_layer, own_layer)
     if direct:
         own_row = lambda: lax.axis_index("slab") * layers + 2
-    if isinstance(start_y, int):
-        first_lane = lambda: lax.rem(
-            width - (lax.axis_index("slab") * edge_y // CPC) * 2 * plane, width
-        )
-    else:
-        first_lane = lambda: width - 4 * plane
     new_shape = jax.ShapeDtypeStruct((2 * layers, flat), jnp.float32)
     solid_shape = jax.ShapeDtypeStruct((edge_x, wide), jnp.float32)
     span = max(width, wide)

time: 20.1 us -> 19.8 us (0.985)
  other arithmetic: 0.62 us -> 0.34 us
    unnamed x4 -> x0, other arithmetic: 0.38 us -> none
  transfers between devices with their start and end apart: 5 -> 5, of which waited for: 4 -> 4; matrix products, arithmetic and copies ran while one was open for 3% -> 1% of each run, Pallas kernels for 18% -> 18%
where the time goes in v6:
time: 19.8 us; the launch traced here: 19.5 us
  starting transfers between devices  9.17 us (46%)
  Pallas kernels  5.72 us (29%)
  waiting for transfers between devices  3.53 us (18%)
  between operations  0.76 us (4%)
  other arithmetic  0.34 us (2%)
    ppermute x5, starting transfers between devices, exchanged(): lax.ppermute(sent, AXES, [(i, i ^ flips) for i in range(devices)])  9.17 us
    ppermute x5, waiting for transfers between devices, exchanged(): lax.ppermute(sent, AXES, [(i, i ^ flips) for i in range(devices)])  3.53 us
    pallas_call x1, Pallas kernels, body(): pl.pallas_call(functools.partial(faces_kernel, depth, flat_cells), out_sh...  1.46 us
    pallas_call x1, Pallas kernels, body(): pl.pallas_call(functools.partial(finish_kernel, plane, depth, flat_cells,...  1.37 us
    pallas_call x1, Pallas kernels, sites(): pl.pallas_call(functools.partial(sites_kernel, flat_cells), out_shape=(ja...  1.23 us
    pallas_call x1, Pallas kernels, body(): pl.pallas_call(pack_kernel, out_shape=[jax.ShapeDtypeStruct((9, unit), jn...  0.85 us
    pallas_call x1, Pallas kernels, body(): pl.pallas_call(functools.partial(cells_kernel, depth, flat_cells), out_sh...  0.81 us
  transfers between devices with their start and end apart: 5, of which 4 were waited for; matrix products, arithmetic and copies ran while one was open for 1% of the time, Pallas kernels for 18%

profile of v6, /device:TPU:0, one launch (start us, length us, event | category | flops | bytes accessed | tf_op | source)
XLA Modules:
  0.0 19.5 jit_solution(6773614106590153570)
XLA Ops:
  0.6 0.8 %pack.1 = f32[9,128]{1,0:T(8,128)S(1)} custom-call(f32[2,128]{1,0:T(2,128)} %state_ref.1, f32[2,128]{1,0:T(2,128)} %heat_ref.1, f32[1,32]{1,0:T(1,128)} %kappa_ref.1, f32[128,128]{1,0:T(8,128)} %frozen_hbm.1, s32[128,128]{1,0:T(8,128)} %label_hbm.1), custom_call_target="tpu_custom_call" | custom-call | tf_op jit(solution)/shard_map/pack/pallas_call | solution.py:482
  1.5 2.4 %collective-permute-start = (f32[9,128]{1,0:T(8,128)S(1)}, f32[9,128]{1,0:T(8,128)S(1)}, u32[]{:S(2)}, u32[]{:S(2)}) collective-permute-start(f32[9,128]{1,0:T(8,128)S(1)} %pack.1), channel_id=1, source_target_pairs={{0,17},{1,16},{2,19},{3,18},{4,21},{5,20},{6,23},{7,22},{8,25},{9,... | collective-permute-start | bytes 13832 | tf_op jit(solution)/shard_map/ppermute | solution.py:473
  4.0 1.5 %faces.1 = (s32[32,128]{1,0:T(8,128)S(1)}, s32[128,128]{1,0:T(8,128)S(1)}, f32[128,128]{1,0:T(8,128)S(1)}, f32[32,128]{1,0:T(8,128)S(1)}) custom-call(s32[6,8000]{1,0:T(8,128)} %bitcast.3, s32[128,128]{1,0:T(8,128)} %label_hbm.1, f32[128,128]{1,0:T(8,128)} %frozen_hbm.1), custom_call_target="tpu_custom_call" | custom-call | tf_op jit(solution)/shard_map/faces/pallas_call | solution.py:512
  5.5 0.0 collective-permute-done
  5.6 2.9 %collective-permute-start.1 = (f32[26,128]{1,0:T(8,128)S(1)}, f32[26,128]{1,0:T(8,128)S(1)}, u32[]{:S(2)}, u32[]{:S(2)}) collective-permute-start(f32[26,128]{1,0:T(8,128)S(1)} %pad_add_fusion.3), channel_id=1, source_target_pairs={{0,9},{1,8},{2,11},{3,10},{4,13},{5,12},{6,15},{7,14},{8,1},{9,0},... | collective-permute-start | bytes 39944 | tf_op jit(solution)/shard_map/ppermute | solution.py:473
  8.5 0.8 %cells.1 = (f32[128,128]{1,0:T(8,128)S(1)}, f32[32,128]{1,0:T(8,128)S(1)}) custom-call(s32[32,128]{1,0:T(8,128)S(1)} %get-tuple-element.13.packed_ref, s32[128,128]{1,0:T(8,128)S(1)} %get-tuple-element.14.label_ref, f32[128,128]{1,0:T(8,128)S(1)} %get-tuple-element.15.frozen_ref, f32[32,128]{1,0:T(8,128)S(1)} %get-tuple-element.12.faces_ref), custom_call_target="tpu_custom_call" | custom-call | tf_op jit(solution)/shard_map/cells/pallas_call | solution.py:530
  9.3 0.6 %collective-permute-done.1 = f32[26,128]{1,0:T(8,128)S(1)} collective-permute-done((f32[26,128]{1,0:T(8,128)S(1)}, f32[26,128]{1,0:T(8,128)S(1)}, u32[]{:S(2)}, u32[]{:S(2)}) %collective-permute-start.1) | collective-permute-done | bytes 13344 | tf_op jit(solution)/shard_map/ppermute | solution.py:473
  10.0 1.7 %collective-permute-start.2 = (f32[36,128]{1,0:T(8,128)S(1)}, f32[36,128]{1,0:T(8,128)S(1)}, u32[]{:S(2)}, u32[]{:S(2)}) collective-permute-start(f32[36,128]{1,0:T(8,128)S(1)} %pad_add_fusion.2), channel_id=1, source_target_pairs={{0,5},{1,4},{2,7},{3,6},{4,1},{5,0},{6,3},{7,2},{8,13},{9,12},{10,... | collective-permute-start | bytes 55304 | tf_op jit(solution)/shard_map/ppermute | solution.py:473
  11.7 1.2 %sites.1 = (f32[128,128]{1,0:T(8,128)S(1)}, f32[2,128]{1,0:T(2,128)S(1)}, bf16[128,640]{1,0:T(8,128)(2,1)S(1)}, f32[32,128]{1,0:T(8,128)S(1)}) custom-call(s32[32,128]{1,0:T(8,128)S(1)} %get-tuple-element.13.packed_ref, f32[4,128]{1,0:T(4,128)S(1)} %slice.71.edge_ref, f32[32,128]{1,0:T(8,128)S(1)} %get-tuple-element.16.faces_ref, s32[2,128]{1,0:T(2,128)} %bitcast.4, ...), custom_call_target="tpu_custom_call" | custom-call | tf_op jit(solution)/shard_map/sites/pallas_call | solution.py:546
  12.9 0.3 %collective-permute-done.2 = f32[36,128]{1,0:T(8,128)S(1)} collective-permute-done((f32[36,128]{1,0:T(8,128)S(1)}, f32[36,128]{1,0:T(8,128)S(1)}, u32[]{:S(2)}, u32[]{:S(2)}) %collective-permute-start.2) | collective-permute-done | bytes 18464 | tf_op jit(solution)/shard_map/ppermute | solution.py:473
  13.3 1.6 %collective-permute-start.3 = (f32[72,128]{1,0:T(8,128)S(1)}, f32[72,128]{1,0:T(8,128)S(1)}, u32[]{:S(2)}, u32[]{:S(2)}) collective-permute-start(f32[72,128]{1,0:T(8,128)S(1)} %pad_add_fusion.1), channel_id=1, source_target_pairs={{0,3},{1,2},{2,1},{3,0},{4,7},{5,6},{6,5},{7,4},{8,11},{9,10},{10,... | collective-permute-start | bytes 110600 | tf_op jit(solution)/shard_map/ppermute | solution.py:473
  14.9 1.8 %collective-permute-done.3 = f32[72,128]{1,0:T(8,128)S(1)} collective-permute-done((f32[72,128]{1,0:T(8,128)S(1)}, f32[72,128]{1,0:T(8,128)S(1)}, u32[]{:S(2)}, u32[]{:S(2)}) %collective-permute-start.3) | collective-permute-done | bytes 36896 | tf_op jit(solution)/shard_map/ppermute | solution.py:473
  16.8 0.5 %collective-permute-start.4 = (f32[114,128]{1,0:T(8,128)S(1)}, f32[114,128]{1,0:T(8,128)S(1)}, u32[]{:S(2)}, u32[]{:S(2)}) collective-permute-start(f32[114,128]{1,0:T(8,128)S(1)} %pad_add_fusion.mine_ref), channel_id=1, source_target_pairs={{0,1},{1,0},{2,3},{3,2},{4,5},{5,4},{6,7},{7,6},{8,9},{9,8},{10,11... | collective-permute-start | bytes 175112 | tf_op jit(solution)/shard_map/ppermute | solution.py:473
  17.3 0.2 fusion.1.weave_ref
  17.4 0.7 %collective-permute-done.4.theirs_ref.across_ref.passing_ref.edge_ref = f32[114,128]{1,0:T(8,128)S(1)} collective-permute-done((f32[114,128]{1,0:T(8,128)S(1)}, f32[114,128]{1,0:T(8,128)S(1)}, u32[]{:S(2)}, u32[]{:S(2)}) %collective-permute-start.4) | collective-permute-done | bytes 58400 | tf_op jit(solution)/shard_map/ppermute | solution.py:473
  18.2 1.4 %finish.1 = (f32[2,128]{1,0:T(2,128)}, f32[128,128]{1,0:T(8,128)}) custom-call(f32[114,128]{1,0:T(8,128)S(1)} %pad_add_fusion.mine_ref, f32[114,128]{1,0:T(8,128)S(1)} %collective-permute-done.4.theirs_ref.across_ref.passing_ref.edge_ref, f32[114,128]{1,0:T(8,128)S(1)} %collective-permute-done.4.theirs_ref.across_ref.passing_ref.edge_ref, ...), custom_call_target="tpu_custom_call" | custom-call | tf_op jit(solution)/shard_map/finish/pallas_call | solution.py:713
  (22 shorter events, 0.2 us)
Async XLA Ops:
  1.5 4.1 %collective-permute-start = (f32[9,128]{1,0:T(8,128)S(1)}, f32[9,128]{1,0:T(8,128)S(1)}, u32[]{:S(2)}, u32[]{:S(2)}) collective-permute-start(f32[9,128]{1,0:T(8,128)S(1)} %pack.1), channel_id=1, source_target_pairs={{0,17},{1,16},{2,19},{3,18},{4,21},{5,20},{6,23},{7,22},{8,25},{9,... | collective-permute-start | bytes 13832 | tf_op jit(solution)/shard_map/ppermute | solution.py:473
  5.6 4.4 %collective-permute-start.1 = (f32[26,128]{1,0:T(8,128)S(1)}, f32[26,128]{1,0:T(8,128)S(1)}, u32[]{:S(2)}, u32[]{:S(2)}) collective-permute-start(f32[26,128]{1,0:T(8,128)S(1)} %pad_add_fusion.3), channel_id=1, source_target_pairs={{0,9},{1,8},{2,11},{3,10},{4,13},{5,12},{6,15},{7,14},{8,1},{9,0},... | collective-permute-start | bytes 39944 | tf_op jit(solution)/shard_map/ppermute | solution.py:473
  10.0 3.3 %collective-permute-start.2 = (f32[36,128]{1,0:T(8,128)S(1)}, f32[36,128]{1,0:T(8,128)S(1)}, u32[]{:S(2)}, u32[]{:S(2)}) collective-permute-start(f32[36,128]{1,0:T(8,128)S(1)} %pad_add_fusion.2), channel_id=1, source_target_pairs={{0,5},{1,4},{2,7},{3,6},{4,1},{5,0},{6,3},{7,2},{8,13},{9,12},{10,... | collective-permute-start | bytes 55304 | tf_op jit(solution)/shard_map/ppermute | solution.py:473
  13.3 3.4 %collective-permute-start.3 = (f32[72,128]{1,0:T(8,128)S(1)}, f32[72,128]{1,0:T(8,128)S(1)}, u32[]{:S(2)}, u32[]{:S(2)}) collective-permute-start(f32[72,128]{1,0:T(8,128)S(1)} %pad_add_fusion.1), channel_id=1, source_target_pairs={{0,3},{1,2},{2,1},{3,0},{4,7},{5,6},{6,5},{7,4},{8,11},{9,10},{10,... | collective-permute-start | bytes 110600 | tf_op jit(solution)/shard_map/ppermute | solution.py:473
  16.8 1.4 %collective-permute-start.4 = (f32[114,128]{1,0:T(8,128)S(1)}, f32[114,128]{1,0:T(8,128)S(1)}, u32[]{:S(2)}, u32[]{:S(2)}) collective-permute-start(f32[114,128]{1,0:T(8,128)S(1)} %pad_add_fusion.mine_ref), channel_id=1, source_target_pairs={{0,1},{1,0},{2,3},{3,2},{4,5},{5,4},{6,7},{7,6},{8,9},{9,8},{10,11... | collective-permute-start | bytes 175112 | tf_op jit(solution)/shard_map/ppermute | solution.py:473

commit v7 on v6

--- a/solution.py
+++ b/solution.py
@@ -98,34 +98,53 @@
 
 def faces_kernel(
     depth, flat, table_hbm, label_hbm, frozen_hbm,
-    packed_ref, label_ref, frozen_ref, faces_ref, line_ref, table_ref, sems,
+    packed_ref, label_ref, frozen_ref, faces_ref, table_ref, sems,
 ):
-    get_table, get_label, get_frozen = started(
-        [(table_hbm, table_ref), (label_hbm, label_ref), (frozen_hbm, frozen_ref)], sems
-    )
     count = table_ref.shape[1]
     half = packed_ref.shape[0]
     edge_x = frozen_ref.shape[0]
-    place = lax.broadcasted_iota(jnp.int32, table_ref.shape, 0)
-    line_ref[...] = jnp.zeros(line_ref.shape, jnp.int32)
+    chunk = up_to(half, 4) // 4 * LANES
+    order = [at for low in range(0, half * LANES, chunk) for at in (low, low + half * LANES)]
+    order = [at for at in order if at < count]
+    parts = [pl.ds(at, min(chunk, count - at)) for at in order]
+    get_label, get_frozen, *get_table = started(
+        [(label_hbm, label_ref), (frozen_hbm, frozen_ref)]
+        + [(table_hbm.at[:, part], table_ref.at[:, part]) for part in parts],
+        sems,
+    )
     get_label.wait()
     get_frozen.wait()
     label = jnp.transpose(label_ref[...])
     label = jnp.concatenate([label[0:depth], label[flat - depth : flat]], 0)
     frozen = jnp.transpose(frozen_ref[...])
     frozen = 0.25 * jnp.concatenate([frozen[0:depth], frozen[flat - depth : flat]], 0)
-    get_table.wait()
-    word = jnp.sum((table_ref[...] - 1) << (2 * place), axis=0, keepdims=True)
-    line_ref[0:1, 0:count] = word
+    directions = table_ref.shape[0]
+    place = 2 * lax.broadcasted_iota(jnp.int32, (directions, LANES), 0)
+
+    def tile(number):
+        size = max(min(LANES, count - number * LANES), 0)
+        here = table_ref[:, number * LANES : number * LANES + size] if size else None
+        if size == LANES:
+            return here
+        blank = jnp.ones((directions, LANES - size), jnp.int32)
+        return jnp.concatenate([here, blank], 1) if size else blank
+
+    waiting = dict(zip(order, get_table))
     for r in range(half):
-        low = line_ref[0:1, r * LANES : (r + 1) * LANES]
-        high = line_ref[0:1, (r + half) * LANES : (r + half + 1) * LANES]
-        packed_ref[r : r + 1, :] = low | (high << 12)
-    for t in range(edge_x // LANES):
-        lanes = slice(t * LANES, (t + 1) * LANES)
+        for at in (r * LANES, (r + half) * LANES):
+            if at in waiting:
+                waiting.pop(at).wait()
+        bits = ((tile(r) - 1) << place) | ((tile(r + half) - 1) << (place + 12))
+        packed_ref[r : r + 1, :] = jnp.sum(bits, axis=0, keepdims=True)
+    short = -edge_x % LANES
+    if short:
+        label = jnp.concatenate([label, jnp.zeros((2 * depth, short), jnp.int32)], 1)
+    for t in range(up_to(edge_x, LANES) // LANES):
+        size = min(LANES, edge_x - t * LANES)
+        lanes = slice(t * LANES, t * LANES + size)
         for part in range(2 * depth // 8):
             rows = slice(part * 8, part * 8 + 8)
-            code = pick_codes(packed_ref, label[rows, lanes])
+            code = pick_codes(packed_ref, label[rows, t * LANES : (t + 1) * LANES])[:, :size]
             faces_ref[rows, lanes] = frozen[rows, lanes] * level(code, 2 if part * 8 < depth else 3)
 
 
@@ -318,13 +337,20 @@
     edge_x, wide = frozen_ref.shape
     _, all_rows, width = state_ref.shape
     rows = even_ref.shape[0]
-    heat_rows, across_row, passing_row, edge_row, devices = sizes
+    heat_rows, across_row, passing_row, edge_row = sizes
     core = lax.axis_index("slab") & 1
     if heat_rows:
-        me = lax.axis_index("grp") * lax.axis_size("slab") + lax.axis_index("slab")
-        for p, off in enumerate(arrival_order(devices)):
-            source, block = (mine_ref, p) if p < devices // 2 else (theirs_ref, p - devices // 2)
-            row = lax.rem((me ^ off) * layers + (all_rows - first_layer()), all_rows)
+        slabs = lax.axis_size("slab")
+        me = lax.axis_index("grp") * slabs + lax.axis_index("slab")
+        state_ref[:, rows - 8 : rows, :] = jnp.zeros((5, 8, width), jnp.float32)
+        numbers = [me ^ off for off in arrival_order(slabs)[: slabs // 2]]
+        numbers += beyond_order(me, slabs)
+        numbers += [me ^ 1 ^ off for off in arrival_order(slabs)[: slabs // 2]]
+        numbers += beyond_order(me ^ 1, slabs)
+        blocks = len(numbers) // 2
+        for p, number in enumerate(numbers):
+            source, block = (mine_ref, p) if p < blocks else (theirs_ref, p - blocks)
+            row = lax.rem(number * layers + (all_rows - first_layer()), all_rows)
             for c in range(5):
                 for layer in range(layers):
                     state_ref[c, pl.ds(row + layer, 1), :] = source[
@@ -424,6 +450,27 @@
     return jnp.where((copy < 5) & (cell < edge_y * depth), part, 0.0).astype(jnp.bfloat16)
 
 
+def beyond_order(me, slabs):
+    top = slabs.bit_length() - 2
+
+    def kept(number, bit):
+        if bit > top:
+            return [number ^ slabs ^ 1]
+        flips = (1 << bit) | 1
+        if bit == 1:
+            return kept(number, 2) + kept(number ^ flips, 2)
+        return [picked(number, bit), picked(number ^ flips, bit)]
+
+    def picked(number, bit):
+        held = kept(number, bit + 1)
+        if len(held) == 1:
+            return held[0]
+        same = ((number >> bit) ^ (number >> (bit + 1))) & 1 == 0
+        return jnp.where(same, held[0], held[1])
+
+    return kept(me, 1)
+
+
 def arrival_order(devices):
     offs = [0]
     for bit in reversed(range(1, devices.bit_length() - 1)):
@@ -508,6 +555,9 @@
     width = up_to(need_y * 2 * plane, LANES)
     if 2 * width > flat:
         width = flat
+    need_layers = brick_layers + 5
+    whole = width == flat and 2 * up_to(need_layers, 8) > all_layers
+    direct = whole and edge_x == unit and wide == unit and groups == 2 and slabs > 2
     table_lanes = up_to(count, 2 * LANES)
     packed, label, frozen, faces = pl.pallas_call(
         functools.partial(faces_kernel, depth, flat_cells),
@@ -520,9 +570,8 @@
         in_specs=[HBM] * 3,
         out_specs=[VMEM] * 4,
         scratch_shapes=[
-            pltpu.VMEM((8, table_lanes), jnp.int32),
             pltpu.VMEM((growth_reach_table.shape[1], count), jnp.int32),
-            pltpu.SemaphoreType.DMA((3,)),
+            pltpu.SemaphoreType.DMA((10,)),
         ],
         compiler_params=PARAMS,
         name="faces",
@@ -576,6 +625,7 @@
 
     onward, backward = packets(faces)
     heat, edges = [held], None
+    beyond = []
     if groups > 2:
         ring = [(i, (i + 1) % groups) for i in range(groups)]
         edges = jnp.concatenate(
@@ -598,9 +648,18 @@
         elif rides:
             extra = [lines(onward, unit), lines(backward, unit)]
         first_sent = packed_rows[0] if joined and 1 << bit == slabs else None
-        sent, got, at = exchanged(heat + extra, (1 << bit) | 1, first_sent)
+        if bit > 1 and len(beyond) == 2:
+            same = ((me >> bit) ^ (me >> (bit + 1))) & 1 == 0
+            beyond = [jnp.where(same, *beyond)]
+        sent, got, at = exchanged(heat + beyond + extra, (1 << bit) | 1, first_sent)
         heat_rows = sum(part.shape[0] for part in heat)
-        heat = heat + [got[:heat_rows]]
+        if direct and 1 << bit == slabs:
+            beyond = [got[:heat_rows]]
+        else:
+            beyond = beyond + [
+                got[row : row + part.shape[0]] for row, part in zip(at[len(heat) :], beyond)
+            ]
+            heat = heat + [got[:heat_rows]]
         parts = [got[row : row + part.shape[0]] for row, part in zip(at[len(at) - len(extra) :], extra)]
         if groups == 2 and 1 << bit == slabs:
             edges = parts[0].reshape(-1)[: 4 * wide].reshape(4, wide)
@@ -621,21 +680,18 @@
     if groups == 2:
         extra.append(lines(ends, unit))
     kept = jnp.where(core == 0, onward, backward)
+    heat = heat + beyond
     sent, got, at = exchanged(heat + extra, 1)
     heat_rows = sum(part.shape[0] for part in heat)
     at = at[len(heat) :]
     across, passing = (as_face(got[row : row + part.shape[0]]) for row, part in zip(at, extra[:2]))
     if groups == 2:
         ends = got[at[2] : at[2] + extra[2].shape[0]].reshape(-1)[: 2 * wide].reshape(2, wide)
-    brick_layers = edge_x // CPC
     first_cell = slab * edge_y
     first_element = first_cell // CPC
-    need_layers = brick_layers + 5
-    whole = width == flat and 2 * up_to(need_layers, 8) > all_layers
-    direct = whole and edge_x == unit and wide == unit and groups == 2
     if direct:
         inputs = (sent, got, got, got, got)
-        sizes = (heat_rows, *at, devices)
+        sizes = (heat_rows, *at)
         start_layer, start_y = group * brick_layers - 2, 0
         rows = min(up_to(need_layers, 8), all_layers)
     else:
@@ -675,7 +731,7 @@
             group * brick_layers - 2, need_layers, first_element - 2, need_y
         )
         inputs = (state, state, across, passing, ends)
-        sizes = (0, 0, 0, 0, devices)
+        sizes = (0, 0, 0, 0)
         rows = state.shape[1]
     if edge_y % CPC == 0 or CPC % edge_y == 0:
         covered = max(edge_y // CPC, 1)

time: 19.8 us -> 19.6 us (0.990)
  no operation moved by 1% of the time
where the time goes in v7:
time: 19.6 us; the launch traced here: 19.4 us
  starting transfers between devices  9.15 us (47%)
  Pallas kernels  5.63 us (29%)
  waiting for transfers between devices  3.47 us (18%)
  between operations  0.77 us (4%)
  other arithmetic  0.35 us (2%)
    ppermute x5, starting transfers between devices, exchanged(): lax.ppermute(sent, AXES, [(i, i ^ flips) for i in range(devices)])  9.15 us
    ppermute x5, waiting for transfers between devices, exchanged(): lax.ppermute(sent, AXES, [(i, i ^ flips) for i in range(devices)])  3.47 us
    pallas_call x1, Pallas kernels, body(): pl.pallas_call(functools.partial(finish_kernel, plane, depth, flat_cells,...  1.38 us
    pallas_call x1, Pallas kernels, body(): pl.pallas_call(functools.partial(faces_kernel, depth, flat_cells), out_sh...  1.36 us
    pallas_call x1, Pallas kernels, sites(): pl.pallas_call(functools.partial(sites_kernel, flat_cells), out_shape=(ja...  1.24 us
    pallas_call x1, Pallas kernels, body(): pl.pallas_call(pack_kernel, out_shape=[jax.ShapeDtypeStruct((9, unit), jn...  0.85 us
    pallas_call x1, Pallas kernels, body(): pl.pallas_call(functools.partial(cells_kernel, depth, flat_cells), out_sh...  0.81 us
  transfers between devices with their start and end apart: 5, of which 4 were waited for; matrix products, arithmetic and copies ran while one was open for 1% of the time, Pallas kernels for 18%

profile of v7, /device:TPU:0, one launch (start us, length us, event | category | flops | bytes accessed | tf_op | source)
XLA Modules:
  0.0 19.4 jit_solution(12659325634593990991)
XLA Ops:
  0.6 0.8 %pack.1 = f32[9,128]{1,0:T(8,128)S(1)} custom-call(f32[2,128]{1,0:T(2,128)} %state_ref.1, f32[2,128]{1,0:T(2,128)} %heat_ref.1, f32[1,32]{1,0:T(1,128)} %kappa_ref.1, f32[128,128]{1,0:T(8,128)} %frozen_hbm.1, s32[128,128]{1,0:T(8,128)} %label_hbm.1), custom_call_target="tpu_custom_call" | custom-call | tf_op jit(solution)/shard_map/pack/pallas_call | solution.py:529
  1.5 2.4 %collective-permute-start = (f32[9,128]{1,0:T(8,128)S(1)}, f32[9,128]{1,0:T(8,128)S(1)}, u32[]{:S(2)}, u32[]{:S(2)}) collective-permute-start(f32[9,128]{1,0:T(8,128)S(1)} %pack.1), channel_id=1, source_target_pairs={{0,17},{1,16},{2,19},{3,18},{4,21},{5,20},{6,23},{7,22},{8,25},{9,... | collective-permute-start | bytes 13832 | tf_op jit(solution)/shard_map/ppermute | solution.py:520
  4.0 1.4 %faces.1 = (s32[32,128]{1,0:T(8,128)S(1)}, s32[128,128]{1,0:T(8,128)S(1)}, f32[128,128]{1,0:T(8,128)S(1)}, f32[32,128]{1,0:T(8,128)S(1)}) custom-call(s32[6,8000]{1,0:T(8,128)} %bitcast.3, s32[128,128]{1,0:T(8,128)} %label_hbm.1, f32[128,128]{1,0:T(8,128)} %frozen_hbm.1), custom_call_target="tpu_custom_call" | custom-call | tf_op jit(solution)/shard_map/faces/pallas_call | solution.py:562
  5.4 0.0 collective-permute-done
  5.5 3.0 %collective-permute-start.1 = (f32[26,128]{1,0:T(8,128)S(1)}, f32[26,128]{1,0:T(8,128)S(1)}, u32[]{:S(2)}, u32[]{:S(2)}) collective-permute-start(f32[26,128]{1,0:T(8,128)S(1)} %pad_add_fusion.3), channel_id=1, source_target_pairs={{0,9},{1,8},{2,11},{3,10},{4,13},{5,12},{6,15},{7,14},{8,1},{9,0},... | collective-permute-start | bytes 39944 | tf_op jit(solution)/shard_map/ppermute | solution.py:520
  8.5 0.8 %cells.1 = (f32[128,128]{1,0:T(8,128)S(1)}, f32[32,128]{1,0:T(8,128)S(1)}) custom-call(s32[32,128]{1,0:T(8,128)S(1)} %get-tuple-element.13.packed_ref, s32[128,128]{1,0:T(8,128)S(1)} %get-tuple-element.14.label_ref, f32[128,128]{1,0:T(8,128)S(1)} %get-tuple-element.15.frozen_ref, f32[32,128]{1,0:T(8,128)S(1)} %get-tuple-element.12.faces_ref), custom_call_target="tpu_custom_call" | custom-call | tf_op jit(solution)/shard_map/cells/pallas_call | solution.py:579
  9.3 0.6 %collective-permute-done.1 = f32[26,128]{1,0:T(8,128)S(1)} collective-permute-done((f32[26,128]{1,0:T(8,128)S(1)}, f32[26,128]{1,0:T(8,128)S(1)}, u32[]{:S(2)}, u32[]{:S(2)}) %collective-permute-start.1) | collective-permute-done | bytes 13344 | tf_op jit(solution)/shard_map/ppermute | solution.py:520
  10.0 1.7 %collective-permute-start.2 = (f32[31,128]{1,0:T(8,128)S(1)}, f32[31,128]{1,0:T(8,128)S(1)}, u32[]{:S(2)}, u32[]{:S(2)}) collective-permute-start(f32[31,128]{1,0:T(8,128)S(1)} %pad_add_fusion.2), channel_id=1, source_target_pairs={{0,5},{1,4},{2,7},{3,6},{4,1},{5,0},{6,3},{7,2},{8,13},{9,12},{10,... | collective-permute-start | bytes 47624 | tf_op jit(solution)/shard_map/ppermute | solution.py:520
  11.7 1.2 %sites.1 = (f32[128,128]{1,0:T(8,128)S(1)}, f32[2,128]{1,0:T(2,128)S(1)}, bf16[128,640]{1,0:T(8,128)(2,1)S(1)}, f32[32,128]{1,0:T(8,128)S(1)}) custom-call(s32[32,128]{1,0:T(8,128)S(1)} %get-tuple-element.13.packed_ref, f32[4,128]{1,0:T(4,128)S(1)} %slice.91.edge_ref, f32[32,128]{1,0:T(8,128)S(1)} %get-tuple-element.16.faces_ref, s32[2,128]{1,0:T(2,128)} %bitcast.4, ...), custom_call_target="tpu_custom_call" | custom-call | tf_op jit(solution)/shard_map/sites/pallas_call | solution.py:595
  12.9 0.3 %collective-permute-done.2 = f32[31,128]{1,0:T(8,128)S(1)} collective-permute-done((f32[31,128]{1,0:T(8,128)S(1)}, f32[31,128]{1,0:T(8,128)S(1)}, u32[]{:S(2)}, u32[]{:S(2)}) %collective-permute-start.2) | collective-permute-done | bytes 15904 | tf_op jit(solution)/shard_map/ppermute | solution.py:520
  13.3 1.6 %collective-permute-start.3 = (f32[62,128]{1,0:T(8,128)S(1)}, f32[62,128]{1,0:T(8,128)S(1)}, u32[]{:S(2)}, u32[]{:S(2)}) collective-permute-start(f32[62,128]{1,0:T(8,128)S(1)} %pad_add_fusion.1), channel_id=1, source_target_pairs={{0,3},{1,2},{2,1},{3,0},{4,7},{5,6},{6,5},{7,4},{8,11},{9,10},{10,... | collective-permute-start | bytes 95240 | tf_op jit(solution)/shard_map/ppermute | solution.py:520
  14.9 1.8 %collective-permute-done.3 = f32[62,128]{1,0:T(8,128)S(1)} collective-permute-done((f32[62,128]{1,0:T(8,128)S(1)}, f32[62,128]{1,0:T(8,128)S(1)}, u32[]{:S(2)}, u32[]{:S(2)}) %collective-permute-start.3) | collective-permute-done | bytes 31776 | tf_op jit(solution)/shard_map/ppermute | solution.py:520
  16.7 0.4 %collective-permute-start.4 = (f32[94,128]{1,0:T(8,128)S(1)}, f32[94,128]{1,0:T(8,128)S(1)}, u32[]{:S(2)}, u32[]{:S(2)}) collective-permute-start(f32[94,128]{1,0:T(8,128)S(1)} %pad_add_fusion.mine_ref), channel_id=1, source_target_pairs={{0,1},{1,0},{2,3},{3,2},{4,5},{5,4},{6,7},{7,6},{8,9},{9,8},{10,11... | collective-permute-start | bytes 144392 | tf_op jit(solution)/shard_map/ppermute | solution.py:520
  17.1 0.2 fusion.1.weave_ref
  17.3 0.7 %collective-permute-done.4.theirs_ref.across_ref.passing_ref.edge_ref = f32[94,128]{1,0:T(8,128)S(1)} collective-permute-done((f32[94,128]{1,0:T(8,128)S(1)}, f32[94,128]{1,0:T(8,128)S(1)}, u32[]{:S(2)}, u32[]{:S(2)}) %collective-permute-start.4) | collective-permute-done | bytes 48160 | tf_op jit(solution)/shard_map/ppermute | solution.py:520
  18.0 1.4 %finish.1 = (f32[2,128]{1,0:T(2,128)}, f32[128,128]{1,0:T(8,128)}) custom-call(f32[94,128]{1,0:T(8,128)S(1)} %pad_add_fusion.mine_ref, f32[94,128]{1,0:T(8,128)S(1)} %collective-permute-done.4.theirs_ref.across_ref.passing_ref.edge_ref, f32[94,128]{1,0:T(8,128)S(1)} %collective-permute-done.4.theirs_ref.across_ref.passing_ref.edge_ref, ...), custom_call_target="tpu_custom_call" | custom-call | tf_op jit(solution)/shard_map/finish/pallas_call | solution.py:769
  (24 shorter events, 0.2 us)
Async XLA Ops:
  1.5 4.0 %collective-permute-start = (f32[9,128]{1,0:T(8,128)S(1)}, f32[9,128]{1,0:T(8,128)S(1)}, u32[]{:S(2)}, u32[]{:S(2)}) collective-permute-start(f32[9,128]{1,0:T(8,128)S(1)} %pack.1), channel_id=1, source_target_pairs={{0,17},{1,16},{2,19},{3,18},{4,21},{5,20},{6,23},{7,22},{8,25},{9,... | collective-permute-start | bytes 13832 | tf_op jit(solution)/shard_map/ppermute | solution.py:520
  5.5 4.5 %collective-permute-start.1 = (f32[26,128]{1,0:T(8,128)S(1)}, f32[26,128]{1,0:T(8,128)S(1)}, u32[]{:S(2)}, u32[]{:S(2)}) collective-permute-start(f32[26,128]{1,0:T(8,128)S(1)} %pad_add_fusion.3), channel_id=1, source_target_pairs={{0,9},{1,8},{2,11},{3,10},{4,13},{5,12},{6,15},{7,14},{8,1},{9,0},... | collective-permute-start | bytes 39944 | tf_op jit(solution)/shard_map/ppermute | solution.py:520
  10.0 3.2 %collective-permute-start.2 = (f32[31,128]{1,0:T(8,128)S(1)}, f32[31,128]{1,0:T(8,128)S(1)}, u32[]{:S(2)}, u32[]{:S(2)}) collective-permute-start(f32[31,128]{1,0:T(8,128)S(1)} %pad_add_fusion.2), channel_id=1, source_target_pairs={{0,5},{1,4},{2,7},{3,6},{4,1},{5,0},{6,3},{7,2},{8,13},{9,12},{10,... | collective-permute-start | bytes 47624 | tf_op jit(solution)/shard_map/ppermute | solution.py:520
  13.3 3.4 %collective-permute-start.3 = (f32[62,128]{1,0:T(8,128)S(1)}, f32[62,128]{1,0:T(8,128)S(1)}, u32[]{:S(2)}, u32[]{:S(2)}) collective-permute-start(f32[62,128]{1,0:T(8,128)S(1)} %pad_add_fusion.1), channel_id=1, source_target_pairs={{0,3},{1,2},{2,1},{3,0},{4,7},{5,6},{6,5},{7,4},{8,11},{9,10},{10,... | collective-permute-start | bytes 95240 | tf_op jit(solution)/shard_map/ppermute | solution.py:520
  16.7 1.3 %collective-permute-start.4 = (f32[94,128]{1,0:T(8,128)S(1)}, f32[94,128]{1,0:T(8,128)S(1)}, u32[]{:S(2)}, u32[]{:S(2)}) collective-permute-start(f32[94,128]{1,0:T(8,128)S(1)} %pad_add_fusion.mine_ref), channel_id=1, source_target_pairs={{0,1},{1,0},{2,3},{3,2},{4,5},{5,4},{6,7},{7,6},{8,9},{9,8},{10,11... | collective-permute-start | bytes 144392 | tf_op jit(solution)/shard_map/ppermute | solution.py:520

commit v8 on v7

--- a/solution.py
+++ b/solution.py
@@ -33,6 +33,19 @@
         return value >> (by.bit_length() - 1), value & (by - 1)
     quotient = lax.div(value, jnp.full_like(value, by))
     return quotient, value - quotient * by
+
+
+def pieces(values):
+    out = []
+    for _ in range(3):
+        out.append(values.astype(jnp.bfloat16).astype(jnp.float32))
+        values = values - out[-1]
+    return out
+
+
+def side_by_side(values, lanes):
+    first, second, third = pieces(values)
+    return first + pltpu.roll(second, lanes, 1) + pltpu.roll(third, 2 * lanes, 1)
 
 
 def pack_kernel(
@@ -56,8 +69,7 @@
         ],
         sems,
     )
-    held_ref[4:5, :] = jnp.zeros((1, held_ref.shape[1]), jnp.float32)
-    for copy in copies:
+    for copy in copies[:3]:
         copy.wait()
     for layer in range(layers):
         lanes = slice(layer * flat, (layer + 1) * flat)
@@ -65,7 +77,11 @@
             row = slice(2 * layer + parity, 2 * layer + parity + 1)
             held_ref[parity : parity + 1, lanes] = state[row, :]
             held_ref[2 + parity : 3 + parity, lanes] = heat[row, :]
-        held_ref[4:5, layer * flat : layer * flat + elements] = kappa[layer : layer + 1, :]
+        wide = jnp.broadcast_to(kappa[layer : layer + 1, :], (8, elements))
+        wide = jnp.concatenate([wide, jnp.zeros((8, flat - elements), jnp.float32)], 1)
+        held_ref[4:5, lanes] = side_by_side(wide, elements)[0:1]
+    for copy in copies[3:]:
+        copy.wait()
     edge_ref[0:1, :] = frozen[1, 7:8, :]
     edge_ref[1:2, :] = label[1, 7:8, :].astype(jnp.float32)
     edge_ref[2:3, :] = frozen[0, 0:1, :]
@@ -241,14 +257,6 @@
     return out
 
 
-def pieces(values):
-    out = []
-    for _ in range(3):
-        out.append(values.astype(jnp.bfloat16).astype(jnp.float32))
-        values = values - out[-1]
-    return out
-
-
 def advance(plane, even, odd, heat_even, heat_odd, kappa, spread):
     rows, width = even.shape
     up = lambda v: pltpu.roll(v, rows - 1, 0)
@@ -257,9 +265,7 @@
     lane = lax.broadcasted_iota(jnp.int32, (rows, width), 1)
     row_y, deep = split_index(lane, plane)
     even_y, even_z = row_y & 1 == 0, deep & 1 == 0
-    first, second, third = pieces(kappa)
-    joined = first + turn(second, width // 4) + turn(third, 2 * (width // 4))
-    lines = jnp.dot(joined.astype(jnp.bfloat16), spread, preferred_element_type=jnp.float32)
+    lines = jnp.dot(kappa.astype(jnp.bfloat16), spread, preferred_element_type=jnp.float32)
     lines = lines * (STEP / 108.0)
     along_x, *others = (lines[:, i * width : (i + 1) * width] for i in range(5))
     behind_x = down(along_x)
@@ -310,7 +316,9 @@
 
 
 def heat_kernel(plane, layers, first_row, state_ref, spread_ref, new_ref, even_ref, odd_ref):
-    even, odd = advance(plane, *(state_ref[i] for i in range(5)), spread_ref[...])
+    state = [state_ref[i] for i in range(5)]
+    state[4] = side_by_side(state[4], state[4].shape[1] // 4)
+    even, odd = advance(plane, *state, spread_ref[...])
     even_ref[...] = even
     odd_ref[...] = odd
     start = first_row()
@@ -329,8 +337,8 @@
 
 
 def finish_kernel(
-    plane, depth, flat, layers, group_lanes, sizes, first_layer, first_row, cell_row, first_lane,
-    wraps, mine_ref, theirs_ref, across_ref, passing_ref, edge_ref, kept_ref, spread_ref, weave_ref,
+    plane, depth, flat, layers, sizes, first_layer, first_row, cell_row, wraps,
+    mine_ref, theirs_ref, across_ref, passing_ref, edge_ref, kept_ref, spread_ref, weave_ref,
     packed_ref, gathered_ref, nucleation_ref, frozen_ref, *refs,
 ):
     solid_out, state_ref, even_ref, odd_ref, side_ref, extra_ref, solid_ref, new_ref, sems = refs[-9:]
@@ -359,6 +367,7 @@
         state = [state_ref[i, 0:rows, :] for i in range(5)]
     else:
         state = [mine_ref[i] for i in range(5)]
+        state[4] = side_by_side(state[4], width // 4)
     side_ref[...] = jnp.zeros(side_ref.shape, jnp.float32)
     there = jnp.where(core == 0, 0, flat - depth)
     side_ref[pl.ds(pl.multiple_of(there, 8), depth), :] = (
@@ -381,20 +390,13 @@
         new_copy = pltpu.make_async_copy(new_ref, refs[0], sems.at[CHUNKS])
         new_copy.start()
     both = jnp.concatenate([even, odd], 0)
-    if group_lanes:
-        lane = lax.broadcasted_iota(jnp.int32, both.shape, 1)
-        first_node = first_lane()
-        inside = (lane >= first_node) & (lane < first_node + group_lanes)
-        inside |= lane + width < first_node + group_lanes
-        first, second, third = pieces(jnp.where(inside, both, 0.0))
-        joined = first
-        for i, piece in enumerate((second, third, first, second)):
-            joined = joined + pltpu.roll(piece, (i + 1) * group_lanes, 1)
-    else:
-        first, second, third = pieces(both)
-        joined = jnp.concatenate([first, second, third, first, second], 1)
+    first, second, third = pieces(both)
+    joined = jnp.concatenate([first, second, third, first, second], 1)
+    high, low = weave_ref[0:width, :], weave_ref[width : 2 * width, :]
     woven = jnp.dot(
-        joined.astype(jnp.bfloat16), weave_ref[...], preferred_element_type=jnp.float32
+        joined.astype(jnp.bfloat16),
+        jnp.concatenate([high, high, high, low, low], 0),
+        preferred_element_type=jnp.float32,
     )
     even_ref[:, 0:wide] = woven[:rows]
     odd_ref[:, 0:wide] = woven[rows:]
@@ -431,23 +433,17 @@
         new_copy.wait()
 
 
-def weave_table(group_lanes, width, plane, depth, edge_y, first_step, first_node, wide):
-    span = group_lanes or width
-    row = jnp.arange(width if group_lanes else 5 * width)[:, None]
-    cell = jnp.arange(wide)[None, :]
-    if group_lanes:
-        row = (row - first_node) % width
-        copy, node = row // span, row % span
-    else:
-        copy, node = row // span, (row % span - first_node) % width
+def weave_table(width, plane, depth, edge_y, first_step, first_node, wide):
+    row, cell = jnp.arange(2 * width)[:, None], jnp.arange(wide)[None, :]
+    node = (row - first_node) % width
     cell_y, cell_z = first_step + cell // depth, cell % depth
     step_y = node // plane - 2 * (cell_y // CPC)
     step_z = (node % plane - 2 * (cell_z // CPC)) % plane
     take = lambda step, at: sum(jnp.where(step == i, v, 0.0) for i, v in enumerate(basis(at % CPC)))
     full = take(step_y, cell_y) * take(step_z, cell_z)
     high = jnp.floor(full * 128.0) * (1.0 / 128.0)
-    part = jnp.where(copy < 3, high, full - high)
-    return jnp.where((copy < 5) & (cell < edge_y * depth), part, 0.0).astype(jnp.bfloat16)
+    part = jnp.where(row < width, high, full - high)
+    return jnp.where(cell < edge_y * depth, part, 0.0).astype(jnp.bfloat16)
 
 
 def beyond_order(me, slabs):
@@ -699,6 +695,8 @@
         blocks = jnp.concatenate([sent[:heat_rows], got[:heat_rows]], 0).reshape(devices, 5, layers, flat)
         blocks = jnp.take(blocks, jnp.asarray(order)[jnp.arange(devices) ^ me], axis=0)
         held = jnp.moveaxis(blocks, 1, 0).reshape(5, all_layers, flat)
+        kappa = sum(held[4:, :, i * elements : (i + 1) * elements] for i in range(3))
+        held = jnp.concatenate([held[:4], jnp.pad(kappa, ((0, 0), (0, 0), (0, flat - elements)))])
 
         def window(first_layer, need_layers, first_element, need_elements):
             rows, lanes = up_to(need_layers, 8), up_to(need_elements * 2 * plane, LANES)
@@ -733,22 +731,13 @@
         inputs = (state, state, across, passing, ends)
         sizes = (0, 0, 0, 0)
         rows = state.shape[1]
-    if edge_y % CPC == 0 or CPC % edge_y == 0:
-        covered = max(edge_y // CPC, 1)
-    else:
-        covered = (edge_y + CPC - 2) // CPC + 1
-    group_lanes = up_to((2 * covered + 1) * plane, 16)
-    if 5 * group_lanes > width:
-        group_lanes = 0
     if isinstance(start_y, int):
         first_lane = lambda: lax.rem(
             lax.div(lax.axis_index("slab") * edge_y, CPC) * (2 * plane), width
         )
     else:
         first_lane = lambda: 4 * plane
-    weave = weave_table(
-        group_lanes, width, plane, depth, edge_y, first_cell % CPC, first_lane(), wide
-    )
+    weave = weave_table(width, plane, depth, edge_y, first_cell % CPC, first_lane(), wide)
 
     def place(start, layer):
         if not isinstance(start, int):
@@ -768,9 +757,8 @@
     span = max(width, wide)
     results = pl.pallas_call(
         functools.partial(
-            finish_kernel, plane, depth, flat_cells, layers, group_lanes, sizes,
-            first_layer, own_row if whole else None, cell_row, first_lane,
-            isinstance(start_layer, int),
+            finish_kernel, plane, depth, flat_cells, layers, sizes, first_layer,
+            own_row if whole else None, cell_row, isinstance(start_layer, int),
         ),
         out_shape=(new_shape, solid_shape) if whole else (solid_shape,),
         in_specs=[VMEM] * 12,

time: 19.6 us -> 19.5 us (level)
  transfers between devices with their start and end apart: 5 -> 5, of which waited for: 4 -> 4; matrix products, arithmetic and copies ran while one was open for 1% -> 2% of each run, Pallas kernels for 18% -> 18%
where the time goes in v8:
time: 19.5 us; the launch traced here: 19.3 us
  starting transfers between devices  9.17 us (47%)
  Pallas kernels  5.49 us (28%)
  waiting for transfers between devices  3.39 us (17%)
  between operations  0.77 us (4%)
  other arithmetic  0.41 us (2%)
    ppermute x5, starting transfers between devices, exchanged(): lax.ppermute(sent, AXES, [(i, i ^ flips) for i in range(devices)])  9.17 us
    ppermute x5, waiting for transfers between devices, exchanged(): lax.ppermute(sent, AXES, [(i, i ^ flips) for i in range(devices)])  3.39 us
    pallas_call x1, Pallas kernels, body(): pl.pallas_call(functools.partial(faces_kernel, depth, flat_cells), out_sh...  1.36 us
    pallas_call x1, Pallas kernels, sites(): pl.pallas_call(functools.partial(sites_kernel, flat_cells), out_shape=(ja...  1.24 us
    pallas_call x1, Pallas kernels, body(): pl.pallas_call(functools.partial(finish_kernel, plane, depth, flat_cells,...  1.24 us
    pallas_call x1, Pallas kernels, body(): pl.pallas_call(pack_kernel, out_shape=[jax.ShapeDtypeStruct((9, unit), jn...  0.85 us
    pallas_call x1, Pallas kernels, body(): pl.pallas_call(functools.partial(cells_kernel, depth, flat_cells), out_sh...  0.81 us
  transfers between devices with their start and end apart: 5, of which 4 were waited for; matrix products, arithmetic and copies ran while one was open for 2% of the time, Pallas kernels for 18%

profile of v8, /device:TPU:0, one launch (start us, length us, event | category | flops | bytes accessed | tf_op | source)
XLA Modules:
  0.0 19.3 jit_solution(7606115007604390009)
XLA Ops:
  0.6 0.8 %pack.1 = f32[9,128]{1,0:T(8,128)S(1)} custom-call(f32[2,128]{1,0:T(2,128)} %state_ref.1, f32[2,128]{1,0:T(2,128)} %heat_ref.1, f32[1,32]{1,0:T(1,128)} %kappa_ref.1, f32[128,128]{1,0:T(8,128)} %frozen_hbm.1, s32[128,128]{1,0:T(8,128)} %label_hbm.1), custom_call_target="tpu_custom_call" | custom-call | tf_op jit(solution)/shard_map/pack/pallas_call | solution.py:525
  1.5 2.4 %collective-permute-start = (f32[9,128]{1,0:T(8,128)S(1)}, f32[9,128]{1,0:T(8,128)S(1)}, u32[]{:S(2)}, u32[]{:S(2)}) collective-permute-start(f32[9,128]{1,0:T(8,128)S(1)} %pack.1), channel_id=1, source_target_pairs={{0,17},{1,16},{2,19},{3,18},{4,21},{5,20},{6,23},{7,22},{8,25},{9,... | collective-permute-start | bytes 13832 | tf_op jit(solution)/shard_map/ppermute | solution.py:516
  4.0 1.4 %faces.1 = (s32[32,128]{1,0:T(8,128)S(1)}, s32[128,128]{1,0:T(8,128)S(1)}, f32[128,128]{1,0:T(8,128)S(1)}, f32[32,128]{1,0:T(8,128)S(1)}) custom-call(s32[6,8000]{1,0:T(8,128)} %bitcast.3, s32[128,128]{1,0:T(8,128)} %label_hbm.1, f32[128,128]{1,0:T(8,128)} %frozen_hbm.1), custom_call_target="tpu_custom_call" | custom-call | tf_op jit(solution)/shard_map/faces/pallas_call | solution.py:558
  5.4 0.0 collective-permute-done
  5.5 3.0 %collective-permute-start.1 = (f32[26,128]{1,0:T(8,128)S(1)}, f32[26,128]{1,0:T(8,128)S(1)}, u32[]{:S(2)}, u32[]{:S(2)}) collective-permute-start(f32[26,128]{1,0:T(8,128)S(1)} %pad_add_fusion.3), channel_id=1, source_target_pairs={{0,9},{1,8},{2,11},{3,10},{4,13},{5,12},{6,15},{7,14},{8,1},{9,0},... | collective-permute-start | bytes 39944 | tf_op jit(solution)/shard_map/ppermute | solution.py:516
  8.5 0.8 %cells.1 = (f32[128,128]{1,0:T(8,128)S(1)}, f32[32,128]{1,0:T(8,128)S(1)}) custom-call(s32[32,128]{1,0:T(8,128)S(1)} %get-tuple-element.13.packed_ref, s32[128,128]{1,0:T(8,128)S(1)} %get-tuple-element.14.label_ref, f32[128,128]{1,0:T(8,128)S(1)} %get-tuple-element.15.frozen_ref, f32[32,128]{1,0:T(8,128)S(1)} %get-tuple-element.12.faces_ref), custom_call_target="tpu_custom_call" | custom-call | tf_op jit(solution)/shard_map/cells/pallas_call | solution.py:575
  9.3 0.6 %collective-permute-done.1 = f32[26,128]{1,0:T(8,128)S(1)} collective-permute-done((f32[26,128]{1,0:T(8,128)S(1)}, f32[26,128]{1,0:T(8,128)S(1)}, u32[]{:S(2)}, u32[]{:S(2)}) %collective-permute-start.1) | collective-permute-done | bytes 13344 | tf_op jit(solution)/shard_map/ppermute | solution.py:516
  10.0 1.7 %collective-permute-start.2 = (f32[31,128]{1,0:T(8,128)S(1)}, f32[31,128]{1,0:T(8,128)S(1)}, u32[]{:S(2)}, u32[]{:S(2)}) collective-permute-start(f32[31,128]{1,0:T(8,128)S(1)} %pad_add_fusion.2), channel_id=1, source_target_pairs={{0,5},{1,4},{2,7},{3,6},{4,1},{5,0},{6,3},{7,2},{8,13},{9,12},{10,... | collective-permute-start | bytes 47624 | tf_op jit(solution)/shard_map/ppermute | solution.py:516
  11.7 1.2 %sites.1 = (f32[128,128]{1,0:T(8,128)S(1)}, f32[2,128]{1,0:T(2,128)S(1)}, bf16[128,640]{1,0:T(8,128)(2,1)S(1)}, f32[32,128]{1,0:T(8,128)S(1)}) custom-call(s32[32,128]{1,0:T(8,128)S(1)} %get-tuple-element.13.packed_ref, f32[4,128]{1,0:T(4,128)S(1)} %slice.91.edge_ref, f32[32,128]{1,0:T(8,128)S(1)} %get-tuple-element.16.faces_ref, s32[2,128]{1,0:T(2,128)} %bitcast.4, ...), custom_call_target="tpu_custom_call" | custom-call | tf_op jit(solution)/shard_map/sites/pallas_call | solution.py:591
  12.9 0.3 %collective-permute-done.2 = f32[31,128]{1,0:T(8,128)S(1)} collective-permute-done((f32[31,128]{1,0:T(8,128)S(1)}, f32[31,128]{1,0:T(8,128)S(1)}, u32[]{:S(2)}, u32[]{:S(2)}) %collective-permute-start.2) | collective-permute-done | bytes 15904 | tf_op jit(solution)/shard_map/ppermute | solution.py:516
  13.3 1.6 %collective-permute-start.3 = (f32[62,128]{1,0:T(8,128)S(1)}, f32[62,128]{1,0:T(8,128)S(1)}, u32[]{:S(2)}, u32[]{:S(2)}) collective-permute-start(f32[62,128]{1,0:T(8,128)S(1)} %pad_add_fusion.1), channel_id=1, source_target_pairs={{0,3},{1,2},{2,1},{3,0},{4,7},{5,6},{6,5},{7,4},{8,11},{9,10},{10,... | collective-permute-start | bytes 95240 | tf_op jit(solution)/shard_map/ppermute | solution.py:516
  14.9 1.8 %collective-permute-done.3 = f32[62,128]{1,0:T(8,128)S(1)} collective-permute-done((f32[62,128]{1,0:T(8,128)S(1)}, f32[62,128]{1,0:T(8,128)S(1)}, u32[]{:S(2)}, u32[]{:S(2)}) %collective-permute-start.3) | collective-permute-done | bytes 31776 | tf_op jit(solution)/shard_map/ppermute | solution.py:516
  16.7 0.4 %collective-permute-start.4 = (f32[94,128]{1,0:T(8,128)S(1)}, f32[94,128]{1,0:T(8,128)S(1)}, u32[]{:S(2)}, u32[]{:S(2)}) collective-permute-start(f32[94,128]{1,0:T(8,128)S(1)} %pad_add_fusion.mine_ref), channel_id=1, source_target_pairs={{0,1},{1,0},{2,3},{3,2},{4,5},{5,4},{6,7},{7,6},{8,9},{9,8},{10,11... | collective-permute-start | bytes 144392 | tf_op jit(solution)/shard_map/ppermute | solution.py:516
  17.1 0.2 %fusion.1.weave_ref = bf16[256,128]{1,0:T(8,128)(2,1)S(1)} fusion(f32[128]{0:T(128)S(1)} %get-tuple-element.34, f32[128]{0:T(128)S(1)} %get-tuple-element.35, f32[128]{0:T(128)S(1)} %get-tuple-element.36, s32[128]{0:T(128)S(1)} %get-tuple-element.39, s32[256]{0:T(256)S(1)} %get-tuple-element.30, f32[128]{0:T(128)S(1)} %get-tuple-element.32, ...), kind=kLoop, calls=%fused_computation.10 | loop fusion | flops 1212416 | bytes 72064 | tf_op jit(solution)/shard_map/convert_element_type | solution.py:446
  17.4 0.6 %collective-permute-done.4.theirs_ref.across_ref.passing_ref.edge_ref = f32[94,128]{1,0:T(8,128)S(1)} collective-permute-done((f32[94,128]{1,0:T(8,128)S(1)}, f32[94,128]{1,0:T(8,128)S(1)}, u32[]{:S(2)}, u32[]{:S(2)}) %collective-permute-start.4) | collective-permute-done | bytes 48160 | tf_op jit(solution)/shard_map/ppermute | solution.py:516
  18.0 1.2 %finish.1 = (f32[2,128]{1,0:T(2,128)}, f32[128,128]{1,0:T(8,128)}) custom-call(f32[94,128]{1,0:T(8,128)S(1)} %pad_add_fusion.mine_ref, f32[94,128]{1,0:T(8,128)S(1)} %collective-permute-done.4.theirs_ref.across_ref.passing_ref.edge_ref, f32[94,128]{1,0:T(8,128)S(1)} %collective-permute-done.4.theirs_ref.across_ref.passing_ref.edge_ref, ...), custom_call_target="tpu_custom_call" | custom-call | tf_op jit(solution)/shard_map/finish/pallas_call | solution.py:758
  (24 shorter events, 0.2 us)
Async XLA Ops:
  1.5 3.9 %collective-permute-start = (f32[9,128]{1,0:T(8,128)S(1)}, f32[9,128]{1,0:T(8,128)S(1)}, u32[]{:S(2)}, u32[]{:S(2)}) collective-permute-start(f32[9,128]{1,0:T(8,128)S(1)} %pack.1), channel_id=1, source_target_pairs={{0,17},{1,16},{2,19},{3,18},{4,21},{5,20},{6,23},{7,22},{8,25},{9,... | collective-permute-start | bytes 13832 | tf_op jit(solution)/shard_map/ppermute | solution.py:516
  5.5 4.5 %collective-permute-start.1 = (f32[26,128]{1,0:T(8,128)S(1)}, f32[26,128]{1,0:T(8,128)S(1)}, u32[]{:S(2)}, u32[]{:S(2)}) collective-permute-start(f32[26,128]{1,0:T(8,128)S(1)} %pad_add_fusion.3), channel_id=1, source_target_pairs={{0,9},{1,8},{2,11},{3,10},{4,13},{5,12},{6,15},{7,14},{8,1},{9,0},... | collective-permute-start | bytes 39944 | tf_op jit(solution)/shard_map/ppermute | solution.py:516
  10.0 3.2 %collective-permute-start.2 = (f32[31,128]{1,0:T(8,128)S(1)}, f32[31,128]{1,0:T(8,128)S(1)}, u32[]{:S(2)}, u32[]{:S(2)}) collective-permute-start(f32[31,128]{1,0:T(8,128)S(1)} %pad_add_fusion.2), channel_id=1, source_target_pairs={{0,5},{1,4},{2,7},{3,6},{4,1},{5,0},{6,3},{7,2},{8,13},{9,12},{10,... | collective-permute-start | bytes 47624 | tf_op jit(solution)/shard_map/ppermute | solution.py:516
  13.3 3.4 %collective-permute-start.3 = (f32[62,128]{1,0:T(8,128)S(1)}, f32[62,128]{1,0:T(8,128)S(1)}, u32[]{:S(2)}, u32[]{:S(2)}) collective-permute-start(f32[62,128]{1,0:T(8,128)S(1)} %pad_add_fusion.1), channel_id=1, source_target_pairs={{0,3},{1,2},{2,1},{3,0},{4,7},{5,6},{6,5},{7,4},{8,11},{9,10},{10,... | collective-permute-start | bytes 95240 | tf_op jit(solution)/shard_map/ppermute | solution.py:516
  16.7 1.3 %collective-permute-start.4 = (f32[94,128]{1,0:T(8,128)S(1)}, f32[94,128]{1,0:T(8,128)S(1)}, u32[]{:S(2)}, u32[]{:S(2)}) collective-permute-start(f32[94,128]{1,0:T(8,128)S(1)} %pad_add_fusion.mine_ref), channel_id=1, source_target_pairs={{0,1},{1,0},{2,3},{3,2},{4,5},{5,4},{6,7},{7,6},{8,9},{9,8},{10,11... | collective-permute-start | bytes 144392 | tf_op jit(solution)/shard_map/ppermute | solution.py:516

commit v9 on v8

--- a/solution.py
+++ b/solution.py
@@ -43,13 +43,24 @@
     return out
 
 
-def side_by_side(values, lanes):
-    first, second, third = pieces(values)
-    return first + pltpu.roll(second, lanes, 1) + pltpu.roll(third, 2 * lanes, 1)
+def at_nodes(plane, flat, row):
+    elements = row.shape[1]
+    wide = up_to(elements, LANES)
+    row = jnp.broadcast_to(row, (8, elements))
+    if wide > elements:
+        row = jnp.concatenate([row, jnp.zeros((8, wide - elements), jnp.float32)], 1)
+    parts = []
+    for start in range(0, flat, LANES):
+        node_y, deep = split_index(lax.broadcasted_iota(jnp.int32, (8, LANES), 1) + start, plane)
+        element = (node_y >> 1) * (plane // 2) + (deep >> 1)
+        tile = start // 4 // LANES * LANES
+        here = row[:, tile : tile + LANES]
+        parts.append(jnp.take_along_axis(here, element - tile, axis=1, mode="promise_in_bounds"))
+    return jnp.concatenate(parts, 1)[0:1] if len(parts) > 1 else parts[0][0:1]
 
 
 def pack_kernel(
-    state_ref, heat_ref, kappa_ref, frozen_ref, label_ref, held_ref, *refs
+    plane, state_ref, heat_ref, kappa_ref, frozen_ref, label_ref, held_ref, *refs
 ):
     state, heat, kappa, frozen, label, sems = refs[-6:]
     edge_ref = refs[0] if len(refs) > 6 else held_ref.at[5:9, :]
@@ -77,9 +88,7 @@
             row = slice(2 * layer + parity, 2 * layer + parity + 1)
             held_ref[parity : parity + 1, lanes] = state[row, :]
             held_ref[2 + parity : 3 + parity, lanes] = heat[row, :]
-        wide = jnp.broadcast_to(kappa[layer : layer + 1, :], (8, elements))
-        wide = jnp.concatenate([wide, jnp.zeros((8, flat - elements), jnp.float32)], 1)
-        held_ref[4:5, lanes] = side_by_side(wide, elements)[0:1]
+        held_ref[4:5, lanes] = at_nodes(plane, flat, kappa[layer : layer + 1, :])
     for copy in copies[3:]:
         copy.wait()
     edge_ref[0:1, :] = frozen[1, 7:8, :]
@@ -198,10 +207,10 @@
 
 
 def sites_kernel(
-    flat, packed_ref, edge_ref, faces_ref, slot_hbm, seed_hbm, spread_hbm,
-    nucleation_ref, ends_ref, spread_ref, onward_ref, slot_ref, seed_ref, sems,
+    flat, packed_ref, edge_ref, faces_ref, slot_hbm, seed_hbm,
+    nucleation_ref, ends_ref, onward_ref, slot_ref, seed_ref, sems,
 ):
-    copies = started([(slot_hbm, slot_ref), (seed_hbm, seed_ref), (spread_hbm, spread_ref)], sems)
+    copies = started([(slot_hbm, slot_ref), (seed_hbm, seed_ref)], sems)
     onward_ref[...] = faces_ref[...]
     edge_x, wide = nucleation_ref.shape
     for t in range(wide // LANES):
@@ -228,36 +237,7 @@
     nucleation_ref[...] = added * (1.0 / 6.0)
 
 
-def spread_tables(width, plane):
-    rows_y, deep = width // plane, plane // 2
-
-    def tables(count):
-        spread, after, before = (np.zeros((count // 2, count), np.float32) for _ in range(3))
-        for element in range(count // 2):
-            for local, weight in enumerate((1, 4, 1)):
-                spread[element, (2 * element + local) % count] += weight
-            for local in range(2):
-                after[element, (2 * element + local) % count] += 1
-                before[element, (2 * element + local + 1) % count] += 1
-        return spread, after, before
-
-    spread_y, after_y, before_y = tables(rows_y)
-    spread_z, after_z, before_z = tables(plane)
-    full = [
-        np.kron(spread_y, spread_z),
-        np.kron(after_y, spread_z),
-        np.kron(before_y, spread_z),
-        np.kron(spread_y, after_z),
-        np.kron(spread_y, before_z),
-    ]
-    half = lambda count: np.where(np.arange(count) % 2 == 1, 0.5, 1.0)
-    inverse = 27.0 * np.kron(half(rows_y), half(plane))
-    out = np.zeros((width, 5 * width), jnp.bfloat16)
-    out[: 3 * (width // 4)] = np.concatenate([np.concatenate([t * inverse for t in full], 1)] * 3, 0)
-    return out
-
-
-def advance(plane, even, odd, heat_even, heat_odd, kappa, spread):
+def advance(plane, even, odd, heat_even, heat_odd, kappa):
     rows, width = even.shape
     up = lambda v: pltpu.roll(v, rows - 1, 0)
     down = lambda v: pltpu.roll(v, 1, 0)
@@ -265,11 +245,24 @@
     lane = lax.broadcasted_iota(jnp.int32, (rows, width), 1)
     row_y, deep = split_index(lane, plane)
     even_y, even_z = row_y & 1 == 0, deep & 1 == 0
-    lines = jnp.dot(kappa.astype(jnp.bfloat16), spread, preferred_element_type=jnp.float32)
-    lines = lines * (STEP / 108.0)
-    along_x, *others = (lines[:, i * width : (i + 1) * width] for i in range(5))
+    back = turn(kappa, 1)
+    low_y = turn(kappa, plane)
+    low_z = jnp.where(deep == 0, turn(kappa, 1 - plane), back)
+    low = jnp.where(deep == 0, back, turn(kappa, plane + 1))
+    spread_z = jnp.where(even_z, kappa + low_z, 4.0 * kappa)
+    spread_z_low = jnp.where(even_z, low_y + low, 4.0 * low_y)
+    spread_y = jnp.where(even_y, kappa + low_y, 4.0 * kappa)
+    spread_y_low = jnp.where(even_y, low_z + low, 4.0 * low_z)
+    scale = STEP * 27.0 * jnp.where(even_y, 1.0, 0.5) * jnp.where(even_z, 1.0, 0.5)
+    share = scale * (1.0 / 108.0)
+    along_x = share * jnp.where(even_y, spread_z + spread_z_low, 4.0 * spread_z)
+    others = [
+        share * spread_z,
+        share * jnp.where(even_y, spread_z_low, spread_z),
+        share * spread_y,
+        share * jnp.where(even_z, spread_y_low, spread_y),
+    ]
     behind_x = down(along_x)
-    scale = STEP * 27.0 * jnp.where(even_y, 1.0, 0.5) * jnp.where(even_z, 1.0, 0.5)
     heat_even, heat_odd = scale * heat_even, (0.5 * scale) * heat_odd
 
     def in_plane(parts):
@@ -315,10 +308,8 @@
     return even + 0.5 * (one_even + two_even), odd + 0.5 * (one_odd + two_odd)
 
 
-def heat_kernel(plane, layers, first_row, state_ref, spread_ref, new_ref, even_ref, odd_ref):
-    state = [state_ref[i] for i in range(5)]
-    state[4] = side_by_side(state[4], state[4].shape[1] // 4)
-    even, odd = advance(plane, *state, spread_ref[...])
+def heat_kernel(plane, layers, first_row, state_ref, new_ref, even_ref, odd_ref):
+    even, odd = advance(plane, *(state_ref[i] for i in range(5)))
     even_ref[...] = even
     odd_ref[...] = odd
     start = first_row()
@@ -338,7 +329,7 @@
 
 def finish_kernel(
     plane, depth, flat, layers, sizes, first_layer, first_row, cell_row, wraps,
-    mine_ref, theirs_ref, across_ref, passing_ref, edge_ref, kept_ref, spread_ref, weave_ref,
+    mine_ref, theirs_ref, across_ref, passing_ref, edge_ref, kept_ref, weave_ref,
     packed_ref, gathered_ref, nucleation_ref, frozen_ref, *refs,
 ):
     solid_out, state_ref, even_ref, odd_ref, side_ref, extra_ref, solid_ref, new_ref, sems = refs[-9:]
@@ -367,7 +358,6 @@
         state = [state_ref[i, 0:rows, :] for i in range(5)]
     else:
         state = [mine_ref[i] for i in range(5)]
-        state[4] = side_by_side(state[4], width // 4)
     side_ref[...] = jnp.zeros(side_ref.shape, jnp.float32)
     there = jnp.where(core == 0, 0, flat - depth)
     side_ref[pl.ds(pl.multiple_of(there, 8), depth), :] = (
@@ -379,7 +369,7 @@
     extra_ref[...] = gathered_ref[...] + jnp.transpose(side_ref[...])
     extra_ref[0:1, :] += edge_ref[edge_row : edge_row + 1, 0:wide]
     extra_ref[edge_x - 1 : edge_x, :] += edge_ref[edge_row + 1 : edge_row + 2, 0:wide]
-    even, odd = advance(plane, *state, spread_ref[...])
+    even, odd = advance(plane, *state)
     if first_row is not None:
         even_ref[:, 0:width] = even
         odd_ref[:, 0:width] = odd
@@ -523,7 +513,7 @@
     frozen, label = widened(frozen_share_map), widened(crystal_label_map)
     joined = groups == 2 and wide == unit
     packed_rows = pl.pallas_call(
-        pack_kernel,
+        functools.partial(pack_kernel, plane),
         out_shape=[jax.ShapeDtypeStruct((9, unit), jnp.float32)]
         if joined
         else [
@@ -593,15 +583,14 @@
             out_shape=(
                 jax.ShapeDtypeStruct((edge_x, wide), jnp.float32),
                 jax.ShapeDtypeStruct((2, wide), jnp.float32),
-                jax.ShapeDtypeStruct((width, 5 * width), jnp.bfloat16),
                 jax.ShapeDtypeStruct((2 * depth, edge_x), jnp.float32),
             ),
-            in_specs=[VMEM] * 3 + [HBM] * 3,
-            out_specs=[VMEM] * 4,
+            in_specs=[VMEM] * 3 + [HBM] * 2,
+            out_specs=[VMEM] * 3,
             scratch_shapes=[
                 pltpu.VMEM((seeds // LANES, LANES), jnp.int32),
                 pltpu.VMEM((seeds // LANES, LANES), jnp.int32),
-                pltpu.SemaphoreType.DMA((3,)),
+                pltpu.SemaphoreType.DMA((2,)),
             ],
             compiler_params=PARAMS,
             name="sites",
@@ -611,7 +600,6 @@
             faces_later,
             in_hbm(jnp.pad(seed_site_slots, (0, short), constant_values=-1).reshape(-1, LANES)),
             in_hbm(jnp.pad(seed_crystal_label, (0, short)).reshape(-1, LANES)),
-            in_hbm(jnp.asarray(spread_tables(width, plane))),
         )
 
     core, pair = me & 1, slab >> 1
@@ -668,7 +656,7 @@
         elif rides:
             onward, backward = as_face(parts[0]), as_face(parts[1])
         if edges is not None and ends is None:
-            nucleation, ends, spread, faces_last = sites(edges)
+            nucleation, ends, faces_last = sites(edges)
     extra = [
         lines(jnp.where(core == 0, faces_last[depth:], faces_last[:depth]), unit),
         lines(jnp.where(core == 1, onward, backward), unit),
@@ -695,8 +683,6 @@
         blocks = jnp.concatenate([sent[:heat_rows], got[:heat_rows]], 0).reshape(devices, 5, layers, flat)
         blocks = jnp.take(blocks, jnp.asarray(order)[jnp.arange(devices) ^ me], axis=0)
         held = jnp.moveaxis(blocks, 1, 0).reshape(5, all_layers, flat)
-        kappa = sum(held[4:, :, i * elements : (i + 1) * elements] for i in range(3))
-        held = jnp.concatenate([held[:4], jnp.pad(kappa, ((0, 0), (0, 0), (0, flat - elements)))])
 
         def window(first_layer, need_layers, first_element, need_elements):
             rows, lanes = up_to(need_layers, 8), up_to(need_elements * 2 * plane, LANES)
@@ -713,16 +699,7 @@
                     jnp.concatenate([v, v[..., :size]], -1), by, size, v.ndim - 1
                 )
                 start = jnp.remainder(first_element, rows_y // 2)
-                part = jnp.concatenate(
-                    [
-                        shifted(part[:4], start * 2 * plane, lanes),
-                        jnp.pad(
-                            shifted(part[4:, :, :elements], start * HEX_COUNT_LATER, lanes // 4),
-                            ((0, 0), (0, 0), (0, lanes - lanes // 4)),
-                        ),
-                    ],
-                    0,
-                )
+                part = shifted(part, start * 2 * plane, lanes)
             return part, start_layer, start_y
 
         state, start_layer, start_y = window(
@@ -761,7 +738,7 @@
             own_row if whole else None, cell_row, isinstance(start_layer, int),
         ),
         out_shape=(new_shape, solid_shape) if whole else (solid_shape,),
-        in_specs=[VMEM] * 12,
+        in_specs=[VMEM] * 11,
         out_specs=(HBM,) * (1 + whole),
         scratch_shapes=[
             pltpu.VMEM((5, all_layers if direct else rows, width), jnp.float32),
@@ -775,7 +752,7 @@
         ],
         compiler_params=PARAMS,
         name="finish",
-    )(*inputs, kept, spread, weave, packed, gathered, nucleation, frozen)
+    )(*inputs, kept, weave, packed, gathered, nucleation, frozen)
     if whole:
         new_field, new_solid = results
     else:
@@ -785,12 +762,12 @@
         new_field = pl.pallas_call(
             functools.partial(heat_kernel, plane, layers, own_row),
             out_shape=new_shape,
-            in_specs=[VMEM] * 2,
+            in_specs=[VMEM],
             out_specs=VMEM,
             scratch_shapes=[pltpu.VMEM(state.shape[1:], jnp.float32)] * 2,
             compiler_params=PARAMS,
             name="heat",
-        )(state, jnp.asarray(spread_tables(flat, plane)))
+        )(state)
     return new_field, new_solid[:, :flat_cells]
 
 

time: 19.5 us -> 19.4 us (level)
  Pallas kernels: 5.49 us -> 5.19 us
  waiting for transfers between devices: 3.39 us -> 3.66 us
    ppermute x5, waiting for transfers between devices: 3.39 us -> 3.66 us  [exchanged(): lax.ppermute(sent, AXES, [(i, i ^ flips) for i in range(devices)])]
    pallas_call x1, Pallas kernels: 1.24 us -> 0.98 us  [sites(): pl.pallas_call(functools.partial(sites_kernel, flat_cells), out_shape=(ja...]
  transfers between devices with their start and end apart: 5 -> 5, of which waited for: 4 -> 4; matrix products, arithmetic and copies ran while one was open for 2% -> 2% of each run, Pallas kernels for 18% -> 16%
where the time goes in v9:
time: 19.4 us; the launch traced here: 19.2 us
  starting transfers between devices  9.17 us (47%)
  Pallas kernels  5.19 us (27%)
  waiting for transfers between devices  3.66 us (19%)
  between operations  0.77 us (4%)
  other arithmetic  0.41 us (2%)
    ppermute x5, starting transfers between devices, exchanged(): lax.ppermute(sent, AXES, [(i, i ^ flips) for i in range(devices)])  9.17 us
    ppermute x5, waiting for transfers between devices, exchanged(): lax.ppermute(sent, AXES, [(i, i ^ flips) for i in range(devices)])  3.66 us
    pallas_call x1, Pallas kernels, body(): pl.pallas_call(functools.partial(faces_kernel, depth, flat_cells), out_sh...  1.36 us
    pallas_call x1, Pallas kernels, body(): pl.pallas_call(functools.partial(finish_kernel, plane, depth, flat_cells,...  1.2 us
    pallas_call x1, Pallas kernels, sites(): pl.pallas_call(functools.partial(sites_kernel, flat_cells), out_shape=(ja...  0.98 us
    pallas_call x1, Pallas kernels, body(): pl.pallas_call(functools.partial(pack_kernel, plane), out_shape=[jax.Shap...  0.85 us
    pallas_call x1, Pallas kernels, body(): pl.pallas_call(functools.partial(cells_kernel, depth, flat_cells), out_sh...  0.81 us
  transfers between devices with their start and end apart: 5, of which 4 were waited for; matrix products, arithmetic and copies ran while one was open for 2% of the time, Pallas kernels for 16%

profile of v9, /device:TPU:0, one launch (start us, length us, event | category | flops | bytes accessed | tf_op | source)
XLA Modules:
  0.0 19.2 jit_solution(2360217563087368677)
XLA Ops:
  0.6 0.8 %pack.1 = f32[9,128]{1,0:T(8,128)S(1)} custom-call(f32[2,128]{1,0:T(2,128)} %state_ref.1, f32[2,128]{1,0:T(2,128)} %heat_ref.1, f32[1,32]{1,0:T(1,128)} %kappa_ref.1, f32[128,128]{1,0:T(8,128)} %frozen_hbm.1, s32[128,128]{1,0:T(8,128)} %label_hbm.1), custom_call_target="tpu_custom_call" | custom-call | tf_op jit(solution)/shard_map/pack/pallas_call | solution.py:515
  1.5 2.4 %collective-permute-start = (f32[9,128]{1,0:T(8,128)S(1)}, f32[9,128]{1,0:T(8,128)S(1)}, u32[]{:S(2)}, u32[]{:S(2)}) collective-permute-start(f32[9,128]{1,0:T(8,128)S(1)} %pack.1), channel_id=1, source_target_pairs={{0,17},{1,16},{2,19},{3,18},{4,21},{5,20},{6,23},{7,22},{8,25},{9,... | collective-permute-start | bytes 13832 | tf_op jit(solution)/shard_map/ppermute | solution.py:506
  4.0 1.4 %faces.1 = (s32[32,128]{1,0:T(8,128)S(1)}, s32[128,128]{1,0:T(8,128)S(1)}, f32[128,128]{1,0:T(8,128)S(1)}, f32[32,128]{1,0:T(8,128)S(1)}) custom-call(s32[6,8000]{1,0:T(8,128)} %bitcast.3, s32[128,128]{1,0:T(8,128)} %label_hbm.1, f32[128,128]{1,0:T(8,128)} %frozen_hbm.1), custom_call_target="tpu_custom_call" | custom-call | tf_op jit(solution)/shard_map/faces/pallas_call | solution.py:548
  5.4 0.0 collective-permute-done
  5.5 3.0 %collective-permute-start.1 = (f32[26,128]{1,0:T(8,128)S(1)}, f32[26,128]{1,0:T(8,128)S(1)}, u32[]{:S(2)}, u32[]{:S(2)}) collective-permute-start(f32[26,128]{1,0:T(8,128)S(1)} %pad_add_fusion.3), channel_id=1, source_target_pairs={{0,9},{1,8},{2,11},{3,10},{4,13},{5,12},{6,15},{7,14},{8,1},{9,0},... | collective-permute-start | bytes 39944 | tf_op jit(solution)/shard_map/ppermute | solution.py:506
  8.5 0.8 %cells.1 = (f32[128,128]{1,0:T(8,128)S(1)}, f32[32,128]{1,0:T(8,128)S(1)}) custom-call(s32[32,128]{1,0:T(8,128)S(1)} %get-tuple-element.12.packed_ref, s32[128,128]{1,0:T(8,128)S(1)} %get-tuple-element.13.label_ref, f32[128,128]{1,0:T(8,128)S(1)} %get-tuple-element.14.frozen_ref, f32[32,128]{1,0:T(8,128)S(1)} %get-tuple-element.11.faces_ref), custom_call_target="tpu_custom_call" | custom-call | tf_op jit(solution)/shard_map/cells/pallas_call | solution.py:565
  9.3 0.6 %collective-permute-done.1 = f32[26,128]{1,0:T(8,128)S(1)} collective-permute-done((f32[26,128]{1,0:T(8,128)S(1)}, f32[26,128]{1,0:T(8,128)S(1)}, u32[]{:S(2)}, u32[]{:S(2)}) %collective-permute-start.1) | collective-permute-done | bytes 13344 | tf_op jit(solution)/shard_map/ppermute | solution.py:506
  10.0 1.7 %collective-permute-start.2 = (f32[31,128]{1,0:T(8,128)S(1)}, f32[31,128]{1,0:T(8,128)S(1)}, u32[]{:S(2)}, u32[]{:S(2)}) collective-permute-start(f32[31,128]{1,0:T(8,128)S(1)} %pad_add_fusion.2), channel_id=1, source_target_pairs={{0,5},{1,4},{2,7},{3,6},{4,1},{5,0},{6,3},{7,2},{8,13},{9,12},{10,... | collective-permute-start | bytes 47624 | tf_op jit(solution)/shard_map/ppermute | solution.py:506
  11.7 1.0 %sites.1 = (f32[128,128]{1,0:T(8,128)S(1)}, f32[2,128]{1,0:T(2,128)S(1)}, f32[32,128]{1,0:T(8,128)S(1)}) custom-call(s32[32,128]{1,0:T(8,128)S(1)} %get-tuple-element.12.packed_ref, f32[4,128]{1,0:T(4,128)S(1)} %slice.91.edge_ref, f32[32,128]{1,0:T(8,128)S(1)} %get-tuple-element.15.faces_ref, s32[2,128]{1,0:T(2,128)} %bitcast.4, s32[2,128]{1,0:T(2,128)} %bitcast.5), custom_call_target="tpu_custom_call" | custom-call | tf_op jit(solution)/shard_map/sites/pallas_call | solution.py:581
  12.6 0.6 %collective-permute-done.2 = f32[31,128]{1,0:T(8,128)S(1)} collective-permute-done((f32[31,128]{1,0:T(8,128)S(1)}, f32[31,128]{1,0:T(8,128)S(1)}, u32[]{:S(2)}, u32[]{:S(2)}) %collective-permute-start.2) | collective-permute-done | bytes 15904 | tf_op jit(solution)/shard_map/ppermute | solution.py:506
  13.3 1.6 %collective-permute-start.3 = (f32[62,128]{1,0:T(8,128)S(1)}, f32[62,128]{1,0:T(8,128)S(1)}, u32[]{:S(2)}, u32[]{:S(2)}) collective-permute-start(f32[62,128]{1,0:T(8,128)S(1)} %pad_add_fusion.1), channel_id=1, source_target_pairs={{0,3},{1,2},{2,1},{3,0},{4,7},{5,6},{6,5},{7,4},{8,11},{9,10},{10,... | collective-permute-start | bytes 95240 | tf_op jit(solution)/shard_map/ppermute | solution.py:506
  14.9 1.8 %collective-permute-done.3 = f32[62,128]{1,0:T(8,128)S(1)} collective-permute-done((f32[62,128]{1,0:T(8,128)S(1)}, f32[62,128]{1,0:T(8,128)S(1)}, u32[]{:S(2)}, u32[]{:S(2)}) %collective-permute-start.3) | collective-permute-done | bytes 31776 | tf_op jit(solution)/shard_map/ppermute | solution.py:506
  16.7 0.4 %collective-permute-start.4 = (f32[94,128]{1,0:T(8,128)S(1)}, f32[94,128]{1,0:T(8,128)S(1)}, u32[]{:S(2)}, u32[]{:S(2)}) collective-permute-start(f32[94,128]{1,0:T(8,128)S(1)} %pad_add_fusion.mine_ref), channel_id=1, source_target_pairs={{0,1},{1,0},{2,3},{3,2},{4,5},{5,4},{6,7},{7,6},{8,9},{9,8},{10,11... | collective-permute-start | bytes 144392 | tf_op jit(solution)/shard_map/ppermute | solution.py:506
  17.1 0.2 %fusion.1.weave_ref = bf16[256,128]{1,0:T(8,128)(2,1)S(1)} fusion(f32[128]{0:T(128)S(1)} %get-tuple-element.32, f32[128]{0:T(128)S(1)} %get-tuple-element.33, f32[128]{0:T(128)S(1)} %get-tuple-element.34, s32[128]{0:T(128)S(1)} %get-tuple-element.37, s32[256]{0:T(256)S(1)} %get-tuple-element.28, f32[128]{0:T(128)S(1)} %get-tuple-element.30, ...), kind=kLoop, calls=%fused_computation.10 | loop fusion | flops 1212416 | bytes 72064 | tf_op jit(solution)/shard_map/convert_element_type | solution.py:436
  17.4 0.6 %collective-permute-done.4.theirs_ref.across_ref.passing_ref.edge_ref = f32[94,128]{1,0:T(8,128)S(1)} collective-permute-done((f32[94,128]{1,0:T(8,128)S(1)}, f32[94,128]{1,0:T(8,128)S(1)}, u32[]{:S(2)}, u32[]{:S(2)}) %collective-permute-start.4) | collective-permute-done | bytes 48160 | tf_op jit(solution)/shard_map/ppermute | solution.py:506
  18.0 1.2 %finish.1 = (f32[2,128]{1,0:T(2,128)}, f32[128,128]{1,0:T(8,128)}) custom-call(f32[94,128]{1,0:T(8,128)S(1)} %pad_add_fusion.mine_ref, f32[94,128]{1,0:T(8,128)S(1)} %collective-permute-done.4.theirs_ref.across_ref.passing_ref.edge_ref, f32[94,128]{1,0:T(8,128)S(1)} %collective-permute-done.4.theirs_ref.across_ref.passing_ref.edge_ref, ...), custom_call_target="tpu_custom_call" | custom-call | tf_op jit(solution)/shard_map/finish/pallas_call | solution.py:735
  (24 shorter events, 0.2 us)
Async XLA Ops:
  1.5 3.9 %collective-permute-start = (f32[9,128]{1,0:T(8,128)S(1)}, f32[9,128]{1,0:T(8,128)S(1)}, u32[]{:S(2)}, u32[]{:S(2)}) collective-permute-start(f32[9,128]{1,0:T(8,128)S(1)} %pack.1), channel_id=1, source_target_pairs={{0,17},{1,16},{2,19},{3,18},{4,21},{5,20},{6,23},{7,22},{8,25},{9,... | collective-permute-start | bytes 13832 | tf_op jit(solution)/shard_map/ppermute | solution.py:506
  5.5 4.5 %collective-permute-start.1 = (f32[26,128]{1,0:T(8,128)S(1)}, f32[26,128]{1,0:T(8,128)S(1)}, u32[]{:S(2)}, u32[]{:S(2)}) collective-permute-start(f32[26,128]{1,0:T(8,128)S(1)} %pad_add_fusion.3), channel_id=1, source_target_pairs={{0,9},{1,8},{2,11},{3,10},{4,13},{5,12},{6,15},{7,14},{8,1},{9,0},... | collective-permute-start | bytes 39944 | tf_op jit(solution)/shard_map/ppermute | solution.py:506
  10.0 3.2 %collective-permute-start.2 = (f32[31,128]{1,0:T(8,128)S(1)}, f32[31,128]{1,0:T(8,128)S(1)}, u32[]{:S(2)}, u32[]{:S(2)}) collective-permute-start(f32[31,128]{1,0:T(8,128)S(1)} %pad_add_fusion.2), channel_id=1, source_target_pairs={{0,5},{1,4},{2,7},{3,6},{4,1},{5,0},{6,3},{7,2},{8,13},{9,12},{10,... | collective-permute-start | bytes 47624 | tf_op jit(solution)/shard_map/ppermute | solution.py:506
  13.3 3.4 %collective-permute-start.3 = (f32[62,128]{1,0:T(8,128)S(1)}, f32[62,128]{1,0:T(8,128)S(1)}, u32[]{:S(2)}, u32[]{:S(2)}) collective-permute-start(f32[62,128]{1,0:T(8,128)S(1)} %pad_add_fusion.1), channel_id=1, source_target_pairs={{0,3},{1,2},{2,1},{3,0},{4,7},{5,6},{6,5},{7,4},{8,11},{9,10},{10,... | collective-permute-start | bytes 95240 | tf_op jit(solution)/shard_map/ppermute | solution.py:506
  16.7 1.3 %collective-permute-start.4 = (f32[94,128]{1,0:T(8,128)S(1)}, f32[94,128]{1,0:T(8,128)S(1)}, u32[]{:S(2)}, u32[]{:S(2)}) collective-permute-start(f32[94,128]{1,0:T(8,128)S(1)} %pad_add_fusion.mine_ref), channel_id=1, source_target_pairs={{0,1},{1,0},{2,3},{3,2},{4,5},{5,4},{6,7},{7,6},{8,9},{9,8},{10,11... | collective-permute-start | bytes 144392 | tf_op jit(solution)/shard_map/ppermute | solution.py:506

commit v10 on v9

--- a/solution.py
+++ b/solution.py
@@ -12,7 +12,6 @@
 CPC = 8
 LANES = 128
 CHUNKS = 4
-HIGHEST = lax.Precision.HIGHEST
 STEP = 0.004
 AXES = ("grp", "slab")
 VMEM = pl.BlockSpec(memory_space=pltpu.VMEM)
@@ -342,9 +341,10 @@
         slabs = lax.axis_size("slab")
         me = lax.axis_index("grp") * slabs + lax.axis_index("slab")
         state_ref[:, rows - 8 : rows, :] = jnp.zeros((5, 8, width), jnp.float32)
-        numbers = [me ^ off for off in arrival_order(slabs)[: slabs // 2]]
+        own = arrival_order(bit_order(slabs, slabs))[: slabs // 2]
+        numbers = [me ^ off for off in own]
         numbers += beyond_order(me, slabs)
-        numbers += [me ^ 1 ^ off for off in arrival_order(slabs)[: slabs // 2]]
+        numbers += [me ^ 1 ^ off for off in own]
         numbers += beyond_order(me ^ 1, slabs)
         blocks = len(numbers) // 2
         for p, number in enumerate(numbers):
@@ -388,10 +388,11 @@
         jnp.concatenate([high, high, high, low, low], 0),
         preferred_element_type=jnp.float32,
     )
-    even_ref[:, 0:wide] = woven[:rows]
-    odd_ref[:, 0:wide] = woven[rows:]
+    base = cell_row()
+    if not isinstance(base, int):
+        even_ref[:, 0:wide] = woven[:rows]
+        odd_ref[:, 0:wide] = woven[rows:]
     first, middle, last = basis(lax.broadcasted_iota(jnp.int32, (CPC, wide), 0))
-    base = cell_row()
     elements = edge_x // CPC
     copies = []
     for a in range(elements):
@@ -399,11 +400,13 @@
         later = base + (a + 1)
         if wraps:
             later = lax.rem(later, rows)
-        temperature = (
-            first * even_ref[pl.ds(base + a, 1), 0:wide]
-            + middle * odd_ref[pl.ds(base + a, 1), 0:wide]
-            + last * even_ref[pl.ds(later, 1), 0:wide]
-        )
+        if isinstance(base, int):
+            at = slice(base + a, base + a + 1)
+            lower, between, higher = woven[at], woven[rows:][at], woven[base + a + 1 : base + a + 2]
+        else:
+            lower, between = (ref[pl.ds(base + a, 1), 0:wide] for ref in (even_ref, odd_ref))
+            higher = even_ref[pl.ds(later, 1), 0:wide]
+        temperature = first * lower + middle * between + last * higher
         under = jnp.maximum(-temperature, 0.0)
         rate = under * (under * extra_ref[cells, :] + nucleation_ref[cells, :])
         frozen = frozen_ref[cells, :]
@@ -436,30 +439,33 @@
     return jnp.where(cell < edge_y * depth, part, 0.0).astype(jnp.bfloat16)
 
 
+def bit_order(devices, slabs):
+    top, middle = devices.bit_length() - 2, slabs.bit_length() - 2
+    return [*range(top, middle, -1), *range(2, middle + 1), *([1] if middle > 0 else [])]
+
+
 def beyond_order(me, slabs):
     top = slabs.bit_length() - 2
 
     def kept(number, bit):
-        if bit > top:
+        if bit < 2:
             return [number ^ slabs ^ 1]
         flips = (1 << bit) | 1
-        if bit == 1:
-            return kept(number, 2) + kept(number ^ flips, 2)
         return [picked(number, bit), picked(number ^ flips, bit)]
 
     def picked(number, bit):
-        held = kept(number, bit + 1)
+        held = kept(number, bit - 1)
         if len(held) == 1:
             return held[0]
-        same = ((number >> bit) ^ (number >> (bit + 1))) & 1 == 0
+        same = ((number >> bit) ^ (number >> (bit - 1))) & 1 == 0
         return jnp.where(same, held[0], held[1])
 
-    return kept(me, 1)
-
-
-def arrival_order(devices):
+    return kept(me, top) + kept(me ^ 3, top)
+
+
+def arrival_order(bits):
     offs = [0]
-    for bit in reversed(range(1, devices.bit_length() - 1)):
+    for bit in bits:
         offs += [off ^ (1 << bit) ^ 1 for off in offs]
     return offs + [off ^ 1 for off in offs]
 
@@ -620,10 +626,10 @@
         )
     moved, ends = 0, None
     as_face = lambda part: part.reshape(-1)[: depth * edge_x].reshape(depth, edge_x)
-    for bit in reversed(range(1, devices.bit_length() - 1)):
+    for bit in bit_order(devices, slabs):
         rides = 1 << bit < slabs
         low = (1 << (bit - 1)) - 1
-        moves_on, moves_back = (pair & low) == low, (pair & low) == 0
+        moves_on, moves_back = (pair & low) == 1, (pair & low) == low - 1
         extra = []
         if groups == 2 and 1 << bit == slabs:
             extra = [lines(edge_rows, unit)]
@@ -633,7 +639,7 @@
             extra = [lines(onward, unit), lines(backward, unit)]
         first_sent = packed_rows[0] if joined and 1 << bit == slabs else None
         if bit > 1 and len(beyond) == 2:
-            same = ((me >> bit) ^ (me >> (bit + 1))) & 1 == 0
+            same = ((me >> bit) ^ (me >> (bit - 1))) & 1 == 0
             beyond = [jnp.where(same, *beyond)]
         sent, got, at = exchanged(heat + beyond + extra, (1 << bit) | 1, first_sent)
         heat_rows = sum(part.shape[0] for part in heat)
@@ -679,7 +685,7 @@
         start_layer, start_y = group * brick_layers - 2, 0
         rows = min(up_to(need_layers, 8), all_layers)
     else:
-        order = np.argsort(arrival_order(devices))
+        order = np.argsort(arrival_order(bit_order(devices, slabs)))
         blocks = jnp.concatenate([sent[:heat_rows], got[:heat_rows]], 0).reshape(devices, 5, layers, flat)
         blocks = jnp.take(blocks, jnp.asarray(order)[jnp.arange(devices) ^ me], axis=0)
         held = jnp.moveaxis(blocks, 1, 0).reshape(5, all_layers, flat)

time: 19.4 us -> 19.4 us (level)
  no operation moved by 1% of the time
where the time goes in v10:
time: 19.4 us; the launch traced here: 19.2 us
  starting transfers between devices  9.31 us (48%)
  Pallas kernels  5.19 us (27%)
  waiting for transfers between devices  3.52 us (18%)
  between operations  0.77 us (4%)
  other arithmetic  0.41 us (2%)
    ppermute x5, starting transfers between devices, exchanged(): lax.ppermute(sent, AXES, [(i, i ^ flips) for i in range(devices)])  9.31 us
    ppermute x5, waiting for transfers between devices, exchanged(): lax.ppermute(sent, AXES, [(i, i ^ flips) for i in range(devices)])  3.52 us
    pallas_call x1, Pallas kernels, body(): pl.pallas_call(functools.partial(faces_kernel, depth, flat_cells), out_sh...  1.36 us
    pallas_call x1, Pallas kernels, body(): pl.pallas_call(functools.partial(finish_kernel, plane, depth, flat_cells,...  1.19 us
    pallas_call x1, Pallas kernels, sites(): pl.pallas_call(functools.partial(sites_kernel, flat_cells), out_shape=(ja...  0.97 us
    pallas_call x1, Pallas kernels, body(): pl.pallas_call(functools.partial(pack_kernel, plane), out_shape=[jax.Shap...  0.85 us
    pallas_call x1, Pallas kernels, body(): pl.pallas_call(functools.partial(cells_kernel, depth, flat_cells), out_sh...  0.81 us
  transfers between devices with their start and end apart: 5, of which 4 were waited for; matrix products, arithmetic and copies ran while one was open for 2% of the time, Pallas kernels for 16%

profile of v10, /device:TPU:0, one launch (start us, length us, event | category | flops | bytes accessed | tf_op | source)
XLA Modules:
  0.0 19.2 jit_solution(10378458814702484877)
XLA Ops:
  0.6 0.8 %pack.1 = f32[9,128]{1,0:T(8,128)S(1)} custom-call(f32[2,128]{1,0:T(2,128)} %state_ref.1, f32[2,128]{1,0:T(2,128)} %heat_ref.1, f32[1,32]{1,0:T(1,128)} %kappa_ref.1, f32[128,128]{1,0:T(8,128)} %frozen_hbm.1, s32[128,128]{1,0:T(8,128)} %label_hbm.1), custom_call_target="tpu_custom_call" | custom-call | tf_op jit(solution)/shard_map/pack/pallas_call | solution.py:521
  1.5 2.4 %collective-permute-start = (f32[9,128]{1,0:T(8,128)S(1)}, f32[9,128]{1,0:T(8,128)S(1)}, u32[]{:S(2)}, u32[]{:S(2)}) collective-permute-start(f32[9,128]{1,0:T(8,128)S(1)} %pack.1), channel_id=1, source_target_pairs={{0,17},{1,16},{2,19},{3,18},{4,21},{5,20},{6,23},{7,22},{8,25},{9,... | collective-permute-start | bytes 13832 | tf_op jit(solution)/shard_map/ppermute | solution.py:512
  4.0 1.4 %faces.1 = (s32[32,128]{1,0:T(8,128)S(1)}, s32[128,128]{1,0:T(8,128)S(1)}, f32[128,128]{1,0:T(8,128)S(1)}, f32[32,128]{1,0:T(8,128)S(1)}) custom-call(s32[6,8000]{1,0:T(8,128)} %bitcast.3, s32[128,128]{1,0:T(8,128)} %label_hbm.1, f32[128,128]{1,0:T(8,128)} %frozen_hbm.1), custom_call_target="tpu_custom_call" | custom-call | tf_op jit(solution)/shard_map/faces/pallas_call | solution.py:554
  5.4 0.0 collective-permute-done
  5.5 2.0 %collective-permute-start.1 = (f32[26,128]{1,0:T(8,128)S(1)}, f32[26,128]{1,0:T(8,128)S(1)}, u32[]{:S(2)}, u32[]{:S(2)}) collective-permute-start(f32[26,128]{1,0:T(8,128)S(1)} %pad_add_fusion.3), channel_id=1, source_target_pairs={{0,5},{1,4},{2,7},{3,6},{4,1},{5,0},{6,3},{7,2},{8,13},{9,12},{10,... | collective-permute-start | bytes 39944 | tf_op jit(solution)/shard_map/ppermute | solution.py:512
  7.5 0.8 %cells.1 = (f32[128,128]{1,0:T(8,128)S(1)}, f32[32,128]{1,0:T(8,128)S(1)}) custom-call(s32[32,128]{1,0:T(8,128)S(1)} %get-tuple-element.12.packed_ref, s32[128,128]{1,0:T(8,128)S(1)} %get-tuple-element.13.label_ref, f32[128,128]{1,0:T(8,128)S(1)} %get-tuple-element.14.frozen_ref, f32[32,128]{1,0:T(8,128)S(1)} %get-tuple-element.11.faces_ref), custom_call_target="tpu_custom_call" | custom-call | tf_op jit(solution)/shard_map/cells/pallas_call | solution.py:571
  8.3 0.6 %collective-permute-done.1 = f32[26,128]{1,0:T(8,128)S(1)} collective-permute-done((f32[26,128]{1,0:T(8,128)S(1)}, f32[26,128]{1,0:T(8,128)S(1)}, u32[]{:S(2)}, u32[]{:S(2)}) %collective-permute-start.1) | collective-permute-done | bytes 13344 | tf_op jit(solution)/shard_map/ppermute | solution.py:512
  9.0 2.8 %collective-permute-start.2 = (f32[31,128]{1,0:T(8,128)S(1)}, f32[31,128]{1,0:T(8,128)S(1)}, u32[]{:S(2)}, u32[]{:S(2)}) collective-permute-start(f32[31,128]{1,0:T(8,128)S(1)} %pad_add_fusion.2), channel_id=1, source_target_pairs={{0,9},{1,8},{2,11},{3,10},{4,13},{5,12},{6,15},{7,14},{8,1},{9,0},... | collective-permute-start | bytes 47624 | tf_op jit(solution)/shard_map/ppermute | solution.py:512
  11.8 1.0 %sites.1 = (f32[128,128]{1,0:T(8,128)S(1)}, f32[2,128]{1,0:T(2,128)S(1)}, f32[32,128]{1,0:T(8,128)S(1)}) custom-call(s32[32,128]{1,0:T(8,128)S(1)} %get-tuple-element.12.packed_ref, f32[4,128]{1,0:T(4,128)S(1)} %slice.91.edge_ref, f32[32,128]{1,0:T(8,128)S(1)} %get-tuple-element.15.faces_ref, s32[2,128]{1,0:T(2,128)} %bitcast.4, s32[2,128]{1,0:T(2,128)} %bitcast.5), custom_call_target="tpu_custom_call" | custom-call | tf_op jit(solution)/shard_map/sites/pallas_call | solution.py:587
  12.8 0.5 %collective-permute-done.2 = f32[31,128]{1,0:T(8,128)S(1)} collective-permute-done((f32[31,128]{1,0:T(8,128)S(1)}, f32[31,128]{1,0:T(8,128)S(1)}, u32[]{:S(2)}, u32[]{:S(2)}) %collective-permute-start.2) | collective-permute-done | bytes 15904 | tf_op jit(solution)/shard_map/ppermute | solution.py:512
  13.2 1.6 %collective-permute-start.3 = (f32[62,128]{1,0:T(8,128)S(1)}, f32[62,128]{1,0:T(8,128)S(1)}, u32[]{:S(2)}, u32[]{:S(2)}) collective-permute-start(f32[62,128]{1,0:T(8,128)S(1)} %pad_add_fusion.1), channel_id=1, source_target_pairs={{0,3},{1,2},{2,1},{3,0},{4,7},{5,6},{6,5},{7,4},{8,11},{9,10},{10,... | collective-permute-start | bytes 95240 | tf_op jit(solution)/shard_map/ppermute | solution.py:512
  14.9 1.8 %collective-permute-done.3 = f32[62,128]{1,0:T(8,128)S(1)} collective-permute-done((f32[62,128]{1,0:T(8,128)S(1)}, f32[62,128]{1,0:T(8,128)S(1)}, u32[]{:S(2)}, u32[]{:S(2)}) %collective-permute-start.3) | collective-permute-done | bytes 31776 | tf_op jit(solution)/shard_map/ppermute | solution.py:512
  16.7 0.4 %collective-permute-start.4 = (f32[94,128]{1,0:T(8,128)S(1)}, f32[94,128]{1,0:T(8,128)S(1)}, u32[]{:S(2)}, u32[]{:S(2)}) collective-permute-start(f32[94,128]{1,0:T(8,128)S(1)} %pad_add_fusion.mine_ref), channel_id=1, source_target_pairs={{0,1},{1,0},{2,3},{3,2},{4,5},{5,4},{6,7},{7,6},{8,9},{9,8},{10,11... | collective-permute-start | bytes 144392 | tf_op jit(solution)/shard_map/ppermute | solution.py:512
  17.1 0.2 %fusion.1.weave_ref = bf16[256,128]{1,0:T(8,128)(2,1)S(1)} fusion(f32[128]{0:T(128)S(1)} %get-tuple-element.32, f32[128]{0:T(128)S(1)} %get-tuple-element.33, f32[128]{0:T(128)S(1)} %get-tuple-element.34, s32[128]{0:T(128)S(1)} %get-tuple-element.37, s32[256]{0:T(256)S(1)} %get-tuple-element.28, f32[128]{0:T(128)S(1)} %get-tuple-element.30, ...), kind=kLoop, calls=%fused_computation.10 | loop fusion | flops 1212416 | bytes 72064 | tf_op jit(solution)/shard_map/convert_element_type | solution.py:439
  17.4 0.6 %collective-permute-done.4.theirs_ref.across_ref.passing_ref.edge_ref = f32[94,128]{1,0:T(8,128)S(1)} collective-permute-done((f32[94,128]{1,0:T(8,128)S(1)}, f32[94,128]{1,0:T(8,128)S(1)}, u32[]{:S(2)}, u32[]{:S(2)}) %collective-permute-start.4) | collective-permute-done | bytes 48160 | tf_op jit(solution)/shard_map/ppermute | solution.py:512
  18.0 1.2 %finish.1 = (f32[2,128]{1,0:T(2,128)}, f32[128,128]{1,0:T(8,128)}) custom-call(f32[94,128]{1,0:T(8,128)S(1)} %pad_add_fusion.mine_ref, f32[94,128]{1,0:T(8,128)S(1)} %collective-permute-done.4.theirs_ref.across_ref.passing_ref.edge_ref, f32[94,128]{1,0:T(8,128)S(1)} %collective-permute-done.4.theirs_ref.across_ref.passing_ref.edge_ref, ...), custom_call_target="tpu_custom_call" | custom-call | tf_op jit(solution)/shard_map/finish/pallas_call | solution.py:741
  (24 shorter events, 0.2 us)
Async XLA Ops:
  1.5 3.9 %collective-permute-start = (f32[9,128]{1,0:T(8,128)S(1)}, f32[9,128]{1,0:T(8,128)S(1)}, u32[]{:S(2)}, u32[]{:S(2)}) collective-permute-start(f32[9,128]{1,0:T(8,128)S(1)} %pack.1), channel_id=1, source_target_pairs={{0,17},{1,16},{2,19},{3,18},{4,21},{5,20},{6,23},{7,22},{8,25},{9,... | collective-permute-start | bytes 13832 | tf_op jit(solution)/shard_map/ppermute | solution.py:512
  5.5 3.5 %collective-permute-start.1 = (f32[26,128]{1,0:T(8,128)S(1)}, f32[26,128]{1,0:T(8,128)S(1)}, u32[]{:S(2)}, u32[]{:S(2)}) collective-permute-start(f32[26,128]{1,0:T(8,128)S(1)} %pad_add_fusion.3), channel_id=1, source_target_pairs={{0,5},{1,4},{2,7},{3,6},{4,1},{5,0},{6,3},{7,2},{8,13},{9,12},{10,... | collective-permute-start | bytes 39944 | tf_op jit(solution)/shard_map/ppermute | solution.py:512
  9.0 4.2 %collective-permute-start.2 = (f32[31,128]{1,0:T(8,128)S(1)}, f32[31,128]{1,0:T(8,128)S(1)}, u32[]{:S(2)}, u32[]{:S(2)}) collective-permute-start(f32[31,128]{1,0:T(8,128)S(1)} %pad_add_fusion.2), channel_id=1, source_target_pairs={{0,9},{1,8},{2,11},{3,10},{4,13},{5,12},{6,15},{7,14},{8,1},{9,0},... | collective-permute-start | bytes 47624 | tf_op jit(solution)/shard_map/ppermute | solution.py:512
  13.2 3.4 %collective-permute-start.3 = (f32[62,128]{1,0:T(8,128)S(1)}, f32[62,128]{1,0:T(8,128)S(1)}, u32[]{:S(2)}, u32[]{:S(2)}) collective-permute-start(f32[62,128]{1,0:T(8,128)S(1)} %pad_add_fusion.1), channel_id=1, source_target_pairs={{0,3},{1,2},{2,1},{3,0},{4,7},{5,6},{6,5},{7,4},{8,11},{9,10},{10,... | collective-permute-start | bytes 95240 | tf_op jit(solution)/shard_map/ppermute | solution.py:512
  16.7 1.3 %collective-permute-start.4 = (f32[94,128]{1,0:T(8,128)S(1)}, f32[94,128]{1,0:T(8,128)S(1)}, u32[]{:S(2)}, u32[]{:S(2)}) collective-permute-start(f32[94,128]{1,0:T(8,128)S(1)} %pad_add_fusion.mine_ref), channel_id=1, source_target_pairs={{0,1},{1,0},{2,3},{3,2},{4,5},{5,4},{6,7},{7,6},{8,9},{9,8},{10,11... | collective-permute-start | bytes 144392 | tf_op jit(solution)/shard_map/ppermute | solution.py:512

commit v11 on v10

--- a/solution.py
+++ b/solution.py
@@ -11,7 +11,7 @@
 HEX_COUNT_LATER = 2
 CPC = 8
 LANES = 128
-CHUNKS = 4
+CHUNKS = 2
 STEP = 0.004
 AXES = ("grp", "slab")
 VMEM = pl.BlockSpec(memory_space=pltpu.VMEM)

time: 19.4 us -> 19.4 us (level)
  no operation moved by 1% of the time
where the time goes in v11:
time: 19.4 us; the launch traced here: 19.2 us
  starting transfers between devices  9.31 us (48%)
  Pallas kernels  5.17 us (27%)
  waiting for transfers between devices  3.52 us (18%)
  between operations  0.77 us (4%)
  other arithmetic  0.41 us (2%)
    ppermute x5, starting transfers between devices, exchanged(): lax.ppermute(sent, AXES, [(i, i ^ flips) for i in range(devices)])  9.31 us
    ppermute x5, waiting for transfers between devices, exchanged(): lax.ppermute(sent, AXES, [(i, i ^ flips) for i in range(devices)])  3.52 us
    pallas_call x1, Pallas kernels, body(): pl.pallas_call(functools.partial(faces_kernel, depth, flat_cells), out_sh...  1.36 us
    pallas_call x1, Pallas kernels, body(): pl.pallas_call(functools.partial(finish_kernel, plane, depth, flat_cells,...  1.18 us
    pallas_call x1, Pallas kernels, sites(): pl.pallas_call(functools.partial(sites_kernel, flat_cells), out_shape=(ja...  0.97 us
    pallas_call x1, Pallas kernels, body(): pl.pallas_call(functools.partial(pack_kernel, plane), out_shape=[jax.Shap...  0.85 us
    pallas_call x1, Pallas kernels, body(): pl.pallas_call(functools.partial(cells_kernel, depth, flat_cells), out_sh...  0.81 us
  transfers between devices with their start and end apart: 5, of which 4 were waited for; matrix products, arithmetic and copies ran while one was open for 2% of the time, Pallas kernels for 16%

profile of v11, /device:TPU:0, one launch (start us, length us, event | category | flops | bytes accessed | tf_op | source)
XLA Modules:
  0.0 19.2 jit_solution(11442815365806011618)
XLA Ops:
  0.6 0.8 %pack.1 = f32[9,128]{1,0:T(8,128)S(1)} custom-call(f32[2,128]{1,0:T(2,128)} %state_ref.1, f32[2,128]{1,0:T(2,128)} %heat_ref.1, f32[1,32]{1,0:T(1,128)} %kappa_ref.1, f32[128,128]{1,0:T(8,128)} %frozen_hbm.1, s32[128,128]{1,0:T(8,128)} %label_hbm.1), custom_call_target="tpu_custom_call" | custom-call | tf_op jit(solution)/shard_map/pack/pallas_call | solution.py:521
  1.5 2.4 %collective-permute-start = (f32[9,128]{1,0:T(8,128)S(1)}, f32[9,128]{1,0:T(8,128)S(1)}, u32[]{:S(2)}, u32[]{:S(2)}) collective-permute-start(f32[9,128]{1,0:T(8,128)S(1)} %pack.1), channel_id=1, source_target_pairs={{0,17},{1,16},{2,19},{3,18},{4,21},{5,20},{6,23},{7,22},{8,25},{9,... | collective-permute-start | bytes 13832 | tf_op jit(solution)/shard_map/ppermute | solution.py:512
  4.0 1.4 %faces.1 = (s32[32,128]{1,0:T(8,128)S(1)}, s32[128,128]{1,0:T(8,128)S(1)}, f32[128,128]{1,0:T(8,128)S(1)}, f32[32,128]{1,0:T(8,128)S(1)}) custom-call(s32[6,8000]{1,0:T(8,128)} %bitcast.3, s32[128,128]{1,0:T(8,128)} %label_hbm.1, f32[128,128]{1,0:T(8,128)} %frozen_hbm.1), custom_call_target="tpu_custom_call" | custom-call | tf_op jit(solution)/shard_map/faces/pallas_call | solution.py:554
  5.4 0.0 collective-permute-done
  5.5 2.0 %collective-permute-start.1 = (f32[26,128]{1,0:T(8,128)S(1)}, f32[26,128]{1,0:T(8,128)S(1)}, u32[]{:S(2)}, u32[]{:S(2)}) collective-permute-start(f32[26,128]{1,0:T(8,128)S(1)} %pad_add_fusion.3), channel_id=1, source_target_pairs={{0,5},{1,4},{2,7},{3,6},{4,1},{5,0},{6,3},{7,2},{8,13},{9,12},{10,... | collective-permute-start | bytes 39944 | tf_op jit(solution)/shard_map/ppermute | solution.py:512
  7.5 0.8 %cells.1 = (f32[128,128]{1,0:T(8,128)S(1)}, f32[32,128]{1,0:T(8,128)S(1)}) custom-call(s32[32,128]{1,0:T(8,128)S(1)} %get-tuple-element.12.packed_ref, s32[128,128]{1,0:T(8,128)S(1)} %get-tuple-element.13.label_ref, f32[128,128]{1,0:T(8,128)S(1)} %get-tuple-element.14.frozen_ref, f32[32,128]{1,0:T(8,128)S(1)} %get-tuple-element.11.faces_ref), custom_call_target="tpu_custom_call" | custom-call | tf_op jit(solution)/shard_map/cells/pallas_call | solution.py:571
  8.3 0.6 %collective-permute-done.1 = f32[26,128]{1,0:T(8,128)S(1)} collective-permute-done((f32[26,128]{1,0:T(8,128)S(1)}, f32[26,128]{1,0:T(8,128)S(1)}, u32[]{:S(2)}, u32[]{:S(2)}) %collective-permute-start.1) | collective-permute-done | bytes 13344 | tf_op jit(solution)/shard_map/ppermute | solution.py:512
  9.0 2.8 %collective-permute-start.2 = (f32[31,128]{1,0:T(8,128)S(1)}, f32[31,128]{1,0:T(8,128)S(1)}, u32[]{:S(2)}, u32[]{:S(2)}) collective-permute-start(f32[31,128]{1,0:T(8,128)S(1)} %pad_add_fusion.2), channel_id=1, source_target_pairs={{0,9},{1,8},{2,11},{3,10},{4,13},{5,12},{6,15},{7,14},{8,1},{9,0},... | collective-permute-start | bytes 47624 | tf_op jit(solution)/shard_map/ppermute | solution.py:512
  11.8 1.0 %sites.1 = (f32[128,128]{1,0:T(8,128)S(1)}, f32[2,128]{1,0:T(2,128)S(1)}, f32[32,128]{1,0:T(8,128)S(1)}) custom-call(s32[32,128]{1,0:T(8,128)S(1)} %get-tuple-element.12.packed_ref, f32[4,128]{1,0:T(4,128)S(1)} %slice.91.edge_ref, f32[32,128]{1,0:T(8,128)S(1)} %get-tuple-element.15.faces_ref, s32[2,128]{1,0:T(2,128)} %bitcast.4, s32[2,128]{1,0:T(2,128)} %bitcast.5), custom_call_target="tpu_custom_call" | custom-call | tf_op jit(solution)/shard_map/sites/pallas_call | solution.py:587
  12.8 0.5 %collective-permute-done.2 = f32[31,128]{1,0:T(8,128)S(1)} collective-permute-done((f32[31,128]{1,0:T(8,128)S(1)}, f32[31,128]{1,0:T(8,128)S(1)}, u32[]{:S(2)}, u32[]{:S(2)}) %collective-permute-start.2) | collective-permute-done | bytes 15904 | tf_op jit(solution)/shard_map/ppermute | solution.py:512
  13.2 1.6 %collective-permute-start.3 = (f32[62,128]{1,0:T(8,128)S(1)}, f32[62,128]{1,0:T(8,128)S(1)}, u32[]{:S(2)}, u32[]{:S(2)}) collective-permute-start(f32[62,128]{1,0:T(8,128)S(1)} %pad_add_fusion.1), channel_id=1, source_target_pairs={{0,3},{1,2},{2,1},{3,0},{4,7},{5,6},{6,5},{7,4},{8,11},{9,10},{10,... | collective-permute-start | bytes 95240 | tf_op jit(solution)/shard_map/ppermute | solution.py:512
  14.9 1.8 %collective-permute-done.3 = f32[62,128]{1,0:T(8,128)S(1)} collective-permute-done((f32[62,128]{1,0:T(8,128)S(1)}, f32[62,128]{1,0:T(8,128)S(1)}, u32[]{:S(2)}, u32[]{:S(2)}) %collective-permute-start.3) | collective-permute-done | bytes 31776 | tf_op jit(solution)/shard_map/ppermute | solution.py:512
  16.7 0.4 %collective-permute-start.4 = (f32[94,128]{1,0:T(8,128)S(1)}, f32[94,128]{1,0:T(8,128)S(1)}, u32[]{:S(2)}, u32[]{:S(2)}) collective-permute-start(f32[94,128]{1,0:T(8,128)S(1)} %pad_add_fusion.mine_ref), channel_id=1, source_target_pairs={{0,1},{1,0},{2,3},{3,2},{4,5},{5,4},{6,7},{7,6},{8,9},{9,8},{10,11... | collective-permute-start | bytes 144392 | tf_op jit(solution)/shard_map/ppermute | solution.py:512
  17.1 0.2 %fusion.1.weave_ref = bf16[256,128]{1,0:T(8,128)(2,1)S(1)} fusion(f32[128]{0:T(128)S(1)} %get-tuple-element.32, f32[128]{0:T(128)S(1)} %get-tuple-element.33, f32[128]{0:T(128)S(1)} %get-tuple-element.34, s32[128]{0:T(128)S(1)} %get-tuple-element.37, s32[256]{0:T(256)S(1)} %get-tuple-element.28, f32[128]{0:T(128)S(1)} %get-tuple-element.30, ...), kind=kLoop, calls=%fused_computation.10 | loop fusion | flops 1212416 | bytes 72064 | tf_op jit(solution)/shard_map/convert_element_type | solution.py:439
  17.4 0.6 %collective-permute-done.4.theirs_ref.across_ref.passing_ref.edge_ref = f32[94,128]{1,0:T(8,128)S(1)} collective-permute-done((f32[94,128]{1,0:T(8,128)S(1)}, f32[94,128]{1,0:T(8,128)S(1)}, u32[]{:S(2)}, u32[]{:S(2)}) %collective-permute-start.4) | collective-permute-done | bytes 48160 | tf_op jit(solution)/shard_map/ppermute | solution.py:512
  18.0 1.2 %finish.1 = (f32[2,128]{1,0:T(2,128)}, f32[128,128]{1,0:T(8,128)}) custom-call(f32[94,128]{1,0:T(8,128)S(1)} %pad_add_fusion.mine_ref, f32[94,128]{1,0:T(8,128)S(1)} %collective-permute-done.4.theirs_ref.across_ref.passing_ref.edge_ref, f32[94,128]{1,0:T(8,128)S(1)} %collective-permute-done.4.theirs_ref.across_ref.passing_ref.edge_ref, ...), custom_call_target="tpu_custom_call" | custom-call | tf_op jit(solution)/shard_map/finish/pallas_call | solution.py:741
  (24 shorter events, 0.2 us)
Async XLA Ops:
  1.5 3.9 %collective-permute-start = (f32[9,128]{1,0:T(8,128)S(1)}, f32[9,128]{1,0:T(8,128)S(1)}, u32[]{:S(2)}, u32[]{:S(2)}) collective-permute-start(f32[9,128]{1,0:T(8,128)S(1)} %pack.1), channel_id=1, source_target_pairs={{0,17},{1,16},{2,19},{3,18},{4,21},{5,20},{6,23},{7,22},{8,25},{9,... | collective-permute-start | bytes 13832 | tf_op jit(solution)/shard_map/ppermute | solution.py:512
  5.5 3.5 %collective-permute-start.1 = (f32[26,128]{1,0:T(8,128)S(1)}, f32[26,128]{1,0:T(8,128)S(1)}, u32[]{:S(2)}, u32[]{:S(2)}) collective-permute-start(f32[26,128]{1,0:T(8,128)S(1)} %pad_add_fusion.3), channel_id=1, source_target_pairs={{0,5},{1,4},{2,7},{3,6},{4,1},{5,0},{6,3},{7,2},{8,13},{9,12},{10,... | collective-permute-start | bytes 39944 | tf_op jit(solution)/shard_map/ppermute | solution.py:512
  9.0 4.2 %collective-permute-start.2 = (f32[31,128]{1,0:T(8,128)S(1)}, f32[31,128]{1,0:T(8,128)S(1)}, u32[]{:S(2)}, u32[]{:S(2)}) collective-permute-start(f32[31,128]{1,0:T(8,128)S(1)} %pad_add_fusion.2), channel_id=1, source_target_pairs={{0,9},{1,8},{2,11},{3,10},{4,13},{5,12},{6,15},{7,14},{8,1},{9,0},... | collective-permute-start | bytes 47624 | tf_op jit(solution)/shard_map/ppermute | solution.py:512
  13.2 3.4 %collective-permute-start.3 = (f32[62,128]{1,0:T(8,128)S(1)}, f32[62,128]{1,0:T(8,128)S(1)}, u32[]{:S(2)}, u32[]{:S(2)}) collective-permute-start(f32[62,128]{1,0:T(8,128)S(1)} %pad_add_fusion.1), channel_id=1, source_target_pairs={{0,3},{1,2},{2,1},{3,0},{4,7},{5,6},{6,5},{7,4},{8,11},{9,10},{10,... | collective-permute-start | bytes 95240 | tf_op jit(solution)/shard_map/ppermute | solution.py:512
  16.7 1.3 %collective-permute-start.4 = (f32[94,128]{1,0:T(8,128)S(1)}, f32[94,128]{1,0:T(8,128)S(1)}, u32[]{:S(2)}, u32[]{:S(2)}) collective-permute-start(f32[94,128]{1,0:T(8,128)S(1)} %pad_add_fusion.mine_ref), channel_id=1, source_target_pairs={{0,1},{1,0},{2,3},{3,2},{4,5},{5,4},{6,7},{7,6},{8,9},{9,8},{10,11... | collective-permute-start | bytes 144392 | tf_op jit(solution)/shard_map/ppermute | solution.py:512
